TPU v7x, 32 devices: a whole 2x2x4 slice. The times are simulated.
32 devices in a mesh: grp: 4 (over y, x), row: 8 (over z, core).
Axes of the slice: x: 2, y: 2, z: 4, core: 2. Of those that a mesh axis runs over, the one named last changes fastest.
Arguments:
- green: bfloat16 [8192, 8192], P('grp', 'row'), may hold values from -0.5 to 0.5
- footprint: int32 [64, 64], P('grp', 'row'), may hold values from 0 to 1, as said below
- set_index: int32 [64], P('grp'), may hold values from 0 to 7
- set_weight: float32 [8], replicated, may hold values from 0.3 to 3
- pixel_scale: float32 [8192], P('grp'), may hold values from 0.1 to 1
- panel_index: int32 [1], replicated, may hold values from 0 to 15
Outputs:
- gram_panel: float32 [8192, 512], P(('row', 'grp'))
Inputs may be any that keep to these rules, and one draw needn't show every extreme that they name: `footprint`: each entry is 0 or 1; how dense a column of blocks is varies between unknown blocks.
All inputs are finite; a program needn't handle non-finite values.
Results may differ from a plain program's by a relative error of at most 0.0026.
Values may be sent and summed in bfloat16 or wider, within the bound.
No kernel may reach another device: no remote copies, remote signals or barrier semaphores. Data moves between devices by JAX's collectives and lax.ppermute only.
A program may use at most 64 MiB of HBM per device.

v0:
```python
import jax
import jax.numpy as jnp
from jax import lax
from jax.sharding import PartitionSpec as P

PANEL = 4
NSETS = 8


def on_device(green, footprint, set_index, set_weight, pixel_scale, panel_index):
    rows, cols = green.shape
    pblocks, blocks = footprint.shape
    width = cols // blocks
    panel_cols = PANEL * width
    first = panel_index[0] * PANEL
    owner = first // blocks
    local_first = first - owner * blocks
    fmask = footprint.astype(jnp.bfloat16)
    mask_cols = lax.dynamic_slice_in_dim(fmask, local_first, PANEL, 1)
    own_panel = lax.dynamic_slice_in_dim(green, local_first * width, panel_cols, 1)
    own_panel = (
        own_panel.reshape(pblocks, width, PANEL, width) * mask_cols[:, None, :, None]
    ).reshape(rows, panel_cols)
    placed = jnp.where(lax.axis_index("row") == owner, own_panel, jnp.zeros_like(own_panel))
    panel = lax.psum(placed, "row").astype(jnp.float32).astype(jnp.bfloat16)
    onehot = (set_index[:, None] == jnp.arange(NSETS, dtype=jnp.int32)[None, :]).astype(jnp.float32)
    block_weight = jnp.sum(onehot * set_weight[None, :], axis=1)
    weight = (pixel_scale.reshape(pblocks, width) * block_weight[:, None]).reshape(rows)
    weighted = (panel.astype(jnp.float32) * weight[:, None]).astype(jnp.bfloat16)
    masked = (green.reshape(pblocks, width, blocks, width) * fmask[:, None, :, None]).reshape(
        rows, cols
    )
    share = cols // lax.axis_size("grp")
    total = lax.psum(
        lax.dot_general(
            masked, weighted, (((0,), (0,)), ((), ())), preferred_element_type=jnp.float32
        ),
        "grp",
    )
    return lax.dynamic_slice_in_dim(total, lax.axis_index("grp") * share, share, 0)


def solution(mesh):
    in_specs = (P("grp", "row"), P("grp", "row"), P("grp"), P(), P("grp"), P())
    out_specs = P(("row", "grp"), None)
    return jax.shard_map(
        on_device, mesh=mesh, in_specs=in_specs, out_specs=out_specs, check_vma=False
    )
```

profile of v0, /device:TPU:0, one launch (start us, length us, event | category | flops | bytes accessed | tf_op | source)
XLA Modules:
  0.0 165.7 jit_solution(10167686593684278887)
XLA Ops:
  6.5 0.0 all-reduce.3.cloned.1.call-start
  7.2 0.7 convert_element_type.12
  7.9 0.1 copy.10
  8.0 0.6 mul.72
  8.6 3.5 %fusion.2 = bf16[2048,512]{1,0:T(8,128)(2,1)} fusion(bf16[256,8,4,128]{3,2,1,0:T(4,128)(2,1)S(1)} %bitcast.14, bf16[2048,1024]{1,0:T(8,128)(2,1)} %param.6, s32[]{:T(128)S(6)} %select_n.24, pred[]{:T(512)S(6)} %eq.16), kind=kLoop, calls=%fused_computation.5 | loop fusion | flops 5242880 | bytes 6291461 | tf_op jit(solution)/shard_map/jit(_where)/select_n | solution.py:24
  12.2 0.0 copy-start.2
  12.2 0.0 copy-start.3
  12.2 0.0 copy-start.1
  12.2 0.0 all-reduce.3.cloned.1.call-update
  12.2 0.0 all-reduce.5.cloned.1.call-start
  12.2 0.1 copy.9
  12.3 0.5 copy-done.2
  12.8 0.0 copy-done.3
  12.8 0.1 select_reduce_fusion
  12.9 0.0 copy-done.1
  12.9 0.1 bitcast_multiply_fusion.3
  13.0 66.9 %all-reduce.3.cloned.1.call-done = bf16[2048,512]{1,0:T(8,128)(2,1)} async-done(((bf16[2048,512]{1,0:T(8,128)(2,1)}), bf16[2048,512]{1,0:T(8,128)(2,1)}) %all-reduce.3.cloned.1.call-update) | async-done | bytes 2097168 | tf_op jit(solution)/shard_map/psum | solution.py:25
  79.9 0.0 copy-start
  79.9 0.6 mul.65
  80.5 1.6 copy-done
  82.1 5.4 %fusion = f32[1024,512]{1,0:T(8,128)} fusion(bf16[2048,1024]{1,0:T(8,128)(2,1)S(1)} %copy-done, bf16[256,8,8,128]{3,2,1,0:T(8,128)(2,1)S(1)} %bitcast.15, bf16[2048,512]{1,0:T(8,128)(2,1)} %all-reduce.3.cloned.1.call-done, f32[2048]{0:T(1024)S(1)} %bitcast_multiply_fusion.3), kind=kOutput, calls=%fused_computation.1 | convolution fusion | flops 2152726528 | bytes 12591104 | tf_op jit(solution)/shard_map/dot_general | solution.py:35
  87.5 0.0 all-reduce.5.cloned.1.call-update
  87.5 69.5 %all-reduce.5.cloned.1.call-done = f32[1024,512]{1,0:T(8,128)} async-done(((f32[1024,512]{1,0:T(8,128)}), f32[1024,512]{1,0:T(8,128)}) %all-reduce.5.cloned.1.call-update) | async-done | bytes 2097168 | tf_op jit(solution)/shard_map/psum | solution.py:34
  157.0 1.9 %constant_dynamic-slice_fusion = f32[256,512]{1,0:T(8,128)} fusion(f32[1024,512]{1,0:T(8,128)} %all-reduce.5.cloned.1.call-done, s32[]{:T(128)S(6)} %select_n.27), kind=kLoop, calls=%fused_computation.10 | loop fusion | bytes 1048580 | tf_op jit(solution)/shard_map/dynamic_slice | solution.py:40
  (1 shorter events, 0.0 us)
Async XLA Ops:
  6.5 73.4 %all-reduce.3.cloned.1.call-start = ((), (), s32[]{:S(2)}) async-start(), calls=%async_computation | async-start | bytes 4194304 | tf_op jit(solution)/shard_map/psum | solution.py:25
  12.2 0.7 copy-start.2
  12.2 0.7 copy-start.3
  12.2 0.8 copy-start.1
  12.2 144.8 %all-reduce.5.cloned.1.call-start = ((), (), s32[]{:S(2)}) async-start(), calls=%async_computation.1 | async-start | bytes 4194304 | tf_op jit(solution)/shard_map/psum | solution.py:34
  79.9 2.2 %copy-start = (bf16[2048,1024]{1,0:T(8,128)(2,1)S(1)}, bf16[2048,1024]{1,0:T(8,128)(2,1)}, u32[]{:S(2)}) copy-start(bf16[2048,1024]{1,0:T(8,128)(2,1)} %param.6) | copy-start | bytes 12582916
Sparse Core Ops, SparseCore 0:
  12.3 67.5 all-reduce.2
  87.6 69.2 all-reduce.4
where the time goes:
time: 166 us
  waiting for transfers between devices  136 us (82%)
  between operations  14.1 us (8%)
  matrix products  5.42 us (3%)
  local copies, waits for them, and re-layouts  5.36 us (3%)
  other arithmetic  4.36 us (3%)
    psum x1, waiting for transfers between devices, on_device(): lax.psum(lax.dot_general(masked, weighted, (((0,), (0,)), ((), ())), pref...  69.5 us
    psum x1, waiting for transfers between devices, on_device(): panel = lax.psum(placed, 'row').astype(jnp.float32).astype(jnp.bfloat16)  66.9 us
    dot_general x1, matrix products, on_device(): lax.dot_general(masked, weighted, (((0,), (0,)), ((), ())), preferred_ele...  5.42 us
    select_n x1, other arithmetic, on_device(): jnp.where(lax.axis_index('row') == owner, own_panel, jnp.zeros_like(own_p...  3.51 us
  transfers between devices with their start and end apart: 2, of which 2 were waited for; matrix products, arithmetic and copies ran while one was open for 0% of the time, Pallas kernels for 0%

commit v1 on v0

v1 whole, which is shorter than its diff:
```python
import functools
import jax
import jax.numpy as jnp
from jax import lax
from jax.experimental import pallas as pl
from jax.experimental.pallas import tpu as pltpu
from jax.sharding import PartitionSpec as P

PANEL = 4
CHUNKS = ((0,), (1,), (2,), (3,))
BATCHES = ((0, 1), (2, 3))
TIE = 1
VMEM_LIMIT = 24 * 1024 * 1024
PREP_LIMIT = 60 * 1024 * 1024


def whole_vmem():
    return pl.BlockSpec(memory_space=pltpu.VMEM)


def smem():
    return pl.BlockSpec(memory_space=pltpu.SMEM)


def prep_body(chunks, lane, width, panel, fp_hbm, set_hbm, sw_hbm, scale_hbm, green_hbm, *refs):
    outs, (fp, sets, sw, scale, green, sems) = refs[: 2 * len(chunks)], refs[2 * len(chunks) :]
    blocks, pblocks = fp_hbm.shape
    half_blocks = pblocks // 2
    half = half_blocks * width
    low = chunks[0][0]
    first = lax.rem(panel[0] * PANEL, blocks)
    at = pl.ds(pl.multiple_of((first + low) * width, width), green.shape[1])
    copies = [
        pltpu.make_async_copy(source, target, sems.at[n])
        for n, (source, target) in enumerate(
            ((fp_hbm, fp), (set_hbm, sets), (sw_hbm, sw), (scale_hbm, scale), (green_hbm.at[:, at], green))
        )
    ]
    for copy in copies:
        copy.start()
    for copy in copies:
        copy.wait()
    core = lax.axis_index(lane) & 1
    for side in (1, 0):
        base = (core if side == 0 else 1 - core) * half_blocks
        for i in range(half_blocks):
            weight = scale[pl.ds(base + i, 1), :] * sw[sets[base + i]]
            weight = jnp.broadcast_to(weight, (width, width)).T
            rows = pl.ds(pl.multiple_of((base + i) * width, width), width)
            for n, cols in enumerate(chunks):
                for m, col in enumerate(cols):
                    block = green[rows, (col - low) * width : (col - low + 1) * width]
                    value = (block.astype(jnp.float32) * weight).astype(jnp.bfloat16)
                    keep = fp[first + col, base + i] != 0
                    to = slice(m * half + i * width, m * half + (i + 1) * width)
                    outs[2 * n + side][to, :] = jnp.where(keep, value, jnp.zeros_like(value))


def prep(chunks, lane, panel_index, footprint, set_index, set_weight, scale, green):
    rows = green.shape[0]
    width = rows // footprint.shape[1]
    count = sum(len(cols) for cols in chunks)
    shapes = [jax.ShapeDtypeStruct((rows // 2 * len(cols), width), jnp.bfloat16) for cols in chunks for _ in range(2)]
    return pl.pallas_call(
        functools.partial(prep_body, chunks, lane, width),
        in_specs=[smem()] + [pl.BlockSpec(memory_space=pltpu.HBM)] * 5,
        out_specs=[whole_vmem()] * len(shapes),
        out_shape=shapes,
        scratch_shapes=[
            pltpu.SMEM(footprint.shape, jnp.int32),
            pltpu.SMEM(set_index.shape, jnp.int32),
            pltpu.SMEM(set_weight.shape, jnp.float32),
            pltpu.VMEM(scale.shape, jnp.float32),
            pltpu.VMEM((rows, count * width), jnp.bfloat16),
            pltpu.SemaphoreType.DMA((5,)),
        ],
        compiler_params=pltpu.CompilerParams(vmem_limit_bytes=PREP_LIMIT),
        name="weigh_panel",
    )(panel_index, footprint, set_index, set_weight, scale, green)


def turn_body(blocks, width, step_blocks, fp_ref, green_ref, out_ref, done_ref):
    step = pl.program_id(0)
    done_ref[...] = jnp.zeros_like(done_ref)
    for i in range(step_blocks):
        for j in range(blocks):
            block = green_ref[i * width : (i + 1) * width, j * width : (j + 1) * width]
            keep = fp_ref[j, step * step_blocks + i] != 0
            block = jnp.where(keep, block, jnp.zeros_like(block))
            out_ref[j * width : (j + 1) * width, i * width : (i + 1) * width] = block.T


def turn(footprint, green):
    rows, cols = green.shape
    blocks, pblocks = footprint.shape
    width = rows // pblocks
    steps = 4
    return pl.pallas_call(
        functools.partial(turn_body, blocks, width, pblocks // steps),
        grid=(steps,),
        in_specs=[smem(), pl.BlockSpec((rows // steps, cols), lambda i: (i, 0))],
        out_specs=[pl.BlockSpec((cols, rows // steps), lambda i: (0, i)), pl.BlockSpec((8, width), lambda i: (0, 0))],
        out_shape=[jax.ShapeDtypeStruct((cols, rows), jnp.bfloat16), jax.ShapeDtypeStruct((8, width), jnp.bfloat16)],
        compiler_params=pltpu.CompilerParams(vmem_limit_bytes=VMEM_LIMIT),
        name="mask_and_turn",
    )(footprint, green)


def gram_body(shares, count, meta, turned_ref, *refs):
    pieces, outs, done_ref, total_ref = refs[:count], refs[count:-2], refs[-2], refs[-1]
    done_ref[...] = jnp.zeros_like(done_ref)
    core, group = meta[0], meta[1]
    half = turned_ref.shape[1] // 2
    share = turned_ref.shape[0] // shares

    def half_of(side):
        return pl.ds(pl.multiple_of((core if side == 0 else 1 - core) * half, half), half)

    def columns(side):
        some = pieces[side::2]
        return jnp.concatenate([p[c : c + half, :] for p in some for c in range(0, p.shape[0], half)], 1)

    @pl.loop(0, shares)
    def _(s):
        at = pl.ds(pl.multiple_of((group ^ s) * share, share), share)
        total_ref[pl.ds(pl.multiple_of(s * share, share), share), :] = sum(
            jnp.dot(turned_ref[at, half_of(side)], columns(side), preferred_element_type=jnp.float32)
            for side in range(2)
        )

    for s in range(shares):
        outs[s][...] = total_ref[s * share : (s + 1) * share, :].astype(outs[s].dtype)


def gram(shares, meta, turned, pieces):
    unknowns, pixels = turned.shape
    cols = sum(p.shape[0] for p in pieces[::2]) // (pixels // 2)
    share, wide = unknowns // shares, pieces[0].shape[1] * cols
    return pl.pallas_call(
        functools.partial(gram_body, shares, len(pieces)),
        in_specs=[smem()] + [whole_vmem()] * (1 + len(pieces)),
        out_specs=[whole_vmem()] * (shares + 1),
        out_shape=[jax.ShapeDtypeStruct((share, wide), jnp.float32 if s == 0 else jnp.bfloat16) for s in range(shares)]
        + [jax.ShapeDtypeStruct((8, pieces[0].shape[1]), jnp.bfloat16)],
        scratch_shapes=[pltpu.VMEM((unknowns, wide), jnp.float32)],
        compiler_params=pltpu.CompilerParams(vmem_limit_bytes=VMEM_LIMIT),
        name="partial_gram",
    )(meta, turned, *pieces)


def sum_body(shares, *refs):
    out_ref, parts = refs[-1], refs[:-1]
    at = 0
    for k in range(0, len(parts), shares):
        total = parts[k][...]
        for s in range(1, shares):
            total += parts[k + s][...].astype(jnp.float32)
        out_ref[:, at : at + total.shape[1]] = total
        at += total.shape[1]


def total_of(shares, parts, panel_cols):
    return pl.pallas_call(
        functools.partial(sum_body, shares),
        in_specs=[whole_vmem()] * len(parts),
        out_specs=whole_vmem(),
        out_shape=jax.ShapeDtypeStruct((parts[0].shape[0], panel_cols), jnp.float32),
        compiler_params=pltpu.CompilerParams(vmem_limit_bytes=VMEM_LIMIT),
        name="sum_groups",
    )(*parts)


def spread(owner, chips):
    levels = {}

    def serve(source, run, depth):
        if not run:
            return
        middle = run[len(run) // 2] if len(run) > 2 else run[0]
        levels.setdefault(depth, []).append((source, middle))
        at = run.index(middle)
        serve(middle, run[:at][::-1], depth + 1)
        serve(middle, run[at + 1 :], depth + 1)

    serve(owner, list(range(owner + 1, chips)), 0)
    serve(owner, list(range(owner - 1, -1, -1)), 0)
    rounds = []
    for depth in sorted(levels):
        left = levels[depth]
        while left:
            used, later, now = set(), [], []
            for edge in left:
                (later if edge[0] in used else now).append(edge)
                used.add(edge[0])
            rounds.append((depth, now))
            left = later
    return rounds


def after(value, *zeros):
    for zero in zeros:
        value = value + zero[:1]
    return value


def on_device(groups, lanes, green, footprint, set_index, set_weight, pixel_scale, panel_index):
    rows, cols = green.shape
    pblocks, blocks = footprint.shape
    width = rows // pblocks
    half = rows // 2
    chips = lanes // 2
    row = lax.axis_index("row")
    core, chip = row & 1, row >> 1
    meta = jnp.stack([core, lax.axis_index("grp")])
    owner = (panel_index[0] * PANEL) // blocks
    swap = [(r, r ^ 1) for r in range(lanes)]
    met = footprint.T
    small = ("row", panel_index, met, set_index, set_weight, pixel_scale.reshape(pblocks, width), green)
    chunks = CHUNKS if chips <= 4 else ((0, 1, 2, 3),)
    batches = BATCHES if len(chunks) == len(CHUNKS) else ((0,),)
    last = len(chunks) - 1

    own, other = prep(chunks[:1], *small)
    start = jnp.where(row == owner, own, lax.ppermute(other, "row", swap))
    rest = prep(chunks[1:], *small) if last else []

    def exchange(shares):
        return [shares[0]] + [
            lax.ppermute(shares[s], "grp", [(g, g ^ s) for g in range(groups)]) for s in range(1, groups)
        ]

    def from_chip(source):
        rounds = spread(source, chips)
        deepest = rounds[-1][0]
        parent = {b: n for n, (_, edges) in enumerate(rounds) for _, b in edges}

        def run(meta, met, green, start, *rest):
            sources = [start]
            for k in range(last):
                sources.append(jnp.where(row == owner, rest[2 * k], lax.ppermute(rest[2 * k + 1], "row", swap)))
            came, held, pieces, parts = {}, list(sources), {}, []
            turned, ready = turn(met, green)
            for step in range(len(chunks) + deepest):
                for n, (depth, edges) in enumerate(rounds):
                    k = step - depth
                    if not 0 <= k <= last:
                        continue
                    if depth == 0:
                        sent = sources[k]
                    else:
                        sent = came[parent[edges[0][0]], k]
                        for a, _ in edges[1:]:
                            sent = jnp.where(chip == a, came[parent[a], k], sent)
                        if k == 0 and depth == 1:
                            sent = after(sent, ready)
                    came[n, k] = lax.ppermute(sent, "row", [(2 * a + c, 2 * b + c) for a, b in edges for c in range(2)])
                    for _, b in edges:
                        held[k] = jnp.where(chip == b, came[n, k], held[k])
                k = step - deepest
                if k >= 0:
                    if k == last and parts:
                        held[k] = after(held[k], *ties)
                    pieces[k] = (held[k], lax.ppermute(held[k], "row", swap))
                    for batch in batches:
                        if k == batch[-1]:
                            shares = gram(groups, meta, turned, [p for b in batch for p in pieces[b]])
                            fresh = exchange(shares[:groups])
                            parts += fresh
                            if TIE == 0:
                                ties = []
                            elif TIE == 1:
                                ties = [shares[groups]]
                            else:
                                ties = [p[:8, :width] * jnp.bfloat16(0) for p in fresh[1:]]
            return total_of(groups, parts, PANEL * width)

        return run

    return lax.switch(owner >> 1, [from_chip(source) for source in range(chips)], meta, met, green, start, *rest)


def solution(mesh):
    in_specs = (P("grp", "row"), P("grp", "row"), P("grp"), P(), P("grp"), P())
    out_specs = P(("row", "grp"), None)
    body = functools.partial(on_device, mesh.shape["grp"], mesh.shape["row"])
    return jax.shard_map(body, mesh=mesh, in_specs=in_specs, out_specs=out_specs, check_vma=False)
```

time: 166 us -> 64.6 us (0.39)
  the two profiles are of different devices: /device:TPU:0 before, /device:TPU:8 now
where the time goes in v1:
time: 64.6 us; the launch traced here: 64.1 us
  waiting for transfers between devices  26.7 us (41%)
  starting transfers between devices  19.3 us (30%)
  Pallas kernels  13.5 us (21%)
  local copies, waits for them, and re-layouts  2.82 us (4%)
  between operations  0.76 us (1%)
    ppermute x12, waiting for transfers between devices, run(): lax.ppermute(sent, 'row', [(2 * a + c, 2 * b + c) for a, b in edges for c...  20.7 us
    ppermute x12, starting transfers between devices, run(): lax.ppermute(sent, 'row', [(2 * a + c, 2 * b + c) for a, b in edges for c...  10.8 us
    ppermute x6, starting transfers between devices, exchange(): lax.ppermute(shares[s], 'grp', [(g, g ^ s) for g in range(groups)])  7.04 us
    ppermute x6, waiting for transfers between devices, exchange(): lax.ppermute(shares[s], 'grp', [(g, g ^ s) for g in range(groups)])  6.03 us
    pallas_call x2, Pallas kernels, gram(): pl.pallas_call(functools.partial(gram_body, shares, len(pieces)), in_spec...  4.83 us
    pallas_call x2, Pallas kernels, prep(): pl.pallas_call(functools.partial(prep_body, chunks, lane, width), in_spec...  4.73 us
    pallas_call x1, Pallas kernels, turn(): pl.pallas_call(functools.partial(turn_body, blocks, width, pblocks // ste...  3.8 us
    cond x4, local copies, waits for them, and re-layouts  2.02 us
  transfers between devices with their start and end apart: 26, of which 8 were waited for; matrix products, arithmetic and copies ran while one was open for 1% of the time, Pallas kernels for 18%

profile of v1, /device:TPU:8, one launch (start us, length us, event | category | flops | bytes accessed | tf_op | source)
XLA Modules:
  0.0 64.1 jit_solution(11153395831404997581)
XLA Ops:
  0.7 2.1 %weigh_panel.2 = (bf16[1024,128]{1,0:T(8,128)(2,1)S(1)}, bf16[1024,128]{1,0:T(8,128)(2,1)}) custom-call(s32[1]{0:T(128)S(6)} %copy.15.panel, s32[8,16]{1,0:T(8,128)} %bitcast.21, s32[16]{0:T(128)} %set_hbm.3, f32[8]{0:T(128)} %sw_hbm.3, f32[16,128]{1,0:T(8,128)} %bitcast.27, bf16[2048,1024]{1,0:T(8,128)(2,1)} %green_hbm.3), custom_call_target="tpu_custom_call" | custom-call | tf_op jit(solution)/shard_map/weigh_panel/pallas_call | solution.py:64
  2.8 2.7 %weigh_panel.3 = (bf16[1024,128]{1,0:T(8,128)(2,1)S(1)}, bf16[1024,128]{1,0:T(8,128)(2,1)S(1)}, bf16[1024,128]{1,0:T(8,128)(2,1)S(1)}, bf16[1024,128]{1,0:T(8,12...) custom-call(s32[1]{0:T(128)S(6)} %copy.15.panel, s32[8,16]{1,0:T(8,128)S(1)} %bitcast.22, s32[16]{0:T(128)} %set_hbm.3, ...), custom_call_target="tpu_custom_call" | custom-call | tf_op jit(solution)/shard_map/weigh_panel/pallas_call | solution.py:64
  5.6 57.6 %conditional.1 = (f32[256,512]{1,0:T(8,128)S(1)}) conditional(s32[]{:T(128)} %clamp.3, (s32[8,16]{1,0:T(8,128)S(1)}, bf16[2048,1024]{1,0:T(8,128)(2,1)}, s32[]{:T(128)}, s32[]{:T(128)}, s32[]{:T(128)}, /*index=5*/s32[]{:T(128)}, bf16[1024,128]{1,0:T(8,128)(2,1)S(1)}, bf16[1024,128]{1,0:T(8,128)(2,1)S(1)}, ...), branch_computations={%region_0.1_spmd, %region_1.2_spmd, %region_2.3_spmd, %region_3.4_... | conditional | flops 2359302 | bytes 65538668 | solution.py:279
  5.6 0.5 collective-permute-start.4
  6.2 0.7 %collective-permute-start = (bf16[1024,128]{1,0:T(8,128)(2,1)S(1)}, bf16[1024,128]{1,0:T(8,128)(2,1)S(1)}, u32[]{:S(2)}, u32[]{:S(2)}) collective-permute-start(bf16[1024,128]{1,0:T(8,128)(2,1)S(1)} %broadcast_select_fusion), channel_id=1, source_target_pairs={{0,4},{1,5},{8,12},{9,13},{16,20},{17,21},{24,28},{25,29}} | collective-permute-start | bytes 786440 | tf_op jit(solution)/shard_map/cond/branch_0_fun/ppermute | solution.py:256
  7.4 3.8 %mask_and_turn.4 = (bf16[1024,2048]{1,0:T(8,128)(2,1)S(1)}, bf16[8,128]{1,0:T(8,128)(2,1)S(1)}) custom-call(s32[8,16]{1,0:T(8,128)S(1)} %get-tuple-element.114.fp_ref, bf16[2048,1024]{1,0:T(8,128)(2,1)} %get-tuple-element.116.green_ref), custom_call_target="tpu_custom_call" | custom-call | tf_op jit(solution)/shard_map/cond/branch_0_fun/mask_and_turn/pallas_call | solution.py:98
  11.2 2.0 %copy-done = bf16[1024,2048]{1,0:T(8,128)(2,1)} copy-done((bf16[1024,2048]{1,0:T(8,128)(2,1)}, bf16[1024,2048]{1,0:T(8,128)(2,1)S(1)}, u32[]{:S(2)}) %copy-start) | copy-done | bytes 4194328 | tf_op jit(solution)/shard_map/cond
  13.3 0.7 %collective-permute-start.5 = (bf16[1024,128]{1,0:T(8,128)(2,1)S(1)}, bf16[1024,128]{1,0:T(8,128)(2,1)S(1)}, u32[]{:S(2)}, u32[]{:S(2)}) collective-permute-start(bf16[1024,128]{1,0:T(8,128)(2,1)S(1)} %broadcast_select_fusion.3), channel_id=1, source_target_pairs={{0,4},{1,5},{8,12},{9,13},{16,20},{17,21},{24,28},{25,29}} | collective-permute-start | bytes 786440 | tf_op jit(solution)/shard_map/cond/branch_0_fun/ppermute | solution.py:256
  14.0 0.7 %collective-permute-start.1 = (bf16[1024,128]{1,0:T(8,128)(2,1)S(1)}, bf16[1024,128]{1,0:T(8,128)(2,1)S(1)}, u32[]{:S(2)}, u32[]{:S(2)}) collective-permute-start(bf16[1024,128]{1,0:T(8,128)(2,1)S(1)} %broadcast_add_fusion), channel_id=1, source_target_pairs={{4,6},{5,7},{12,14},{13,15},{20,22},{21,23},{28,30},{29,31}} | collective-permute-start | bytes 786440 | tf_op jit(solution)/shard_map/cond/branch_0_fun/ppermute | solution.py:256
  14.8 0.7 %collective-permute-start.13 = (bf16[1024,128]{1,0:T(8,128)(2,1)S(1)}, bf16[1024,128]{1,0:T(8,128)(2,1)S(1)}, u32[]{:S(2)}, u32[]{:S(2)}) collective-permute-start(bf16[1024,128]{1,0:T(8,128)(2,1)S(1)} %broadcast_select_fusion.2), channel_id=1, source_target_pairs={{0,4},{1,5},{8,12},{9,13},{16,20},{17,21},{24,28},{25,29}} | collective-permute-start | bytes 786440 | tf_op jit(solution)/shard_map/cond/branch_0_fun/ppermute | solution.py:256
  15.4 1.3 %collective-permute-start.2 = (bf16[1024,128]{1,0:T(8,128)(2,1)S(1)}, bf16[1024,128]{1,0:T(8,128)(2,1)S(1)}, u32[]{:S(2)}, u32[]{:S(2)}) collective-permute-start(bf16[1024,128]{1,0:T(8,128)(2,1)S(1)} %broadcast_add_fusion), channel_id=1, source_target_pairs={{4,2},{5,3},{12,10},{13,11},{20,18},{21,19},{28,26},{29,27}} | collective-permute-start | bytes 786440 | tf_op jit(solution)/shard_map/cond/branch_0_fun/ppermute | solution.py:256
  16.8 0.8 %collective-permute-start.6 = (bf16[1024,128]{1,0:T(8,128)(2,1)S(1)}, bf16[1024,128]{1,0:T(8,128)(2,1)S(1)}, u32[]{:S(2)}, u32[]{:S(2)}) collective-permute-start(bf16[1024,128]{1,0:T(8,128)(2,1)S(1)} %collective-permute-done.5), channel_id=1, source_target_pairs={{4,6},{5,7},{12,14},{13,15},{20,22},{21,23},{28,30},{29,31}} | collective-permute-start | bytes 786440 | tf_op jit(solution)/shard_map/cond/branch_0_fun/ppermute | solution.py:256
  17.6 1.4 %collective-permute-start.7 = (bf16[1024,128]{1,0:T(8,128)(2,1)S(1)}, bf16[1024,128]{1,0:T(8,128)(2,1)S(1)}, u32[]{:S(2)}, u32[]{:S(2)}) collective-permute-start(bf16[1024,128]{1,0:T(8,128)(2,1)S(1)} %collective-permute-done.5), channel_id=1, source_target_pairs={{4,2},{5,3},{12,10},{13,11},{20,18},{21,19},{28,26},{29,27}} | collective-permute-start | bytes 786440 | tf_op jit(solution)/shard_map/cond/branch_0_fun/ppermute | solution.py:256
  19.1 0.7 %collective-permute-start.18 = (bf16[1024,128]{1,0:T(8,128)(2,1)S(1)}, bf16[1024,128]{1,0:T(8,128)(2,1)S(1)}, u32[]{:S(2)}, u32[]{:S(2)}) collective-permute-start(bf16[1024,128]{1,0:T(8,128)(2,1)S(1)} %broadcast_select_fusion.1), channel_id=1, source_target_pairs={{0,4},{1,5},{8,12},{9,13},{16,20},{17,21},{24,28},{25,29}} | collective-permute-start | bytes 786440 | tf_op jit(solution)/shard_map/cond/branch_0_fun/ppermute | solution.py:256
  19.8 0.7 %collective-permute-start.14 = (bf16[1024,128]{1,0:T(8,128)(2,1)S(1)}, bf16[1024,128]{1,0:T(8,128)(2,1)S(1)}, u32[]{:S(2)}, u32[]{:S(2)}) collective-permute-start(bf16[1024,128]{1,0:T(8,128)(2,1)S(1)} %collective-permute-done.13), channel_id=1, source_target_pairs={{4,6},{5,7},{12,14},{13,15},{20,22},{21,23},{28,30},{29,31}} | collective-permute-start | bytes 786440 | tf_op jit(solution)/shard_map/cond/branch_0_fun/ppermute | solution.py:256
  20.5 7.9 %collective-permute-done.2 = bf16[1024,128]{1,0:T(8,128)(2,1)S(1)} collective-permute-done((bf16[1024,128]{1,0:T(8,128)(2,1)S(1)}, bf16[1024,128]{1,0:T(8,128)(2,1)S(1)}, u32[]{:S(2)}, u32[]{:S(2)}) %collective-permute-start.2) | collective-permute-done | bytes 262176 | tf_op jit(solution)/shard_map/cond/branch_0_fun/ppermute | solution.py:256
  28.4 1.3 %collective-permute-start.15 = (bf16[1024,128]{1,0:T(8,128)(2,1)S(1)}, bf16[1024,128]{1,0:T(8,128)(2,1)S(1)}, u32[]{:S(2)}, u32[]{:S(2)}) collective-permute-start(bf16[1024,128]{1,0:T(8,128)(2,1)S(1)} %collective-permute-done.13), channel_id=1, source_target_pairs={{4,2},{5,3},{12,10},{13,11},{20,18},{21,19},{28,26},{29,27}} | collective-permute-start | bytes 786440 | tf_op jit(solution)/shard_map/cond/branch_0_fun/ppermute | solution.py:256
  29.8 5.6 %collective-permute-done.7 = bf16[1024,128]{1,0:T(8,128)(2,1)S(1)} collective-permute-done((bf16[1024,128]{1,0:T(8,128)(2,1)S(1)}, bf16[1024,128]{1,0:T(8,128)(2,1)S(1)}, u32[]{:S(2)}, u32[]{:S(2)}) %collective-permute-start.7) | collective-permute-done | bytes 262176 | tf_op jit(solution)/shard_map/cond/branch_0_fun/ppermute | solution.py:256
  35.6 0.7 %collective-permute-start.19 = (bf16[1024,128]{1,0:T(8,128)(2,1)S(1)}, bf16[1024,128]{1,0:T(8,128)(2,1)S(1)}, u32[]{:S(2)}, u32[]{:S(2)}) collective-permute-start(bf16[1024,128]{1,0:T(8,128)(2,1)S(1)} %collective-permute-done.18), channel_id=1, source_target_pairs={{4,6},{5,7},{12,14},{13,15},{20,22},{21,23},{28,30},{29,31}} | collective-permute-start | bytes 786440 | tf_op jit(solution)/shard_map/cond/branch_0_fun/ppermute | solution.py:256
  36.3 1.3 %collective-permute-start.20 = (bf16[1024,128]{1,0:T(8,128)(2,1)S(1)}, bf16[1024,128]{1,0:T(8,128)(2,1)S(1)}, u32[]{:S(2)}, u32[]{:S(2)}) collective-permute-start(bf16[1024,128]{1,0:T(8,128)(2,1)S(1)} %collective-permute-done.18), channel_id=1, source_target_pairs={{4,2},{5,3},{12,10},{13,11},{20,18},{21,19},{28,26},{29,27}} | collective-permute-start | bytes 786440 | tf_op jit(solution)/shard_map/cond/branch_0_fun/ppermute | solution.py:256
  37.6 3.5 %collective-permute-done.15 = bf16[1024,128]{1,0:T(8,128)(2,1)S(1)} collective-permute-done((bf16[1024,128]{1,0:T(8,128)(2,1)S(1)}, bf16[1024,128]{1,0:T(8,128)(2,1)S(1)}, u32[]{:S(2)}, u32[]{:S(2)}) %collective-permute-start.15) | collective-permute-done | bytes 262176 | tf_op jit(solution)/shard_map/cond/branch_0_fun/ppermute | solution.py:256
  41.3 2.4 %partial_gram.8 = (f32[256,256]{1,0:T(8,128)S(1)}, bf16[256,256]{1,0:T(8,128)(2,1)S(1)}, bf16[256,256]{1,0:T(8,128)(2,1)S(1)}, bf16[256,256]{1,0:T(8,128)(2,1)S(1)}, bf16[8,128]{1,0:T(8,128)(2,1)S(1)}) custom-call(s32[2]{0:T(128)S(1)} %get-tuple-element.112.meta, bf16[1024,2048]{1,0:T(8,128)(2,1)S(1)} %copy-done.1, ...), custom_call_target="tpu_custom_call" | custom-call | tf_op jit(solution)/shard_map/cond/branch_0_fun/partial_gram/pallas_call | solution.py:139
  43.6 3.6 %collective-permute-done.20 = bf16[1024,128]{1,0:T(8,128)(2,1)S(1)} collective-permute-done((bf16[1024,128]{1,0:T(8,128)(2,1)S(1)}, bf16[1024,128]{1,0:T(8,128)(2,1)S(1)}, u32[]{:S(2)}, u32[]{:S(2)}) %collective-permute-start.20) | collective-permute-done | bytes 262176 | tf_op jit(solution)/shard_map/cond/branch_0_fun/ppermute | solution.py:256
  47.4 1.6 %collective-permute-start.9 = (bf16[256,256]{1,0:T(8,128)(2,1)S(1)}, bf16[256,256]{1,0:T(8,128)(2,1)S(1)}, u32[]{:S(2)}, u32[]{:S(2)}) collective-permute-start(bf16[256,256]{1,0:T(8,128)(2,1)S(1)} %get-tuple-element.126), channel_id=1, source_target_pairs={{0,8},{8,0},{16,24},{24,16},{1,9},{9,1},{17,25},{25,17},{2,10},{10... | collective-permute-start | bytes 393224 | tf_op jit(solution)/shard_map/cond/branch_0_fun/ppermute | solution.py:229
  48.9 1.5 %collective-permute-start.10 = (bf16[256,256]{1,0:T(8,128)(2,1)S(1)}, bf16[256,256]{1,0:T(8,128)(2,1)S(1)}, u32[]{:S(2)}, u32[]{:S(2)}) collective-permute-start(bf16[256,256]{1,0:T(8,128)(2,1)S(1)} %get-tuple-element.127), channel_id=1, source_target_pairs={{0,16},{8,24},{16,0},{24,8},{1,17},{9,25},{17,1},{25,9},{2,18},{10... | collective-permute-start | bytes 393224 | tf_op jit(solution)/shard_map/cond/branch_0_fun/ppermute | solution.py:229
  50.9 2.5 %partial_gram.9 = (f32[256,256]{1,0:T(8,128)S(1)}, bf16[256,256]{1,0:T(8,128)(2,1)S(1)}, bf16[256,256]{1,0:T(8,128)(2,1)S(1)}, bf16[256,256]{1,0:T(8,128)(2,1)S(1)}, bf16[8,128]{1,0:T(8,128)(2,1)}) custom-call(s32[2]{0:T(128)S(1)} %get-tuple-element.112.meta, bf16[1024,2048]{1,0:T(8,128)(2,1)S(1)} %copy-done.1, ...), custom_call_target="tpu_custom_call" | custom-call | tf_op jit(solution)/shard_map/cond/branch_0_fun/partial_gram/pallas_call | solution.py:139
  53.4 1.5 %collective-permute-start.22 = (bf16[256,256]{1,0:T(8,128)(2,1)S(1)}, bf16[256,256]{1,0:T(8,128)(2,1)S(1)}, u32[]{:S(2)}, u32[]{:S(2)}) collective-permute-start(bf16[256,256]{1,0:T(8,128)(2,1)S(1)} %get-tuple-element.135), channel_id=1, source_target_pairs={{0,8},{8,0},{16,24},{24,16},{1,9},{9,1},{17,25},{25,17},{2,10},{10... | collective-permute-start | bytes 393224 | tf_op jit(solution)/shard_map/cond/branch_0_fun/ppermute | solution.py:229
  54.9 1.5 %collective-permute-start.23 = (bf16[256,256]{1,0:T(8,128)(2,1)S(1)}, bf16[256,256]{1,0:T(8,128)(2,1)S(1)}, u32[]{:S(2)}, u32[]{:S(2)}) collective-permute-start(bf16[256,256]{1,0:T(8,128)(2,1)S(1)} %get-tuple-element.136), channel_id=1, source_target_pairs={{0,16},{8,24},{16,0},{24,8},{1,17},{9,25},{17,1},{25,9},{2,18},{10... | collective-permute-start | bytes 393224 | tf_op jit(solution)/shard_map/cond/branch_0_fun/ppermute | solution.py:229
  56.4 0.5 collective-permute-start.24
  57.6 2.3 %collective-permute-done.22.refs_5_ = bf16[256,256]{1,0:T(8,128)(2,1)S(1)} collective-permute-done((bf16[256,256]{1,0:T(8,128)(2,1)S(1)}, bf16[256,256]{1,0:T(8,128)(2,1)S(1)}, u32[]{:S(2)}, u32[]{:S(2)}) %collective-permute-start.22) | collective-permute-done | bytes 131104 | tf_op jit(solution)/shard_map/cond/branch_0_fun/ppermute | solution.py:229
  59.8 3.1 %collective-permute-done.23.refs_6_ = bf16[256,256]{1,0:T(8,128)(2,1)S(1)} collective-permute-done((bf16[256,256]{1,0:T(8,128)(2,1)S(1)}, bf16[256,256]{1,0:T(8,128)(2,1)S(1)}, u32[]{:S(2)}, u32[]{:S(2)}) %collective-permute-start.23) | collective-permute-done | bytes 131104 | tf_op jit(solution)/shard_map/cond/branch_0_fun/ppermute | solution.py:229
  63.3 0.8 %copy-done.8 = f32[256,512]{1,0:T(8,128)} copy-done((f32[256,512]{1,0:T(8,128)}, f32[256,512]{1,0:T(8,128)S(1)}, u32[]{:S(2)}) %copy-start.8) | copy-done | bytes 524312
  (47 shorter events, 2.7 us)
Async XLA Ops:
  0.0 2.8 %copy-start.9 = (s32[16,8]{0,1:T(8,128)S(1)}, s32[16,8]{0,1:T(8,128)}, u32[]{:S(2)}) copy-start(s32[16,8]{0,1:T(8,128)} %param.11) | copy-start | bytes 1540
  2.8 2.9 %collective-permute-start.100 = (bf16[1024,128]{1,0:T(8,128)(2,1)}, bf16[1024,128]{1,0:T(8,128)(2,1)S(1)}, u32[]{:S(2)}, u32[]{:S(2)}) collective-permute-start(bf16[1024,128]{1,0:T(8,128)(2,1)} %get-tuple-element.219), channel_id=1, source_target_pairs={{0,1},{1,0},{2,3},{3,2},{4,5},{5,4},{6,7},{7,6},{8,9},{9,8},{10,11... | collective-permute-start | bytes 786440 | tf_op jit(solution)/shard_map/ppermute | solution.py:224
  5.6 7.6 %collective-permute-start.4 = (bf16[1024,128]{1,0:T(8,128)(2,1)S(1)}, bf16[1024,128]{1,0:T(8,128)(2,1)S(1)}, u32[]{:S(2)}, u32[]{:S(2)}) collective-permute-start(bf16[1024,128]{1,0:T(8,128)(2,1)S(1)} %get-tuple-element.124), channel_id=1, source_target_pairs={{0,1},{1,0},{2,3},{3,2},{4,5},{5,4},{6,7},{7,6},{8,9},{9,8},{10,11... | collective-permute-start | bytes 786440 | tf_op jit(solution)/shard_map/cond/branch_0_fun/ppermute | solution.py:240
  6.2 7.8 %collective-permute-start = (bf16[1024,128]{1,0:T(8,128)(2,1)S(1)}, bf16[1024,128]{1,0:T(8,128)(2,1)S(1)}, u32[]{:S(2)}, u32[]{:S(2)}) collective-permute-start(bf16[1024,128]{1,0:T(8,128)(2,1)S(1)} %broadcast_select_fusion), channel_id=1, source_target_pairs={{0,4},{1,5},{8,12},{9,13},{16,20},{17,21},{24,28},{25,29}} | collective-permute-start | bytes 786440 | tf_op jit(solution)/shard_map/cond/branch_0_fun/ppermute | solution.py:256
  6.9 7.9 %collective-permute-start.12 = (bf16[1024,128]{1,0:T(8,128)(2,1)}, bf16[1024,128]{1,0:T(8,128)(2,1)S(1)}, u32[]{:S(2)}, u32[]{:S(2)}) collective-permute-start(bf16[1024,128]{1,0:T(8,128)(2,1)} %get-tuple-element.130), channel_id=1, source_target_pairs={{0,1},{1,0},{2,3},{3,2},{4,5},{5,4},{6,7},{7,6},{8,9},{9,8},{10,11... | collective-permute-start | bytes 786440 | tf_op jit(solution)/shard_map/cond/branch_0_fun/ppermute | solution.py:240
  7.0 10.6 %collective-permute-start.17 = (bf16[1024,128]{1,0:T(8,128)(2,1)}, bf16[1024,128]{1,0:T(8,128)(2,1)S(1)}, u32[]{:S(2)}, u32[]{:S(2)}) collective-permute-start(bf16[1024,128]{1,0:T(8,128)(2,1)} %get-tuple-element.132), channel_id=1, source_target_pairs={{0,1},{1,0},{2,3},{3,2},{4,5},{5,4},{6,7},{7,6},{8,9},{9,8},{10,11... | collective-permute-start | bytes 786440 | tf_op jit(solution)/shard_map/cond/branch_0_fun/ppermute | solution.py:240
  11.2 2.0 %copy-start = (bf16[1024,2048]{1,0:T(8,128)(2,1)}, bf16[1024,2048]{1,0:T(8,128)(2,1)S(1)}, u32[]{:S(2)}) copy-start(bf16[1024,2048]{1,0:T(8,128)(2,1)S(1)} %get-tuple-element.117.turned_ref) | copy-start | bytes 12582916 | tf_op jit(solution)/shard_map/cond
  13.3 3.5 %collective-permute-start.5 = (bf16[1024,128]{1,0:T(8,128)(2,1)S(1)}, bf16[1024,128]{1,0:T(8,128)(2,1)S(1)}, u32[]{:S(2)}, u32[]{:S(2)}) collective-permute-start(bf16[1024,128]{1,0:T(8,128)(2,1)S(1)} %broadcast_select_fusion.3), channel_id=1, source_target_pairs={{0,4},{1,5},{8,12},{9,13},{16,20},{17,21},{24,28},{25,29}} | collective-permute-start | bytes 786440 | tf_op jit(solution)/shard_map/cond/branch_0_fun/ppermute | solution.py:256
  14.0 5.0 %collective-permute-start.1 = (bf16[1024,128]{1,0:T(8,128)(2,1)S(1)}, bf16[1024,128]{1,0:T(8,128)(2,1)S(1)}, u32[]{:S(2)}, u32[]{:S(2)}) collective-permute-start(bf16[1024,128]{1,0:T(8,128)(2,1)S(1)} %broadcast_add_fusion), channel_id=1, source_target_pairs={{4,6},{5,7},{12,14},{13,15},{20,22},{21,23},{28,30},{29,31}} | collective-permute-start | bytes 786440 | tf_op jit(solution)/shard_map/cond/branch_0_fun/ppermute | solution.py:256
  14.8 5.0 %collective-permute-start.13 = (bf16[1024,128]{1,0:T(8,128)(2,1)S(1)}, bf16[1024,128]{1,0:T(8,128)(2,1)S(1)}, u32[]{:S(2)}, u32[]{:S(2)}) collective-permute-start(bf16[1024,128]{1,0:T(8,128)(2,1)S(1)} %broadcast_select_fusion.2), channel_id=1, source_target_pairs={{0,4},{1,5},{8,12},{9,13},{16,20},{17,21},{24,28},{25,29}} | collective-permute-start | bytes 786440 | tf_op jit(solution)/shard_map/cond/branch_0_fun/ppermute | solution.py:256
  15.4 13.0 %collective-permute-start.2 = (bf16[1024,128]{1,0:T(8,128)(2,1)S(1)}, bf16[1024,128]{1,0:T(8,128)(2,1)S(1)}, u32[]{:S(2)}, u32[]{:S(2)}) collective-permute-start(bf16[1024,128]{1,0:T(8,128)(2,1)S(1)} %broadcast_add_fusion), channel_id=1, source_target_pairs={{4,2},{5,3},{12,10},{13,11},{20,18},{21,19},{28,26},{29,27}} | collective-permute-start | bytes 786440 | tf_op jit(solution)/shard_map/cond/branch_0_fun/ppermute | solution.py:256
  16.8 24.5 %copy-start.1 = (bf16[1024,2048]{1,0:T(8,128)(2,1)S(1)}, bf16[1024,2048]{1,0:T(8,128)(2,1)}, u32[]{:S(2)}) copy-start(bf16[1024,2048]{1,0:T(8,128)(2,1)} %copy-done) | copy-start | bytes 12582916 | tf_op jit(solution)/shard_map/cond
  16.8 13.0 %collective-permute-start.6 = (bf16[1024,128]{1,0:T(8,128)(2,1)S(1)}, bf16[1024,128]{1,0:T(8,128)(2,1)S(1)}, u32[]{:S(2)}, u32[]{:S(2)}) collective-permute-start(bf16[1024,128]{1,0:T(8,128)(2,1)S(1)} %collective-permute-done.5), channel_id=1, source_target_pairs={{4,6},{5,7},{12,14},{13,15},{20,22},{21,23},{28,30},{29,31}} | collective-permute-start | bytes 786440 | tf_op jit(solution)/shard_map/cond/branch_0_fun/ppermute | solution.py:256
  17.6 17.9 %collective-permute-start.7 = (bf16[1024,128]{1,0:T(8,128)(2,1)S(1)}, bf16[1024,128]{1,0:T(8,128)(2,1)S(1)}, u32[]{:S(2)}, u32[]{:S(2)}) collective-permute-start(bf16[1024,128]{1,0:T(8,128)(2,1)S(1)} %collective-permute-done.5), channel_id=1, source_target_pairs={{4,2},{5,3},{12,10},{13,11},{20,18},{21,19},{28,26},{29,27}} | collective-permute-start | bytes 786440 | tf_op jit(solution)/shard_map/cond/branch_0_fun/ppermute | solution.py:256
  19.1 16.5 %collective-permute-start.18 = (bf16[1024,128]{1,0:T(8,128)(2,1)S(1)}, bf16[1024,128]{1,0:T(8,128)(2,1)S(1)}, u32[]{:S(2)}, u32[]{:S(2)}) collective-permute-start(bf16[1024,128]{1,0:T(8,128)(2,1)S(1)} %broadcast_select_fusion.1), channel_id=1, source_target_pairs={{0,4},{1,5},{8,12},{9,13},{16,20},{17,21},{24,28},{25,29}} | collective-permute-start | bytes 786440 | tf_op jit(solution)/shard_map/cond/branch_0_fun/ppermute | solution.py:256
  19.8 16.5 %collective-permute-start.14 = (bf16[1024,128]{1,0:T(8,128)(2,1)S(1)}, bf16[1024,128]{1,0:T(8,128)(2,1)S(1)}, u32[]{:S(2)}, u32[]{:S(2)}) collective-permute-start(bf16[1024,128]{1,0:T(8,128)(2,1)S(1)} %collective-permute-done.13), channel_id=1, source_target_pairs={{4,6},{5,7},{12,14},{13,15},{20,22},{21,23},{28,30},{29,31}} | collective-permute-start | bytes 786440 | tf_op jit(solution)/shard_map/cond/branch_0_fun/ppermute | solution.py:256
  28.4 12.7 %collective-permute-start.15 = (bf16[1024,128]{1,0:T(8,128)(2,1)S(1)}, bf16[1024,128]{1,0:T(8,128)(2,1)S(1)}, u32[]{:S(2)}, u32[]{:S(2)}) collective-permute-start(bf16[1024,128]{1,0:T(8,128)(2,1)S(1)} %collective-permute-done.13), channel_id=1, source_target_pairs={{4,2},{5,3},{12,10},{13,11},{20,18},{21,19},{28,26},{29,27}} | collective-permute-start | bytes 786440 | tf_op jit(solution)/shard_map/cond/branch_0_fun/ppermute | solution.py:256
  29.8 11.5 %collective-permute-start.3 = (bf16[1024,128]{1,0:T(8,128)(2,1)S(1)}, bf16[1024,128]{1,0:T(8,128)(2,1)S(1)}, u32[]{:S(2)}, u32[]{:S(2)}) collective-permute-start(bf16[1024,128]{1,0:T(8,128)(2,1)S(1)} %select_select_fusion.2.refs_0_), channel_id=1, source_target_pairs={{0,1},{1,0},{2,3},{3,2},{4,5},{5,4},{6,7},{7,6},{8,9},{9,8},{10,11... | collective-permute-start | bytes 786440 | tf_op jit(solution)/shard_map/cond/branch_0_fun/ppermute | solution.py:263
  35.5 5.7 %collective-permute-start.8 = (bf16[1024,128]{1,0:T(8,128)(2,1)S(1)}, bf16[1024,128]{1,0:T(8,128)(2,1)S(1)}, u32[]{:S(2)}, u32[]{:S(2)}) collective-permute-start(bf16[1024,128]{1,0:T(8,128)(2,1)S(1)} %select_select_fusion.1.refs_2_), channel_id=1, source_target_pairs={{0,1},{1,0},{2,3},{3,2},{4,5},{5,4},{6,7},{7,6},{8,9},{9,8},{10,11... | collective-permute-start | bytes 786440 | tf_op jit(solution)/shard_map/cond/branch_0_fun/ppermute | solution.py:263
  35.6 8.0 %collective-permute-start.19 = (bf16[1024,128]{1,0:T(8,128)(2,1)S(1)}, bf16[1024,128]{1,0:T(8,128)(2,1)S(1)}, u32[]{:S(2)}, u32[]{:S(2)}) collective-permute-start(bf16[1024,128]{1,0:T(8,128)(2,1)S(1)} %collective-permute-done.18), channel_id=1, source_target_pairs={{4,6},{5,7},{12,14},{13,15},{20,22},{21,23},{28,30},{29,31}} | collective-permute-start | bytes 786440 | tf_op jit(solution)/shard_map/cond/branch_0_fun/ppermute | solution.py:256
  36.3 10.9 %collective-permute-start.20 = (bf16[1024,128]{1,0:T(8,128)(2,1)S(1)}, bf16[1024,128]{1,0:T(8,128)(2,1)S(1)}, u32[]{:S(2)}, u32[]{:S(2)}) collective-permute-start(bf16[1024,128]{1,0:T(8,128)(2,1)S(1)} %collective-permute-done.18), channel_id=1, source_target_pairs={{4,2},{5,3},{12,10},{13,11},{20,18},{21,19},{28,26},{29,27}} | collective-permute-start | bytes 786440 | tf_op jit(solution)/shard_map/cond/branch_0_fun/ppermute | solution.py:256
  41.2 9.8 %collective-permute-start.16 = (bf16[1024,128]{1,0:T(8,128)(2,1)S(1)}, bf16[1024,128]{1,0:T(8,128)(2,1)S(1)}, u32[]{:S(2)}, u32[]{:S(2)}) collective-permute-start(bf16[1024,128]{1,0:T(8,128)(2,1)S(1)} %select_select_fusion.refs_0_), channel_id=1, source_target_pairs={{0,1},{1,0},{2,3},{3,2},{4,5},{5,4},{6,7},{7,6},{8,9},{9,8},{10,11... | collective-permute-start | bytes 786440 | tf_op jit(solution)/shard_map/cond/branch_0_fun/ppermute | solution.py:263
  47.3 3.6 %collective-permute-start.21 = (bf16[1024,128]{1,0:T(8,128)(2,1)S(1)}, bf16[1024,128]{1,0:T(8,128)(2,1)S(1)}, u32[]{:S(2)}, u32[]{:S(2)}) collective-permute-start(bf16[1024,128]{1,0:T(8,128)(2,1)S(1)} %select_add_fusion.refs_2_), channel_id=1, source_target_pairs={{0,1},{1,0},{2,3},{3,2},{4,5},{5,4},{6,7},{7,6},{8,9},{9,8},{10,11... | collective-permute-start | bytes 786440 | tf_op jit(solution)/shard_map/cond/branch_0_fun/ppermute | solution.py:263
  47.4 9.0 %collective-permute-start.9 = (bf16[256,256]{1,0:T(8,128)(2,1)S(1)}, bf16[256,256]{1,0:T(8,128)(2,1)S(1)}, u32[]{:S(2)}, u32[]{:S(2)}) collective-permute-start(bf16[256,256]{1,0:T(8,128)(2,1)S(1)} %get-tuple-element.126), channel_id=1, source_target_pairs={{0,8},{8,0},{16,24},{24,16},{1,9},{9,1},{17,25},{25,17},{2,10},{10... | collective-permute-start | bytes 393224 | tf_op jit(solution)/shard_map/cond/branch_0_fun/ppermute | solution.py:229
  48.9 8.2 %collective-permute-start.10 = (bf16[256,256]{1,0:T(8,128)(2,1)S(1)}, bf16[256,256]{1,0:T(8,128)(2,1)S(1)}, u32[]{:S(2)}, u32[]{:S(2)}) collective-permute-start(bf16[256,256]{1,0:T(8,128)(2,1)S(1)} %get-tuple-element.127), channel_id=1, source_target_pairs={{0,16},{8,24},{16,0},{24,8},{1,17},{9,25},{17,1},{25,9},{2,18},{10... | collective-permute-start | bytes 393224 | tf_op jit(solution)/shard_map/cond/branch_0_fun/ppermute | solution.py:229
  50.5 7.1 %collective-permute-start.11 = (bf16[256,256]{1,0:T(8,128)(2,1)S(1)}, bf16[256,256]{1,0:T(8,128)(2,1)S(1)}, u32[]{:S(2)}, u32[]{:S(2)}) collective-permute-start(bf16[256,256]{1,0:T(8,128)(2,1)S(1)} %get-tuple-element.128), channel_id=1, source_target_pairs={{0,24},{8,16},{16,8},{24,0},{1,25},{9,17},{17,9},{25,1},{2,26},{10... | collective-permute-start | bytes 393224 | tf_op jit(solution)/shard_map/cond/branch_0_fun/ppermute | solution.py:229
  53.4 6.4 %collective-permute-start.22 = (bf16[256,256]{1,0:T(8,128)(2,1)S(1)}, bf16[256,256]{1,0:T(8,128)(2,1)S(1)}, u32[]{:S(2)}, u32[]{:S(2)}) collective-permute-start(bf16[256,256]{1,0:T(8,128)(2,1)S(1)} %get-tuple-element.135), channel_id=1, source_target_pairs={{0,8},{8,0},{16,24},{24,16},{1,9},{9,1},{17,25},{25,17},{2,10},{10... | collective-permute-start | bytes 393224 | tf_op jit(solution)/shard_map/cond/branch_0_fun/ppermute | solution.py:229
  54.9 8.0 %collective-permute-start.23 = (bf16[256,256]{1,0:T(8,128)(2,1)S(1)}, bf16[256,256]{1,0:T(8,128)(2,1)S(1)}, u32[]{:S(2)}, u32[]{:S(2)}) collective-permute-start(bf16[256,256]{1,0:T(8,128)(2,1)S(1)} %get-tuple-element.136), channel_id=1, source_target_pairs={{0,16},{8,24},{16,0},{24,8},{1,17},{9,25},{17,1},{25,9},{2,18},{10... | collective-permute-start | bytes 393224 | tf_op jit(solution)/shard_map/cond/branch_0_fun/ppermute | solution.py:229
  56.4 6.5 %collective-permute-start.24 = (bf16[256,256]{1,0:T(8,128)(2,1)S(1)}, bf16[256,256]{1,0:T(8,128)(2,1)S(1)}, u32[]{:S(2)}, u32[]{:S(2)}) collective-permute-start(bf16[256,256]{1,0:T(8,128)(2,1)S(1)} %get-tuple-element.137), channel_id=1, source_target_pairs={{0,24},{8,16},{16,8},{24,0},{1,25},{9,17},{17,9},{25,1},{2,26},{10... | collective-permute-start | bytes 393224 | tf_op jit(solution)/shard_map/cond/branch_0_fun/ppermute | solution.py:229
  63.3 0.8 %copy-start.8 = (f32[256,512]{1,0:T(8,128)}, f32[256,512]{1,0:T(8,128)S(1)}, u32[]{:S(2)}) copy-start(f32[256,512]{1,0:T(8,128)S(1)} %get-tuple-element.372) | copy-start | bytes 1572868

commit v2 on v1

--- a/solution.py
+++ b/solution.py
@@ -10,7 +10,10 @@
 CHUNKS = ((0,), (1,), (2,), (3,))
 BATCHES = ((0, 1), (2, 3))
 TIE = 1
-VMEM_LIMIT = 24 * 1024 * 1024
+MERGE = False
+FULL = True
+GATE = "held"
+VMEM_LIMIT = 16 * 1024 * 1024
 PREP_LIMIT = 60 * 1024 * 1024
 
 
@@ -79,73 +82,55 @@
     )(panel_index, footprint, set_index, set_weight, scale, green)
 
 
-def turn_body(blocks, width, step_blocks, fp_ref, green_ref, out_ref, done_ref):
-    step = pl.program_id(0)
-    done_ref[...] = jnp.zeros_like(done_ref)
-    for i in range(step_blocks):
-        for j in range(blocks):
-            block = green_ref[i * width : (i + 1) * width, j * width : (j + 1) * width]
-            keep = fp_ref[j, step * step_blocks + i] != 0
-            block = jnp.where(keep, block, jnp.zeros_like(block))
-            out_ref[j * width : (j + 1) * width, i * width : (i + 1) * width] = block.T
-
-
-def turn(footprint, green):
-    rows, cols = green.shape
-    blocks, pblocks = footprint.shape
-    width = rows // pblocks
-    steps = 4
-    return pl.pallas_call(
-        functools.partial(turn_body, blocks, width, pblocks // steps),
-        grid=(steps,),
-        in_specs=[smem(), pl.BlockSpec((rows // steps, cols), lambda i: (i, 0))],
-        out_specs=[pl.BlockSpec((cols, rows // steps), lambda i: (0, i)), pl.BlockSpec((8, width), lambda i: (0, 0))],
-        out_shape=[jax.ShapeDtypeStruct((cols, rows), jnp.bfloat16), jax.ShapeDtypeStruct((8, width), jnp.bfloat16)],
-        compiler_params=pltpu.CompilerParams(vmem_limit_bytes=VMEM_LIMIT),
-        name="mask_and_turn",
-    )(footprint, green)
-
-
-def gram_body(shares, count, meta, turned_ref, *refs):
-    pieces, outs, done_ref, total_ref = refs[:count], refs[count:-2], refs[-2], refs[-1]
+def gram_body(shares, count, width, meta, fp_ref, green_ref, *refs):
+    pieces, outs, done_ref = refs[:count], refs[count:-4], refs[-4]
+    total_ref, masked_ref, left_ref = refs[-3:]
     done_ref[...] = jnp.zeros_like(done_ref)
     core, group = meta[0], meta[1]
-    half = turned_ref.shape[1] // 2
-    share = turned_ref.shape[0] // shares
-
-    def half_of(side):
-        return pl.ds(pl.multiple_of((core if side == 0 else 1 - core) * half, half), half)
-
-    def columns(side):
-        some = pieces[side::2]
-        return jnp.concatenate([p[c : c + half, :] for p in some for c in range(0, p.shape[0], half)], 1)
-
-    @pl.loop(0, shares)
-    def _(s):
+    rows, cols = green_ref.shape
+    half = rows // 2
+    share = cols // shares
+    step = masked_ref.shape[1]
+    for side in range(2):
+        to = pl.ds(pl.multiple_of((core if side == 0 else 1 - core) * half, half), half)
+        some = [p[c : c + half, :] for p in pieces[side::2] for c in range(0, p.shape[0], half)]
+        for n, piece in enumerate(some):
+            left_ref[n * width : (n + 1) * width, to] = piece.T
+
+    @pl.loop(0, cols // step)
+    def _(n):
+        for i in range(rows // width):
+            for j in range(step // width):
+                at = pl.ds(pl.multiple_of(n * step + j * width, width), width)
+                block = green_ref[i * width : (i + 1) * width, at]
+                block = jnp.where(fp_ref[n * (step // width) + j, i] != 0, block, jnp.zeros_like(block))
+                masked_ref[i * width : (i + 1) * width, j * width : (j + 1) * width] = block
+        total = jnp.dot(left_ref[...], masked_ref[...], preferred_element_type=jnp.float32)
+        total_ref[pl.ds(pl.multiple_of(n * step, step), step), :] = total.T
+
+    for s in range(shares):
         at = pl.ds(pl.multiple_of((group ^ s) * share, share), share)
-        total_ref[pl.ds(pl.multiple_of(s * share, share), share), :] = sum(
-            jnp.dot(turned_ref[at, half_of(side)], columns(side), preferred_element_type=jnp.float32)
-            for side in range(2)
-        )
-
-    for s in range(shares):
-        outs[s][...] = total_ref[s * share : (s + 1) * share, :].astype(outs[s].dtype)
-
-
-def gram(shares, meta, turned, pieces):
-    unknowns, pixels = turned.shape
-    cols = sum(p.shape[0] for p in pieces[::2]) // (pixels // 2)
-    share, wide = unknowns // shares, pieces[0].shape[1] * cols
+        outs[s][...] = total_ref[at, :].astype(outs[s].dtype)
+
+
+def gram(shares, meta, footprint, green, pieces):
+    rows, unknowns = green.shape
+    width = rows // footprint.shape[1]
+    share, wide = unknowns // shares, sum(p.shape[0] for p in pieces[::2]) // (rows // 2) * width
     return pl.pallas_call(
-        functools.partial(gram_body, shares, len(pieces)),
-        in_specs=[smem()] + [whole_vmem()] * (1 + len(pieces)),
+        functools.partial(gram_body, shares, len(pieces), width),
+        in_specs=[smem()] * 2 + [whole_vmem()] * (1 + len(pieces)),
         out_specs=[whole_vmem()] * (shares + 1),
         out_shape=[jax.ShapeDtypeStruct((share, wide), jnp.float32 if s == 0 else jnp.bfloat16) for s in range(shares)]
-        + [jax.ShapeDtypeStruct((8, pieces[0].shape[1]), jnp.bfloat16)],
-        scratch_shapes=[pltpu.VMEM((unknowns, wide), jnp.float32)],
+        + [jax.ShapeDtypeStruct((8, width), jnp.bfloat16)],
+        scratch_shapes=[
+            pltpu.VMEM((unknowns, wide), jnp.float32),
+            pltpu.VMEM((rows, 2 * width), jnp.bfloat16),
+            pltpu.VMEM((wide, rows), jnp.bfloat16),
+        ],
         compiler_params=pltpu.CompilerParams(vmem_limit_bytes=VMEM_LIMIT),
         name="partial_gram",
-    )(meta, turned, *pieces)
+    )(meta, footprint, green, *pieces)
 
 
 def sum_body(shares, *refs):
@@ -195,6 +180,23 @@
             rounds.append((depth, now))
             left = later
     return rounds
+
+
+def links(edge):
+    a, b = edge
+    return {(c, c + 1) for c in range(a, b)} | {(c + 1, c) for c in range(b, a)}
+
+
+def pairs(edges, rounds, first):
+    forth = [(2 * a + c, 2 * b + c) for a, b in edges for c in range(2)]
+    taken = set().union(*(links(e) for _, some in rounds for e in some))
+    back = set().union(*(links((b, a)) for a, b in edges))
+    busy = [c for e in edges for c in e]
+    if not FULL or len(set(busy)) < len(busy) or (back & taken and not first):
+        return forth
+    lanes = 2 * (1 + max(c for _, some in rounds for e in some for c in e))
+    rest = [(r, r ^ 1) for r in range(lanes) if r >> 1 not in busy]
+    return forth + [(b, a) for a, b in forth] + rest
 
 
 def after(value, *zeros):
@@ -222,7 +224,7 @@
 
     own, other = prep(chunks[:1], *small)
     start = jnp.where(row == owner, own, lax.ppermute(other, "row", swap))
-    rest = prep(chunks[1:], *small) if last else []
+    rest = prep((sum(chunks[1:], ()),) if MERGE else chunks[1:], *small) if last else []
 
     def exchange(shares):
         return [shares[0]] + [
@@ -236,10 +238,15 @@
 
         def run(meta, met, green, start, *rest):
             sources = [start]
-            for k in range(last):
-                sources.append(jnp.where(row == owner, rest[2 * k], lax.ppermute(rest[2 * k + 1], "row", swap)))
+            if rest and MERGE:
+                own, other = rest[0], lax.ppermute(rest[1], "row", swap)
+                for k in range(last):
+                    at = slice(k * half, (k + 1) * half)
+                    sources.append(jnp.where(row == owner, own[at], other[at]))
+            elif rest:
+                for k in range(last):
+                    sources.append(jnp.where(row == owner, rest[2 * k], lax.ppermute(rest[2 * k + 1], "row", swap)))
             came, held, pieces, parts = {}, list(sources), {}, []
-            turned, ready = turn(met, green)
             for step in range(len(chunks) + deepest):
                 for n, (depth, edges) in enumerate(rounds):
                     k = step - depth
@@ -251,25 +258,27 @@
                         sent = came[parent[edges[0][0]], k]
                         for a, _ in edges[1:]:
                             sent = jnp.where(chip == a, came[parent[a], k], sent)
-                        if k == 0 and depth == 1:
-                            sent = after(sent, ready)
-                    came[n, k] = lax.ppermute(sent, "row", [(2 * a + c, 2 * b + c) for a, b in edges for c in range(2)])
+                    if GATE == "sent" and k == last and depth and parts:
+                        sent = after(sent, *ties)
+                    came[n, k] = lax.ppermute(sent, "row", pairs(edges, rounds, depth == 0 and k == 0))
                     for _, b in edges:
                         held[k] = jnp.where(chip == b, came[n, k], held[k])
                 k = step - deepest
                 if k >= 0:
-                    if k == last and parts:
+                    if GATE == "held" and k == last and parts:
                         held[k] = after(held[k], *ties)
                     pieces[k] = (held[k], lax.ppermute(held[k], "row", swap))
                     for batch in batches:
                         if k == batch[-1]:
-                            shares = gram(groups, meta, turned, [p for b in batch for p in pieces[b]])
+                            shares = gram(groups, meta, met, green, [p for b in batch for p in pieces[b]])
                             fresh = exchange(shares[:groups])
                             parts += fresh
                             if TIE == 0:
                                 ties = []
                             elif TIE == 1:
                                 ties = [shares[groups]]
+                            elif TIE == 3:
+                                ties = [fresh[1][:8, :width] * jnp.bfloat16(0)]
                             else:
                                 ties = [p[:8, :width] * jnp.bfloat16(0) for p in fresh[1:]]
             return total_of(groups, parts, PANEL * width)

time: 64.6 us -> 61.5 us (0.952)
  local copies, waits for them, and re-layouts: 2.82 us -> 0.8 us
  waiting for transfers between devices: 26.7 us -> 24.8 us
  starting transfers between devices: 19.3 us -> 20.4 us
  Pallas kernels: 13.5 us -> 12.6 us
    cond x4 -> x2, local copies, waits for them, and re-layouts: 2.02 us -> 0.01 us
    ppermute x12, waiting for transfers between devices: 20.7 us -> 19 us  [run(): lax.ppermute(sent, 'row', pairs(edges, rounds, depth == 0 and k == 0))]
    ppermute x12, starting transfers between devices: 10.8 us -> 12 us  [run(): lax.ppermute(sent, 'row', pairs(edges, rounds, depth == 0 and k == 0))]
    pallas_call x3 -> x2, Pallas kernels: 8.63 us -> 7.88 us  [gram(): pl.pallas_call(functools.partial(gram_body, shares, len(pieces), width),...]
  transfers between devices with their start and end apart: 26 -> 26, of which waited for: 8 -> 10; matrix products, arithmetic and copies ran while one was open for 1% -> 1% of each run, Pallas kernels for 18% -> 17%
where the time goes in v2:
time: 61.5 us; the launch traced here: 60.5 us
  waiting for transfers between devices  24.8 us (40%)
  starting transfers between devices  20.4 us (33%)
  Pallas kernels  12.6 us (20%)
  local copies, waits for them, and re-layouts  0.8 us (1%)
  between operations  0.76 us (1%)
  loops' own time  0.65 us (1%)
    ppermute x12, waiting for transfers between devices, run(): lax.ppermute(sent, 'row', pairs(edges, rounds, depth == 0 and k == 0))  19 us
    ppermute x12, starting transfers between devices, run(): lax.ppermute(sent, 'row', pairs(edges, rounds, depth == 0 and k == 0))  12 us
    pallas_call x2, Pallas kernels, gram(): pl.pallas_call(functools.partial(gram_body, shares, len(pieces), width),...  7.88 us
    ppermute x6, starting transfers between devices, exchange(): lax.ppermute(shares[s], 'grp', [(g, g ^ s) for g in range(groups)])  7.04 us
    ppermute x6, waiting for transfers between devices, exchange(): lax.ppermute(shares[s], 'grp', [(g, g ^ s) for g in range(groups)])  5.79 us
    pallas_call x2, Pallas kernels, prep(): pl.pallas_call(functools.partial(prep_body, chunks, lane, width), in_spec...  4.6 us
  transfers between devices with their start and end apart: 26, of which 10 were waited for; matrix products, arithmetic and copies ran while one was open for 1% of the time, Pallas kernels for 17%

profile of v2, /device:TPU:8, one launch (start us, length us, event | category | flops | bytes accessed | tf_op | source)
XLA Modules:
  0.0 60.5 jit_solution(14090162025412205351)
XLA Ops:
  0.7 2.0 %weigh_panel.2 = (bf16[1024,128]{1,0:T(8,128)(2,1)S(1)}, bf16[1024,128]{1,0:T(8,128)(2,1)}) custom-call(s32[1]{0:T(128)S(6)} %copy.15.panel, s32[8,16]{1,0:T(8,128)} %bitcast.13, s32[16]{0:T(128)} %set_hbm.3, f32[8]{0:T(128)} %sw_hbm.3, f32[16,128]{1,0:T(8,128)} %bitcast.19, bf16[2048,1024]{1,0:T(8,128)(2,1)} %green_hbm.3), custom_call_target="tpu_custom_call" | custom-call | tf_op jit(solution)/shard_map/weigh_panel/pallas_call | solution.py:67
  2.8 2.6 %weigh_panel.3 = (bf16[1024,128]{1,0:T(8,128)(2,1)S(1)}, bf16[1024,128]{1,0:T(8,128)(2,1)S(1)}, bf16[1024,128]{1,0:T(8,128)(2,1)S(1)}, bf16[1024,128]{1,0:T(8,12...) custom-call(s32[1]{0:T(128)S(6)} %copy.15.panel, s32[8,16]{1,0:T(8,128)S(1)} %bitcast.14, ...), custom_call_target="tpu_custom_call" | custom-call | tf_op jit(solution)/shard_map/weigh_panel/pallas_call | solution.py:67
  5.5 54.2 %conditional.1 = (f32[256,512]{1,0:T(8,128)S(1)}) conditional(s32[]{:T(128)} %clamp.3, (s32[]{:T(128)}, s32[]{:T(128)}, s32[]{:T(128)}, s32[]{:T(128)}, bf16[1024,128]{1,0:T(8,128)(2,1)S(1)}, /*index=5*/bf16[1024,128]{1,0:T(8,128)(2,1)S(1)}, s32[2]{0:T(128)S(1)}, s32[8,16]{1,0:T(8,128)S(1)}, ...), branch_computations={%region_0.1_spmd, %region_1.2_spmd, %region_2.3_spmd, %region_3.4_... | conditional | flops 2228230 | bytes 48236368 | solution.py:288
  5.7 0.5 collective-permute-start.79
  6.2 2.7 %collective-permute-start.75 = (bf16[1024,128]{1,0:T(8,128)(2,1)S(1)}, bf16[1024,128]{1,0:T(8,128)(2,1)S(1)}, u32[]{:S(2)}, u32[]{:S(2)}) collective-permute-start(bf16[1024,128]{1,0:T(8,128)(2,1)S(1)} %broadcast_select_fusion.12), channel_id=1, source_target_pairs={{6,2},{7,3},{2,6},{3,7},{0,1},{1,0},{4,5},{5,4},{14,10},{15,11},{1... | collective-permute-start | bytes 786440 | tf_op jit(solution)/shard_map/cond/branch_3_fun/ppermute | solution.py:263
  8.9 1.3 %collective-permute-start.80 = (bf16[1024,128]{1,0:T(8,128)(2,1)S(1)}, bf16[1024,128]{1,0:T(8,128)(2,1)S(1)}, u32[]{:S(2)}, u32[]{:S(2)}) collective-permute-start(bf16[1024,128]{1,0:T(8,128)(2,1)S(1)} %broadcast_select_fusion.15), channel_id=1, source_target_pairs={{6,2},{7,3},{14,10},{15,11},{22,18},{23,19},{30,26},{31,27}} | collective-permute-start | bytes 786440 | tf_op jit(solution)/shard_map/cond/branch_3_fun/ppermute | solution.py:263
  10.2 0.6 collective-permute-start.92
  10.8 5.2 %collective-permute-done.75 = bf16[1024,128]{1,0:T(8,128)(2,1)S(1)} collective-permute-done((bf16[1024,128]{1,0:T(8,128)(2,1)S(1)}, bf16[1024,128]{1,0:T(8,128)(2,1)S(1)}, u32[]{:S(2)}, u32[]{:S(2)}) %collective-permute-start.75) | collective-permute-done | bytes 262176 | tf_op jit(solution)/shard_map/cond/branch_3_fun/ppermute | solution.py:263
  16.0 1.3 %collective-permute-start.77 = (bf16[1024,128]{1,0:T(8,128)(2,1)S(1)}, bf16[1024,128]{1,0:T(8,128)(2,1)S(1)}, u32[]{:S(2)}, u32[]{:S(2)}) collective-permute-start(bf16[1024,128]{1,0:T(8,128)(2,1)S(1)} %collective-permute-done.75), channel_id=1, source_target_pairs={{2,4},{3,5},{10,12},{11,13},{18,20},{19,21},{26,28},{27,29}} | collective-permute-start | bytes 786440 | tf_op jit(solution)/shard_map/cond/branch_3_fun/ppermute | solution.py:263
  17.4 1.3 %collective-permute-start.88 = (bf16[1024,128]{1,0:T(8,128)(2,1)S(1)}, bf16[1024,128]{1,0:T(8,128)(2,1)S(1)}, u32[]{:S(2)}, u32[]{:S(2)}) collective-permute-start(bf16[1024,128]{1,0:T(8,128)(2,1)S(1)} %broadcast_select_fusion.14), channel_id=1, source_target_pairs={{6,2},{7,3},{14,10},{15,11},{22,18},{23,19},{30,26},{31,27}} | collective-permute-start | bytes 786440 | tf_op jit(solution)/shard_map/cond/branch_3_fun/ppermute | solution.py:263
  18.8 2.3 %collective-permute-done.80 = bf16[1024,128]{1,0:T(8,128)(2,1)S(1)} collective-permute-done((bf16[1024,128]{1,0:T(8,128)(2,1)S(1)}, bf16[1024,128]{1,0:T(8,128)(2,1)S(1)}, u32[]{:S(2)}, u32[]{:S(2)}) %collective-permute-start.80) | collective-permute-done | bytes 262176 | tf_op jit(solution)/shard_map/cond/branch_3_fun/ppermute | solution.py:263
  21.1 1.3 %collective-permute-start.82 = (bf16[1024,128]{1,0:T(8,128)(2,1)S(1)}, bf16[1024,128]{1,0:T(8,128)(2,1)S(1)}, u32[]{:S(2)}, u32[]{:S(2)}) collective-permute-start(bf16[1024,128]{1,0:T(8,128)(2,1)S(1)} %collective-permute-done.80), channel_id=1, source_target_pairs={{2,4},{3,5},{10,12},{11,13},{18,20},{19,21},{26,28},{27,29}} | collective-permute-start | bytes 786440 | tf_op jit(solution)/shard_map/cond/branch_3_fun/ppermute | solution.py:263
  22.5 1.3 %collective-permute-start.93 = (bf16[1024,128]{1,0:T(8,128)(2,1)S(1)}, bf16[1024,128]{1,0:T(8,128)(2,1)S(1)}, u32[]{:S(2)}, u32[]{:S(2)}) collective-permute-start(bf16[1024,128]{1,0:T(8,128)(2,1)S(1)} %broadcast_select_fusion.13), channel_id=1, source_target_pairs={{6,2},{7,3},{14,10},{15,11},{22,18},{23,19},{30,26},{31,27}} | collective-permute-start | bytes 786440 | tf_op jit(solution)/shard_map/cond/branch_3_fun/ppermute | solution.py:263
  23.8 3.2 %collective-permute-done.88 = bf16[1024,128]{1,0:T(8,128)(2,1)S(1)} collective-permute-done((bf16[1024,128]{1,0:T(8,128)(2,1)S(1)}, bf16[1024,128]{1,0:T(8,128)(2,1)S(1)}, u32[]{:S(2)}, u32[]{:S(2)}) %collective-permute-start.88) | collective-permute-done | bytes 262176 | tf_op jit(solution)/shard_map/cond/branch_3_fun/ppermute | solution.py:263
  27.0 1.3 %collective-permute-start.90 = (bf16[1024,128]{1,0:T(8,128)(2,1)S(1)}, bf16[1024,128]{1,0:T(8,128)(2,1)S(1)}, u32[]{:S(2)}, u32[]{:S(2)}) collective-permute-start(bf16[1024,128]{1,0:T(8,128)(2,1)S(1)} %collective-permute-done.88), channel_id=1, source_target_pairs={{2,4},{3,5},{10,12},{11,13},{18,20},{19,21},{26,28},{27,29}} | collective-permute-start | bytes 786440 | tf_op jit(solution)/shard_map/cond/branch_3_fun/ppermute | solution.py:263
  28.4 0.6 collective-permute-done.82
  29.1 3.0 %collective-permute-done.81 = bf16[1024,128]{1,0:T(8,128)(2,1)S(1)} collective-permute-done((bf16[1024,128]{1,0:T(8,128)(2,1)S(1)}, bf16[1024,128]{1,0:T(8,128)(2,1)S(1)}, u32[]{:S(2)}, u32[]{:S(2)}) %collective-permute-start.81) | collective-permute-done | bytes 262176 | tf_op jit(solution)/shard_map/cond/branch_3_fun/ppermute | solution.py:263
  32.3 0.8 %collective-permute-done.93 = bf16[1024,128]{1,0:T(8,128)(2,1)S(1)} collective-permute-done((bf16[1024,128]{1,0:T(8,128)(2,1)S(1)}, bf16[1024,128]{1,0:T(8,128)(2,1)S(1)}, u32[]{:S(2)}, u32[]{:S(2)}) %collective-permute-start.93) | collective-permute-done | bytes 262176 | tf_op jit(solution)/shard_map/cond/branch_3_fun/ppermute | solution.py:263
  33.1 1.3 %collective-permute-start.95 = (bf16[1024,128]{1,0:T(8,128)(2,1)S(1)}, bf16[1024,128]{1,0:T(8,128)(2,1)S(1)}, u32[]{:S(2)}, u32[]{:S(2)}) collective-permute-start(bf16[1024,128]{1,0:T(8,128)(2,1)S(1)} %collective-permute-done.93), channel_id=1, source_target_pairs={{2,4},{3,5},{10,12},{11,13},{18,20},{19,21},{26,28},{27,29}} | collective-permute-start | bytes 786440 | tf_op jit(solution)/shard_map/cond/branch_3_fun/ppermute | solution.py:263
  34.5 2.4 %collective-permute-done.89 = bf16[1024,128]{1,0:T(8,128)(2,1)S(1)} collective-permute-done((bf16[1024,128]{1,0:T(8,128)(2,1)S(1)}, bf16[1024,128]{1,0:T(8,128)(2,1)S(1)}, u32[]{:S(2)}, u32[]{:S(2)}) %collective-permute-start.89) | collective-permute-done | bytes 262176 | tf_op jit(solution)/shard_map/cond/branch_3_fun/ppermute | solution.py:263
  37.0 3.9 %partial_gram.14 = (f32[256,256]{1,0:T(8,128)S(1)}, bf16[256,256]{1,0:T(8,128)(2,1)S(1)}, bf16[256,256]{1,0:T(8,128)(2,1)S(1)}, bf16[256,256]{1,0:T(8,128)(2,1)S(1)}, bf16[8,128]{1,0:T(8,128)(2,1)S(1)}) custom-call(s32[2]{0:T(128)S(1)} %get-tuple-element.180.meta, s32[8,16]{1,0:T(8,128)S(1)} %get-tuple-element.181.fp_ref, bf16[2048,1024]{1,0:T(8,128)(2,1)S(1)} %copy-done.3, ...), custom_call_target="tpu_custom_call" | custom-call | tf_op jit(solution)/shard_map/cond/branch_3_fun/partial_gram/pallas_call | solution.py:120
  40.9 1.5 %collective-permute-done.94 = bf16[1024,128]{1,0:T(8,128)(2,1)S(1)} collective-permute-done((bf16[1024,128]{1,0:T(8,128)(2,1)S(1)}, bf16[1024,128]{1,0:T(8,128)(2,1)S(1)}, u32[]{:S(2)}, u32[]{:S(2)}) %collective-permute-start.94) | collective-permute-done | bytes 262176 | tf_op jit(solution)/shard_map/cond/branch_3_fun/ppermute | solution.py:263
  42.6 1.6 %collective-permute-start.84 = (bf16[256,256]{1,0:T(8,128)(2,1)S(1)}, bf16[256,256]{1,0:T(8,128)(2,1)S(1)}, u32[]{:S(2)}, u32[]{:S(2)}) collective-permute-start(bf16[256,256]{1,0:T(8,128)(2,1)S(1)} %get-tuple-element.190), channel_id=1, source_target_pairs={{0,8},{8,0},{16,24},{24,16},{1,9},{9,1},{17,25},{25,17},{2,10},{10... | collective-permute-start | bytes 393224 | tf_op jit(solution)/shard_map/cond/branch_3_fun/ppermute | solution.py:231
  44.1 1.5 %collective-permute-start.85 = (bf16[256,256]{1,0:T(8,128)(2,1)S(1)}, bf16[256,256]{1,0:T(8,128)(2,1)S(1)}, u32[]{:S(2)}, u32[]{:S(2)}) collective-permute-start(bf16[256,256]{1,0:T(8,128)(2,1)S(1)} %get-tuple-element.191), channel_id=1, source_target_pairs={{0,16},{8,24},{16,0},{24,8},{1,17},{9,25},{17,1},{25,9},{2,18},{10... | collective-permute-start | bytes 393224 | tf_op jit(solution)/shard_map/cond/branch_3_fun/ppermute | solution.py:231
  45.6 0.5 collective-permute-start.86
  46.1 4.0 %partial_gram.15 = (f32[256,256]{1,0:T(8,128)S(1)}, bf16[256,256]{1,0:T(8,128)(2,1)S(1)}, bf16[256,256]{1,0:T(8,128)(2,1)S(1)}, bf16[256,256]{1,0:T(8,128)(2,1)S(1)}, bf16[8,128]{1,0:T(8,128)(2,1)}) custom-call(s32[2]{0:T(128)S(1)} %get-tuple-element.180.meta, s32[8,16]{1,0:T(8,128)S(1)} %get-tuple-element.181.fp_ref, bf16[2048,1024]{1,0:T(8,128)(2,1)S(1)} %copy-done.3, ...), custom_call_target="tpu_custom_call" | custom-call | tf_op jit(solution)/shard_map/cond/branch_3_fun/partial_gram/pallas_call | solution.py:120
  50.1 1.5 %collective-permute-start.97 = (bf16[256,256]{1,0:T(8,128)(2,1)S(1)}, bf16[256,256]{1,0:T(8,128)(2,1)S(1)}, u32[]{:S(2)}, u32[]{:S(2)}) collective-permute-start(bf16[256,256]{1,0:T(8,128)(2,1)S(1)} %get-tuple-element.199), channel_id=1, source_target_pairs={{0,8},{8,0},{16,24},{24,16},{1,9},{9,1},{17,25},{25,17},{2,10},{10... | collective-permute-start | bytes 393224 | tf_op jit(solution)/shard_map/cond/branch_3_fun/ppermute | solution.py:231
  51.6 1.5 %collective-permute-start.98 = (bf16[256,256]{1,0:T(8,128)(2,1)S(1)}, bf16[256,256]{1,0:T(8,128)(2,1)S(1)}, u32[]{:S(2)}, u32[]{:S(2)}) collective-permute-start(bf16[256,256]{1,0:T(8,128)(2,1)S(1)} %get-tuple-element.200), channel_id=1, source_target_pairs={{0,16},{8,24},{16,0},{24,8},{1,17},{9,25},{17,1},{25,9},{2,18},{10... | collective-permute-start | bytes 393224 | tf_op jit(solution)/shard_map/cond/branch_3_fun/ppermute | solution.py:231
  53.1 0.5 collective-permute-start.99
  53.6 1.9 %collective-permute-done.97.refs_5_ = bf16[256,256]{1,0:T(8,128)(2,1)S(1)} collective-permute-done((bf16[256,256]{1,0:T(8,128)(2,1)S(1)}, bf16[256,256]{1,0:T(8,128)(2,1)S(1)}, u32[]{:S(2)}, u32[]{:S(2)}) %collective-permute-start.97) | collective-permute-done | bytes 131104 | tf_op jit(solution)/shard_map/cond/branch_3_fun/ppermute | solution.py:231
  55.5 3.9 %collective-permute-done.98.refs_6_ = bf16[256,256]{1,0:T(8,128)(2,1)S(1)} collective-permute-done((bf16[256,256]{1,0:T(8,128)(2,1)S(1)}, bf16[256,256]{1,0:T(8,128)(2,1)S(1)}, u32[]{:S(2)}, u32[]{:S(2)}) %collective-permute-start.98) | collective-permute-done | bytes 131104 | tf_op jit(solution)/shard_map/cond/branch_3_fun/ppermute | solution.py:231
  59.8 0.8 %copy-done.4 = f32[256,512]{1,0:T(8,128)} copy-done((f32[256,512]{1,0:T(8,128)}, f32[256,512]{1,0:T(8,128)S(1)}, u32[]{:S(2)}) %copy-start.4) | copy-done | bytes 524312
  (42 shorter events, 1.2 us)
Async XLA Ops:
  0.0 2.8 %copy-start.5 = (s32[16,8]{0,1:T(8,128)S(1)}, s32[16,8]{0,1:T(8,128)}, u32[]{:S(2)}) copy-start(s32[16,8]{0,1:T(8,128)} %param.11) | copy-start | bytes 1540
  2.7 2.8 %collective-permute-start.100 = (bf16[1024,128]{1,0:T(8,128)(2,1)}, bf16[1024,128]{1,0:T(8,128)(2,1)S(1)}, u32[]{:S(2)}, u32[]{:S(2)}) collective-permute-start(bf16[1024,128]{1,0:T(8,128)(2,1)} %get-tuple-element.211), channel_id=1, source_target_pairs={{0,1},{1,0},{2,3},{3,2},{4,5},{5,4},{6,7},{7,6},{8,9},{9,8},{10,11... | collective-permute-start | bytes 786440 | tf_op jit(solution)/shard_map/ppermute | solution.py:226
  5.7 3.2 %collective-permute-start.79 = (bf16[1024,128]{1,0:T(8,128)(2,1)S(1)}, bf16[1024,128]{1,0:T(8,128)(2,1)S(1)}, u32[]{:S(2)}, u32[]{:S(2)}) collective-permute-start(bf16[1024,128]{1,0:T(8,128)(2,1)S(1)} %get-tuple-element.188), channel_id=1, source_target_pairs={{0,1},{1,0},{2,3},{3,2},{4,5},{5,4},{6,7},{7,6},{8,9},{9,8},{10,11... | collective-permute-start | bytes 786440 | tf_op jit(solution)/shard_map/cond/branch_3_fun/ppermute | solution.py:248
  6.2 9.8 %collective-permute-start.75 = (bf16[1024,128]{1,0:T(8,128)(2,1)S(1)}, bf16[1024,128]{1,0:T(8,128)(2,1)S(1)}, u32[]{:S(2)}, u32[]{:S(2)}) collective-permute-start(bf16[1024,128]{1,0:T(8,128)(2,1)S(1)} %broadcast_select_fusion.12), channel_id=1, source_target_pairs={{6,2},{7,3},{2,6},{3,7},{0,1},{1,0},{4,5},{5,4},{14,10},{15,11},{1... | collective-permute-start | bytes 786440 | tf_op jit(solution)/shard_map/cond/branch_3_fun/ppermute | solution.py:263
  8.9 8.4 %collective-permute-start.87 = (bf16[1024,128]{1,0:T(8,128)(2,1)S(1)}, bf16[1024,128]{1,0:T(8,128)(2,1)S(1)}, u32[]{:S(2)}, u32[]{:S(2)}) collective-permute-start(bf16[1024,128]{1,0:T(8,128)(2,1)S(1)} %get-tuple-element.194), channel_id=1, source_target_pairs={{0,1},{1,0},{2,3},{3,2},{4,5},{5,4},{6,7},{7,6},{8,9},{9,8},{10,11... | collective-permute-start | bytes 786440 | tf_op jit(solution)/shard_map/cond/branch_3_fun/ppermute | solution.py:248
  8.9 12.1 %collective-permute-start.80 = (bf16[1024,128]{1,0:T(8,128)(2,1)S(1)}, bf16[1024,128]{1,0:T(8,128)(2,1)S(1)}, u32[]{:S(2)}, u32[]{:S(2)}) collective-permute-start(bf16[1024,128]{1,0:T(8,128)(2,1)S(1)} %broadcast_select_fusion.15), channel_id=1, source_target_pairs={{6,2},{7,3},{14,10},{15,11},{22,18},{23,19},{30,26},{31,27}} | collective-permute-start | bytes 786440 | tf_op jit(solution)/shard_map/cond/branch_3_fun/ppermute | solution.py:263
  10.2 12.1 %collective-permute-start.92 = (bf16[1024,128]{1,0:T(8,128)(2,1)}, bf16[1024,128]{1,0:T(8,128)(2,1)S(1)}, u32[]{:S(2)}, u32[]{:S(2)}) collective-permute-start(bf16[1024,128]{1,0:T(8,128)(2,1)} %get-tuple-element.196), channel_id=1, source_target_pairs={{0,1},{1,0},{2,3},{3,2},{4,5},{5,4},{6,7},{7,6},{8,9},{9,8},{10,11... | collective-permute-start | bytes 786440 | tf_op jit(solution)/shard_map/cond/branch_3_fun/ppermute | solution.py:248
  16.0 6.5 %collective-permute-start.77 = (bf16[1024,128]{1,0:T(8,128)(2,1)S(1)}, bf16[1024,128]{1,0:T(8,128)(2,1)S(1)}, u32[]{:S(2)}, u32[]{:S(2)}) collective-permute-start(bf16[1024,128]{1,0:T(8,128)(2,1)S(1)} %collective-permute-done.75), channel_id=1, source_target_pairs={{2,4},{3,5},{10,12},{11,13},{18,20},{19,21},{26,28},{27,29}} | collective-permute-start | bytes 786440 | tf_op jit(solution)/shard_map/cond/branch_3_fun/ppermute | solution.py:263
  17.4 9.6 %collective-permute-start.88 = (bf16[1024,128]{1,0:T(8,128)(2,1)S(1)}, bf16[1024,128]{1,0:T(8,128)(2,1)S(1)}, u32[]{:S(2)}, u32[]{:S(2)}) collective-permute-start(bf16[1024,128]{1,0:T(8,128)(2,1)S(1)} %broadcast_select_fusion.14), channel_id=1, source_target_pairs={{6,2},{7,3},{14,10},{15,11},{22,18},{23,19},{30,26},{31,27}} | collective-permute-start | bytes 786440 | tf_op jit(solution)/shard_map/cond/branch_3_fun/ppermute | solution.py:263
  18.7 9.6 %collective-permute-start.76 = (bf16[1024,128]{1,0:T(8,128)(2,1)S(1)}, bf16[1024,128]{1,0:T(8,128)(2,1)S(1)}, u32[]{:S(2)}, u32[]{:S(2)}) collective-permute-start(bf16[1024,128]{1,0:T(8,128)(2,1)S(1)} %collective-permute-done.75), channel_id=1, source_target_pairs={{2,0},{3,1},{0,2},{1,3},{4,5},{5,4},{6,7},{7,6},{10,8},{11,9},{8,1... | collective-permute-start | bytes 786440 | tf_op jit(solution)/shard_map/cond/branch_3_fun/ppermute | solution.py:263
  18.7 18.3 %copy-start.3 = (bf16[2048,1024]{1,0:T(8,128)(2,1)S(1)}, bf16[2048,1024]{1,0:T(8,128)(2,1)}, u32[]{:S(2)}) copy-start(bf16[2048,1024]{1,0:T(8,128)(2,1)} %get-tuple-element.182.green_ref) | copy-start | bytes 12582916 | tf_op jit(solution)/shard_map/cond
  21.1 8.0 %collective-permute-start.82 = (bf16[1024,128]{1,0:T(8,128)(2,1)S(1)}, bf16[1024,128]{1,0:T(8,128)(2,1)S(1)}, u32[]{:S(2)}, u32[]{:S(2)}) collective-permute-start(bf16[1024,128]{1,0:T(8,128)(2,1)S(1)} %collective-permute-done.80), channel_id=1, source_target_pairs={{2,4},{3,5},{10,12},{11,13},{18,20},{19,21},{26,28},{27,29}} | collective-permute-start | bytes 786440 | tf_op jit(solution)/shard_map/cond/branch_3_fun/ppermute | solution.py:263
  22.4 9.7 %collective-permute-start.81 = (bf16[1024,128]{1,0:T(8,128)(2,1)S(1)}, bf16[1024,128]{1,0:T(8,128)(2,1)S(1)}, u32[]{:S(2)}, u32[]{:S(2)}) collective-permute-start(bf16[1024,128]{1,0:T(8,128)(2,1)S(1)} %collective-permute-done.80), channel_id=1, source_target_pairs={{2,0},{3,1},{0,2},{1,3},{4,5},{5,4},{6,7},{7,6},{10,8},{11,9},{8,1... | collective-permute-start | bytes 786440 | tf_op jit(solution)/shard_map/cond/branch_3_fun/ppermute | solution.py:263
  22.5 10.6 %collective-permute-start.93 = (bf16[1024,128]{1,0:T(8,128)(2,1)S(1)}, bf16[1024,128]{1,0:T(8,128)(2,1)S(1)}, u32[]{:S(2)}, u32[]{:S(2)}) collective-permute-start(bf16[1024,128]{1,0:T(8,128)(2,1)S(1)} %broadcast_select_fusion.13), channel_id=1, source_target_pairs={{6,2},{7,3},{14,10},{15,11},{22,18},{23,19},{30,26},{31,27}} | collective-permute-start | bytes 786440 | tf_op jit(solution)/shard_map/cond/branch_3_fun/ppermute | solution.py:263
  27.0 7.4 %collective-permute-start.90 = (bf16[1024,128]{1,0:T(8,128)(2,1)S(1)}, bf16[1024,128]{1,0:T(8,128)(2,1)S(1)}, u32[]{:S(2)}, u32[]{:S(2)}) collective-permute-start(bf16[1024,128]{1,0:T(8,128)(2,1)S(1)} %collective-permute-done.88), channel_id=1, source_target_pairs={{2,4},{3,5},{10,12},{11,13},{18,20},{19,21},{26,28},{27,29}} | collective-permute-start | bytes 786440 | tf_op jit(solution)/shard_map/cond/branch_3_fun/ppermute | solution.py:263
  28.3 8.5 %collective-permute-start.89 = (bf16[1024,128]{1,0:T(8,128)(2,1)S(1)}, bf16[1024,128]{1,0:T(8,128)(2,1)S(1)}, u32[]{:S(2)}, u32[]{:S(2)}) collective-permute-start(bf16[1024,128]{1,0:T(8,128)(2,1)S(1)} %collective-permute-done.88), channel_id=1, source_target_pairs={{2,0},{3,1},{0,2},{1,3},{4,5},{5,4},{6,7},{7,6},{10,8},{11,9},{8,1... | collective-permute-start | bytes 786440 | tf_op jit(solution)/shard_map/cond/branch_3_fun/ppermute | solution.py:263
  29.0 7.9 %collective-permute-start.78 = (bf16[1024,128]{1,0:T(8,128)(2,1)S(1)}, bf16[1024,128]{1,0:T(8,128)(2,1)S(1)}, u32[]{:S(2)}, u32[]{:S(2)}) collective-permute-start(bf16[1024,128]{1,0:T(8,128)(2,1)S(1)} %select_select_fusion.11.refs_0_), channel_id=1, source_target_pairs={{0,1},{1,0},{2,3},{3,2},{4,5},{5,4},{6,7},{7,6},{8,9},{9,8},{10,11... | collective-permute-start | bytes 786440 | tf_op jit(solution)/shard_map/cond/branch_3_fun/ppermute | solution.py:270
  32.2 4.8 %collective-permute-start.83 = (bf16[1024,128]{1,0:T(8,128)(2,1)S(1)}, bf16[1024,128]{1,0:T(8,128)(2,1)S(1)}, u32[]{:S(2)}, u32[]{:S(2)}) collective-permute-start(bf16[1024,128]{1,0:T(8,128)(2,1)S(1)} %select_select_fusion.10.refs_2_), channel_id=1, source_target_pairs={{0,1},{1,0},{2,3},{3,2},{4,5},{5,4},{6,7},{7,6},{8,9},{9,8},{10,11... | collective-permute-start | bytes 786440 | tf_op jit(solution)/shard_map/cond/branch_3_fun/ppermute | solution.py:270
  33.1 7.8 %collective-permute-start.95 = (bf16[1024,128]{1,0:T(8,128)(2,1)S(1)}, bf16[1024,128]{1,0:T(8,128)(2,1)S(1)}, u32[]{:S(2)}, u32[]{:S(2)}) collective-permute-start(bf16[1024,128]{1,0:T(8,128)(2,1)S(1)} %collective-permute-done.93), channel_id=1, source_target_pairs={{2,4},{3,5},{10,12},{11,13},{18,20},{19,21},{26,28},{27,29}} | collective-permute-start | bytes 786440 | tf_op jit(solution)/shard_map/cond/branch_3_fun/ppermute | solution.py:263
  34.4 8.0 %collective-permute-start.94 = (bf16[1024,128]{1,0:T(8,128)(2,1)S(1)}, bf16[1024,128]{1,0:T(8,128)(2,1)S(1)}, u32[]{:S(2)}, u32[]{:S(2)}) collective-permute-start(bf16[1024,128]{1,0:T(8,128)(2,1)S(1)} %collective-permute-done.93), channel_id=1, source_target_pairs={{2,0},{3,1},{0,2},{1,3},{4,5},{5,4},{6,7},{7,6},{10,8},{11,9},{8,1... | collective-permute-start | bytes 786440 | tf_op jit(solution)/shard_map/cond/branch_3_fun/ppermute | solution.py:263
  36.9 9.2 %collective-permute-start.91 = (bf16[1024,128]{1,0:T(8,128)(2,1)S(1)}, bf16[1024,128]{1,0:T(8,128)(2,1)S(1)}, u32[]{:S(2)}, u32[]{:S(2)}) collective-permute-start(bf16[1024,128]{1,0:T(8,128)(2,1)S(1)} %select_select_fusion.9.refs_0_), channel_id=1, source_target_pairs={{0,1},{1,0},{2,3},{3,2},{4,5},{5,4},{6,7},{7,6},{8,9},{9,8},{10,11... | collective-permute-start | bytes 786440 | tf_op jit(solution)/shard_map/cond/branch_3_fun/ppermute | solution.py:270
  42.5 3.6 %collective-permute-start.96 = (bf16[1024,128]{1,0:T(8,128)(2,1)S(1)}, bf16[1024,128]{1,0:T(8,128)(2,1)S(1)}, u32[]{:S(2)}, u32[]{:S(2)}) collective-permute-start(bf16[1024,128]{1,0:T(8,128)(2,1)S(1)} %select_add_fusion.3.refs_2_), channel_id=1, source_target_pairs={{0,1},{1,0},{2,3},{3,2},{4,5},{5,4},{6,7},{7,6},{8,9},{9,8},{10,11... | collective-permute-start | bytes 786440 | tf_op jit(solution)/shard_map/cond/branch_3_fun/ppermute | solution.py:270
  42.6 10.6 %collective-permute-start.84 = (bf16[256,256]{1,0:T(8,128)(2,1)S(1)}, bf16[256,256]{1,0:T(8,128)(2,1)S(1)}, u32[]{:S(2)}, u32[]{:S(2)}) collective-permute-start(bf16[256,256]{1,0:T(8,128)(2,1)S(1)} %get-tuple-element.190), channel_id=1, source_target_pairs={{0,8},{8,0},{16,24},{24,16},{1,9},{9,1},{17,25},{25,17},{2,10},{10... | collective-permute-start | bytes 393224 | tf_op jit(solution)/shard_map/cond/branch_3_fun/ppermute | solution.py:231
  44.1 9.5 %collective-permute-start.85 = (bf16[256,256]{1,0:T(8,128)(2,1)S(1)}, bf16[256,256]{1,0:T(8,128)(2,1)S(1)}, u32[]{:S(2)}, u32[]{:S(2)}) collective-permute-start(bf16[256,256]{1,0:T(8,128)(2,1)S(1)} %get-tuple-element.191), channel_id=1, source_target_pairs={{0,16},{8,24},{16,0},{24,8},{1,17},{9,25},{17,1},{25,9},{2,18},{10... | collective-permute-start | bytes 393224 | tf_op jit(solution)/shard_map/cond/branch_3_fun/ppermute | solution.py:231
  45.6 8.0 %collective-permute-start.86 = (bf16[256,256]{1,0:T(8,128)(2,1)S(1)}, bf16[256,256]{1,0:T(8,128)(2,1)S(1)}, u32[]{:S(2)}, u32[]{:S(2)}) collective-permute-start(bf16[256,256]{1,0:T(8,128)(2,1)S(1)} %get-tuple-element.192), channel_id=1, source_target_pairs={{0,24},{8,16},{16,8},{24,0},{1,25},{9,17},{17,9},{25,1},{2,26},{10... | collective-permute-start | bytes 393224 | tf_op jit(solution)/shard_map/cond/branch_3_fun/ppermute | solution.py:231
  50.1 5.4 %collective-permute-start.97 = (bf16[256,256]{1,0:T(8,128)(2,1)S(1)}, bf16[256,256]{1,0:T(8,128)(2,1)S(1)}, u32[]{:S(2)}, u32[]{:S(2)}) collective-permute-start(bf16[256,256]{1,0:T(8,128)(2,1)S(1)} %get-tuple-element.199), channel_id=1, source_target_pairs={{0,8},{8,0},{16,24},{24,16},{1,9},{9,1},{17,25},{25,17},{2,10},{10... | collective-permute-start | bytes 393224 | tf_op jit(solution)/shard_map/cond/branch_3_fun/ppermute | solution.py:231
  51.6 7.8 %collective-permute-start.98 = (bf16[256,256]{1,0:T(8,128)(2,1)S(1)}, bf16[256,256]{1,0:T(8,128)(2,1)S(1)}, u32[]{:S(2)}, u32[]{:S(2)}) collective-permute-start(bf16[256,256]{1,0:T(8,128)(2,1)S(1)} %get-tuple-element.200), channel_id=1, source_target_pairs={{0,16},{8,24},{16,0},{24,8},{1,17},{9,25},{17,1},{25,9},{2,18},{10... | collective-permute-start | bytes 393224 | tf_op jit(solution)/shard_map/cond/branch_3_fun/ppermute | solution.py:231
  53.1 6.3 %collective-permute-start.99 = (bf16[256,256]{1,0:T(8,128)(2,1)S(1)}, bf16[256,256]{1,0:T(8,128)(2,1)S(1)}, u32[]{:S(2)}, u32[]{:S(2)}) collective-permute-start(bf16[256,256]{1,0:T(8,128)(2,1)S(1)} %get-tuple-element.201), channel_id=1, source_target_pairs={{0,24},{8,16},{16,8},{24,0},{1,25},{9,17},{17,9},{25,1},{2,26},{10... | collective-permute-start | bytes 393224 | tf_op jit(solution)/shard_map/cond/branch_3_fun/ppermute | solution.py:231
  59.7 0.8 %copy-start.4 = (f32[256,512]{1,0:T(8,128)}, f32[256,512]{1,0:T(8,128)S(1)}, u32[]{:S(2)}) copy-start(f32[256,512]{1,0:T(8,128)S(1)} %get-tuple-element.360) | copy-start | bytes 1572868

commit v3 on v2

--- a/solution.py
+++ b/solution.py
@@ -9,10 +9,11 @@
 PANEL = 4
 CHUNKS = ((0,), (1,), (2,), (3,))
 BATCHES = ((0, 1), (2, 3))
-TIE = 1
+GATES = ((3, ((1, 0),)),)
 MERGE = False
+STEP = 4
+SWAPPED = True
 FULL = True
-GATE = "held"
 VMEM_LIMIT = 16 * 1024 * 1024
 PREP_LIMIT = 60 * 1024 * 1024
 
@@ -29,7 +30,6 @@
     outs, (fp, sets, sw, scale, green, sems) = refs[: 2 * len(chunks)], refs[2 * len(chunks) :]
     blocks, pblocks = fp_hbm.shape
     half_blocks = pblocks // 2
-    half = half_blocks * width
     low = chunks[0][0]
     first = lax.rem(panel[0] * PANEL, blocks)
     at = pl.ds(pl.multiple_of((first + low) * width, width), green.shape[1])
@@ -48,22 +48,21 @@
         base = (core if side == 0 else 1 - core) * half_blocks
         for i in range(half_blocks):
             weight = scale[pl.ds(base + i, 1), :] * sw[sets[base + i]]
-            weight = jnp.broadcast_to(weight, (width, width)).T
             rows = pl.ds(pl.multiple_of((base + i) * width, width), width)
             for n, cols in enumerate(chunks):
                 for m, col in enumerate(cols):
                     block = green[rows, (col - low) * width : (col - low + 1) * width]
-                    value = (block.astype(jnp.float32) * weight).astype(jnp.bfloat16)
+                    value = (block.T.astype(jnp.float32) * weight).astype(jnp.bfloat16)
                     keep = fp[first + col, base + i] != 0
-                    to = slice(m * half + i * width, m * half + (i + 1) * width)
-                    outs[2 * n + side][to, :] = jnp.where(keep, value, jnp.zeros_like(value))
+                    to = (slice(m * width, (m + 1) * width), slice(i * width, (i + 1) * width))
+                    outs[2 * n + side][to] = jnp.where(keep, value, jnp.zeros_like(value))
 
 
 def prep(chunks, lane, panel_index, footprint, set_index, set_weight, scale, green):
     rows = green.shape[0]
     width = rows // footprint.shape[1]
     count = sum(len(cols) for cols in chunks)
-    shapes = [jax.ShapeDtypeStruct((rows // 2 * len(cols), width), jnp.bfloat16) for cols in chunks for _ in range(2)]
+    shapes = [jax.ShapeDtypeStruct((len(cols) * width, rows // 2), jnp.bfloat16) for cols in chunks for _ in range(2)]
     return pl.pallas_call(
         functools.partial(prep_body, chunks, lane, width),
         in_specs=[smem()] + [pl.BlockSpec(memory_space=pltpu.HBM)] * 5,
@@ -83,19 +82,12 @@
 
 
 def gram_body(shares, count, width, meta, fp_ref, green_ref, *refs):
-    pieces, outs, done_ref = refs[:count], refs[count:-4], refs[-4]
-    total_ref, masked_ref, left_ref = refs[-3:]
+    pieces, outs, done_ref, total_ref, masked_ref = refs[:count], refs[count:-3], refs[-3], refs[-2], refs[-1]
     done_ref[...] = jnp.zeros_like(done_ref)
     core, group = meta[0], meta[1]
     rows, cols = green_ref.shape
     half = rows // 2
-    share = cols // shares
     step = masked_ref.shape[1]
-    for side in range(2):
-        to = pl.ds(pl.multiple_of((core if side == 0 else 1 - core) * half, half), half)
-        some = [p[c : c + half, :] for p in pieces[side::2] for c in range(0, p.shape[0], half)]
-        for n, piece in enumerate(some):
-            left_ref[n * width : (n + 1) * width, to] = piece.T
 
     @pl.loop(0, cols // step)
     def _(n):
@@ -105,32 +97,41 @@
                 block = green_ref[i * width : (i + 1) * width, at]
                 block = jnp.where(fp_ref[n * (step // width) + j, i] != 0, block, jnp.zeros_like(block))
                 masked_ref[i * width : (i + 1) * width, j * width : (j + 1) * width] = block
-        total = jnp.dot(left_ref[...], masked_ref[...], preferred_element_type=jnp.float32)
-        total_ref[pl.ds(pl.multiple_of(n * step, step), step), :] = total.T
-
-    for s in range(shares):
-        at = pl.ds(pl.multiple_of((group ^ s) * share, share), share)
-        outs[s][...] = total_ref[at, :].astype(outs[s].dtype)
+        total = 0.0
+        for side in range(2):
+            at = pl.ds(pl.multiple_of((core if side == 0 else 1 - core) * half, half), half)
+            left = jnp.concatenate([p[...] for p in pieces[side::2]], 0)
+            total += jnp.dot(left, masked_ref[at, :], preferred_element_type=jnp.float32)
+        total_ref[:, pl.ds(pl.multiple_of(n * step, step), step)] = total
+
+    share = cols // shares
+    for s in range(len(outs)):
+        if len(outs) > 1:
+            outs[s][...] = total_ref[:, pl.ds(pl.multiple_of((group ^ s) * share, share), share)].astype(outs[s].dtype)
+        else:
+            outs[s][...] = total_ref[...]
 
 
 def gram(shares, meta, footprint, green, pieces):
     rows, unknowns = green.shape
     width = rows // footprint.shape[1]
-    share, wide = unknowns // shares, sum(p.shape[0] for p in pieces[::2]) // (rows // 2) * width
-    return pl.pallas_call(
+    share, wide = unknowns // shares, sum(p.shape[0] for p in pieces[::2])
+    apart = share % width == 0
+    shapes = [jax.ShapeDtypeStruct((wide, share), jnp.float32 if s == 0 else jnp.bfloat16) for s in range(shares)]
+    out = pl.pallas_call(
         functools.partial(gram_body, shares, len(pieces), width),
         in_specs=[smem()] * 2 + [whole_vmem()] * (1 + len(pieces)),
-        out_specs=[whole_vmem()] * (shares + 1),
-        out_shape=[jax.ShapeDtypeStruct((share, wide), jnp.float32 if s == 0 else jnp.bfloat16) for s in range(shares)]
-        + [jax.ShapeDtypeStruct((8, width), jnp.bfloat16)],
-        scratch_shapes=[
-            pltpu.VMEM((unknowns, wide), jnp.float32),
-            pltpu.VMEM((rows, 2 * width), jnp.bfloat16),
-            pltpu.VMEM((wide, rows), jnp.bfloat16),
-        ],
+        out_specs=[whole_vmem()] * ((shares if apart else 1) + 1),
+        out_shape=(shapes if apart else [jax.ShapeDtypeStruct((wide, unknowns), jnp.float32)])
+        + [jax.ShapeDtypeStruct((8, rows // 2), jnp.bfloat16)],
+        scratch_shapes=[pltpu.VMEM((wide, unknowns), jnp.float32), pltpu.VMEM((rows, STEP * width), jnp.bfloat16)],
         compiler_params=pltpu.CompilerParams(vmem_limit_bytes=VMEM_LIMIT),
         name="partial_gram",
     )(meta, footprint, green, *pieces)
+    if apart:
+        return out
+    cut = [lax.dynamic_slice_in_dim(out[0], (meta[1] ^ s) * share, share, 1).astype(shapes[s].dtype) for s in range(shares)]
+    return [*cut, out[1]]
 
 
 def sum_body(shares, *refs):
@@ -140,16 +141,19 @@
         total = parts[k][...]
         for s in range(1, shares):
             total += parts[k + s][...].astype(jnp.float32)
-        out_ref[:, at : at + total.shape[1]] = total
-        at += total.shape[1]
+        out_ref[:, at : at + total.shape[0]] = total.T
+        at += total.shape[0]
 
 
 def total_of(shares, parts, panel_cols):
+    share = parts[0].shape[1]
+    if share % 128:
+        return jnp.concatenate([sum(p.astype(jnp.float32) for p in parts[k : k + shares]) for k in range(0, len(parts), shares)]).T
     return pl.pallas_call(
         functools.partial(sum_body, shares),
         in_specs=[whole_vmem()] * len(parts),
         out_specs=whole_vmem(),
-        out_shape=jax.ShapeDtypeStruct((parts[0].shape[0], panel_cols), jnp.float32),
+        out_shape=jax.ShapeDtypeStruct((share, panel_cols), jnp.float32),
         compiler_params=pltpu.CompilerParams(vmem_limit_bytes=VMEM_LIMIT),
         name="sum_groups",
     )(*parts)
@@ -233,6 +237,8 @@
 
     def from_chip(source):
         rounds = spread(source, chips)
+        if SWAPPED and len(rounds) == 3 and rounds[1][0] == rounds[2][0]:
+            rounds = [rounds[0], rounds[2], rounds[1]]
         deepest = rounds[-1][0]
         parent = {b: n for n, (_, edges) in enumerate(rounds) for _, b in edges}
 
@@ -241,12 +247,13 @@
             if rest and MERGE:
                 own, other = rest[0], lax.ppermute(rest[1], "row", swap)
                 for k in range(last):
-                    at = slice(k * half, (k + 1) * half)
+                    at = slice(k * width, (k + 1) * width)
                     sources.append(jnp.where(row == owner, own[at], other[at]))
             elif rest:
                 for k in range(last):
                     sources.append(jnp.where(row == owner, rest[2 * k], lax.ppermute(rest[2 * k + 1], "row", swap)))
-            came, held, pieces, parts = {}, list(sources), {}, []
+            came, held, pieces, parts, signs = {}, list(sources), {}, [], {}
+            gates = {k: (lambda some=some: [signs[b][n] for b, n in some]) for k, some in GATES} if last else {}
             for step in range(len(chunks) + deepest):
                 for n, (depth, edges) in enumerate(rounds):
                     k = step - depth
@@ -258,29 +265,20 @@
                         sent = came[parent[edges[0][0]], k]
                         for a, _ in edges[1:]:
                             sent = jnp.where(chip == a, came[parent[a], k], sent)
-                    if GATE == "sent" and k == last and depth and parts:
-                        sent = after(sent, *ties)
                     came[n, k] = lax.ppermute(sent, "row", pairs(edges, rounds, depth == 0 and k == 0))
                     for _, b in edges:
                         held[k] = jnp.where(chip == b, came[n, k], held[k])
                 k = step - deepest
                 if k >= 0:
-                    if GATE == "held" and k == last and parts:
-                        held[k] = after(held[k], *ties)
+                    if k in gates:
+                        held[k] = after(held[k], *gates[k]())
                     pieces[k] = (held[k], lax.ppermute(held[k], "row", swap))
                     for batch in batches:
                         if k == batch[-1]:
                             shares = gram(groups, meta, met, green, [p for b in batch for p in pieces[b]])
                             fresh = exchange(shares[:groups])
                             parts += fresh
-                            if TIE == 0:
-                                ties = []
-                            elif TIE == 1:
-                                ties = [shares[groups]]
-                            elif TIE == 3:
-                                ties = [fresh[1][:8, :width] * jnp.bfloat16(0)]
-                            else:
-                                ties = [p[:8, :width] * jnp.bfloat16(0) for p in fresh[1:]]
+                            signs[k] = (shares[groups], *(p[:1, :1] * jnp.bfloat16(0) for p in fresh[1:]))
             return total_of(groups, parts, PANEL * width)
 
         return run

time: 61.5 us -> 57 us (0.927)
  the two profiles are of different devices: /device:TPU:8 before, /device:TPU:0 now
where the time goes in v3:
time: 57 us; the launch traced here: 56.8 us
  starting transfers between devices  28.6 us (50%)
  waiting for transfers between devices  14.7 us (26%)
  Pallas kernels  11.2 us (20%)
  local copies, waits for them, and re-layouts  0.82 us (1%)
  between operations  0.74 us (1%)
    ppermute x12, starting transfers between devices, run(): lax.ppermute(sent, 'row', pairs(edges, rounds, depth == 0 and k == 0))  19.2 us
    ppermute x12, waiting for transfers between devices, run(): lax.ppermute(sent, 'row', pairs(edges, rounds, depth == 0 and k == 0))  8.47 us
    ppermute x6, starting transfers between devices, exchange(): lax.ppermute(shares[s], 'grp', [(g, g ^ s) for g in range(groups)])  7.11 us
    pallas_call x2, Pallas kernels, gram(): pl.pallas_call(functools.partial(gram_body, shares, len(pieces), width),...  6.4 us
    ppermute x6, waiting for transfers between devices, exchange(): lax.ppermute(shares[s], 'grp', [(g, g ^ s) for g in range(groups)])  5.78 us
    pallas_call x2, Pallas kernels, prep(): pl.pallas_call(functools.partial(prep_body, chunks, lane, width), in_spec...  4.54 us
    ppermute x4, starting transfers between devices, run(): pieces[k] = (held[k], lax.ppermute(held[k], 'row', swap))  1.21 us
  transfers between devices with their start and end apart: 26, of which 6 were waited for; matrix products, arithmetic and copies ran while one was open for 1% of the time, Pallas kernels for 16%

profile of v3, /device:TPU:0, one launch (start us, length us, event | category | flops | bytes accessed | tf_op | source)
XLA Modules:
  0.0 56.8 jit_solution(15556275416002813755)
XLA Ops:
  0.7 2.0 %weigh_panel.2 = (bf16[128,1024]{1,0:T(8,128)(2,1)S(1)}, bf16[128,1024]{1,0:T(8,128)(2,1)}) custom-call(s32[1]{0:T(128)S(6)} %copy.15.panel, s32[8,16]{1,0:T(8,128)} %bitcast.5, s32[16]{0:T(128)} %set_hbm.3, f32[8]{0:T(128)} %sw_hbm.3, f32[16,128]{1,0:T(8,128)} %bitcast.11, bf16[2048,1024]{1,0:T(8,128)(2,1)} %green_hbm.3), custom_call_target="tpu_custom_call" | custom-call | tf_op jit(solution)/shard_map/weigh_panel/pallas_call | solution.py:66
  2.6 0.5 collective-permute-start.100
  3.2 2.6 %weigh_panel.3 = (bf16[128,1024]{1,0:T(8,128)(2,1)S(1)}, bf16[128,1024]{1,0:T(8,128)(2,1)S(1)}, bf16[128,1024]{1,0:T(8,128)(2,1)S(1)}, bf16[128,1024]{1,0:T(8,12...) custom-call(s32[1]{0:T(128)S(6)} %copy.15.panel, s32[8,16]{1,0:T(8,128)S(1)} %bitcast.6, ...), custom_call_target="tpu_custom_call" | custom-call | tf_op jit(solution)/shard_map/weigh_panel/pallas_call | solution.py:66
  5.9 50.1 %conditional.1 = (f32[256,512]{1,0:T(8,128)S(1)}) conditional(s32[]{:T(128)} %clamp.3, (s32[]{:T(128)}, s32[]{:T(128)}, s32[]{:T(128)}, s32[]{:T(128)}, bf16[128,1024]{1,0:T(8,128)(2,1)S(1)}, /*index=5*/bf16[128,1024]{1,0:T(8,128)(2,1)S(1)}, s32[2]{0:T(128)S(1)}, s32[8,16]{1,0:T(8,128)S(1)}, ...), branch_computations={%region_0.1_spmd, %region_1.2_spmd, %region_2.3_spmd, %region_3.4_... | conditional | flops 2228230 | bytes 48241744 | solution.py:286
  6.0 0.5 collective-permute-start.25
  6.6 0.4 collective-permute-start.42
  7.0 0.4 collective-permute-done.29
  7.5 0.2 collective-permute-start.30
  7.7 4.2 %collective-permute-start.27 = (bf16[128,1024]{1,0:T(8,128)(2,1)S(1)}, bf16[128,1024]{1,0:T(8,128)(2,1)S(1)}, u32[]{:S(2)}, u32[]{:S(2)}) collective-permute-start(bf16[128,1024]{1,0:T(8,128)(2,1)S(1)} %broadcast_select_fusion.4), channel_id=1, source_target_pairs={{2,0},{3,1},{0,2},{1,3},{4,5},{5,4},{6,7},{7,6},{10,8},{11,9},{8,1... | collective-permute-start | bytes 786440 | tf_op jit(solution)/shard_map/cond/branch_1_fun/ppermute | solution.py:268
  11.9 0.6 collective-permute-start.38
  12.5 7.5 %collective-permute-start.32 = (bf16[128,1024]{1,0:T(8,128)(2,1)S(1)}, bf16[128,1024]{1,0:T(8,128)(2,1)S(1)}, u32[]{:S(2)}, u32[]{:S(2)}) collective-permute-start(bf16[128,1024]{1,0:T(8,128)(2,1)S(1)} %broadcast_select_fusion.7), channel_id=1, source_target_pairs={{2,0},{3,1},{0,2},{1,3},{4,5},{5,4},{6,7},{7,6},{10,8},{11,9},{8,1... | collective-permute-start | bytes 786440 | tf_op jit(solution)/shard_map/cond/branch_1_fun/ppermute | solution.py:268
  20.0 4.0 %collective-permute-start.40 = (bf16[128,1024]{1,0:T(8,128)(2,1)S(1)}, bf16[128,1024]{1,0:T(8,128)(2,1)S(1)}, u32[]{:S(2)}, u32[]{:S(2)}) collective-permute-start(bf16[128,1024]{1,0:T(8,128)(2,1)S(1)} %broadcast_select_fusion.6), channel_id=1, source_target_pairs={{2,0},{3,1},{0,2},{1,3},{4,5},{5,4},{6,7},{7,6},{10,8},{11,9},{8,1... | collective-permute-start | bytes 786440 | tf_op jit(solution)/shard_map/cond/branch_1_fun/ppermute | solution.py:268
  24.0 0.2 collective-permute-start.43
  24.2 0.3 collective-permute-start.39
  24.5 0.9 %collective-permute-done.32 = bf16[128,1024]{1,0:T(8,128)(2,1)S(1)} collective-permute-done((bf16[128,1024]{1,0:T(8,128)(2,1)S(1)}, bf16[128,1024]{1,0:T(8,128)(2,1)S(1)}, u32[]{:S(2)}, u32[]{:S(2)}) %collective-permute-start.32) | collective-permute-done | bytes 262176 | tf_op jit(solution)/shard_map/cond/branch_1_fun/ppermute | solution.py:268
  25.6 0.6 %collective-permute-start.33 = (bf16[128,1024]{1,0:T(8,128)(2,1)S(1)}, bf16[128,1024]{1,0:T(8,128)(2,1)S(1)}, u32[]{:S(2)}, u32[]{:S(2)}) collective-permute-start(bf16[128,1024]{1,0:T(8,128)(2,1)S(1)} %select_select_fusion.4.refs_2_), channel_id=1, source_target_pairs={{0,1},{1,0},{2,3},{3,2},{4,5},{5,4},{6,7},{7,6},{8,9},{9,8},{10,11... | collective-permute-start | bytes 786440 | tf_op jit(solution)/shard_map/cond/branch_1_fun/ppermute | solution.py:275
  26.1 4.9 %collective-permute-done.40 = bf16[128,1024]{1,0:T(8,128)(2,1)S(1)} collective-permute-done((bf16[128,1024]{1,0:T(8,128)(2,1)S(1)}, bf16[128,1024]{1,0:T(8,128)(2,1)S(1)}, u32[]{:S(2)}, u32[]{:S(2)}) %collective-permute-start.40) | collective-permute-done | bytes 262176 | tf_op jit(solution)/shard_map/cond/branch_1_fun/ppermute | solution.py:268
  31.1 1.7 %collective-permute-start.45 = (bf16[128,1024]{1,0:T(8,128)(2,1)S(1)}, bf16[128,1024]{1,0:T(8,128)(2,1)S(1)}, u32[]{:S(2)}, u32[]{:S(2)}) collective-permute-start(bf16[128,1024]{1,0:T(8,128)(2,1)S(1)} %broadcast_select_fusion.5), channel_id=1, source_target_pairs={{2,0},{3,1},{0,2},{1,3},{4,5},{5,4},{6,7},{7,6},{10,8},{11,9},{8,1... | collective-permute-start | bytes 786440 | tf_op jit(solution)/shard_map/cond/branch_1_fun/ppermute | solution.py:268
  32.9 0.6 collective-permute-start.41
  33.5 3.2 %partial_gram.10 = (f32[256,256]{1,0:T(8,128)S(1)}, bf16[256,256]{1,0:T(8,128)(2,1)S(1)}, bf16[256,256]{1,0:T(8,128)(2,1)S(1)}, bf16[256,256]{1,0:T(8,128)(2,1)S(1)}, bf16[8,1024]{1,0:T(8,128)(2,1)S(1)}) custom-call(s32[2]{0:T(128)S(1)} %get-tuple-element.136.meta, s32[8,16]{1,0:T(8,128)S(1)} %get-tuple-element.137.fp_ref, bf16[2048,1024]{1,0:T(8,128)(2,1)S(1)} %copy-done.1, ...), custom_call_target="tpu_custom_call" | custom-call | tf_op jit(solution)/shard_map/cond/branch_1_fun/partial_gram/pallas_call | solution.py:121
  36.7 2.6 %collective-permute-done.45 = bf16[128,1024]{1,0:T(8,128)(2,1)S(1)} collective-permute-done((bf16[128,1024]{1,0:T(8,128)(2,1)S(1)}, bf16[128,1024]{1,0:T(8,128)(2,1)S(1)}, u32[]{:S(2)}, u32[]{:S(2)}) %collective-permute-start.45) | collective-permute-done | bytes 262176 | tf_op jit(solution)/shard_map/cond/branch_1_fun/ppermute | solution.py:268
  39.4 1.6 %collective-permute-start.34 = (bf16[256,256]{1,0:T(8,128)(2,1)S(1)}, bf16[256,256]{1,0:T(8,128)(2,1)S(1)}, u32[]{:S(2)}, u32[]{:S(2)}) collective-permute-start(bf16[256,256]{1,0:T(8,128)(2,1)S(1)} %get-tuple-element.146), channel_id=1, source_target_pairs={{0,8},{8,0},{16,24},{24,16},{1,9},{9,1},{17,25},{25,17},{2,10},{10... | collective-permute-start | bytes 393224 | tf_op jit(solution)/shard_map/cond/branch_1_fun/ppermute | solution.py:235
  41.0 1.5 %collective-permute-start.35 = (bf16[256,256]{1,0:T(8,128)(2,1)S(1)}, bf16[256,256]{1,0:T(8,128)(2,1)S(1)}, u32[]{:S(2)}, u32[]{:S(2)}) collective-permute-start(bf16[256,256]{1,0:T(8,128)(2,1)S(1)} %get-tuple-element.147), channel_id=1, source_target_pairs={{0,16},{8,24},{16,0},{24,8},{1,17},{9,25},{17,1},{25,9},{2,18},{10... | collective-permute-start | bytes 393224 | tf_op jit(solution)/shard_map/cond/branch_1_fun/ppermute | solution.py:235
  42.5 0.5 collective-permute-start.36
  43.0 3.2 %partial_gram.11 = (f32[256,256]{1,0:T(8,128)S(1)}, bf16[256,256]{1,0:T(8,128)(2,1)S(1)}, bf16[256,256]{1,0:T(8,128)(2,1)S(1)}, bf16[256,256]{1,0:T(8,128)(2,1)S(1)}, bf16[8,1024]{1,0:T(8,128)(2,1)}) custom-call(s32[2]{0:T(128)S(1)} %get-tuple-element.136.meta, s32[8,16]{1,0:T(8,128)S(1)} %get-tuple-element.137.fp_ref, bf16[2048,1024]{1,0:T(8,128)(2,1)S(1)} %copy-done.1, ...), custom_call_target="tpu_custom_call" | custom-call | tf_op jit(solution)/shard_map/cond/branch_1_fun/partial_gram/pallas_call | solution.py:121
  46.2 1.6 %collective-permute-start.47 = (bf16[256,256]{1,0:T(8,128)(2,1)S(1)}, bf16[256,256]{1,0:T(8,128)(2,1)S(1)}, u32[]{:S(2)}, u32[]{:S(2)}) collective-permute-start(bf16[256,256]{1,0:T(8,128)(2,1)S(1)} %get-tuple-element.155), channel_id=1, source_target_pairs={{0,8},{8,0},{16,24},{24,16},{1,9},{9,1},{17,25},{25,17},{2,10},{10... | collective-permute-start | bytes 393224 | tf_op jit(solution)/shard_map/cond/branch_1_fun/ppermute | solution.py:235
  47.8 1.5 %collective-permute-start.48 = (bf16[256,256]{1,0:T(8,128)(2,1)S(1)}, bf16[256,256]{1,0:T(8,128)(2,1)S(1)}, u32[]{:S(2)}, u32[]{:S(2)}) collective-permute-start(bf16[256,256]{1,0:T(8,128)(2,1)S(1)} %get-tuple-element.156), channel_id=1, source_target_pairs={{0,16},{8,24},{16,0},{24,8},{1,17},{9,25},{17,1},{25,9},{2,18},{10... | collective-permute-start | bytes 393224 | tf_op jit(solution)/shard_map/cond/branch_1_fun/ppermute | solution.py:235
  49.3 0.5 collective-permute-start.49
  49.8 1.9 %collective-permute-done.47.refs_5_ = bf16[256,256]{1,0:T(8,128)(2,1)S(1)} collective-permute-done((bf16[256,256]{1,0:T(8,128)(2,1)S(1)}, bf16[256,256]{1,0:T(8,128)(2,1)S(1)}, u32[]{:S(2)}, u32[]{:S(2)}) %collective-permute-start.47) | collective-permute-done | bytes 131104 | tf_op jit(solution)/shard_map/cond/branch_1_fun/ppermute | solution.py:235
  51.7 3.9 %collective-permute-done.48.refs_6_ = bf16[256,256]{1,0:T(8,128)(2,1)S(1)} collective-permute-done((bf16[256,256]{1,0:T(8,128)(2,1)S(1)}, bf16[256,256]{1,0:T(8,128)(2,1)S(1)}, u32[]{:S(2)}, u32[]{:S(2)}) %collective-permute-start.48) | collective-permute-done | bytes 131104 | tf_op jit(solution)/shard_map/cond/branch_1_fun/ppermute | solution.py:235
  55.5 0.2 sum_groups.5
  56.0 0.8 %copy-done.4 = f32[256,512]{1,0:T(8,128)} copy-done((f32[256,512]{1,0:T(8,128)}, f32[256,512]{1,0:T(8,128)S(1)}, u32[]{:S(2)}) %copy-start.4) | copy-done | bytes 524312
  (42 shorter events, 0.8 us)
Async XLA Ops:
  0.0 3.1 %copy-start.5 = (s32[16,8]{0,1:T(8,128)S(1)}, s32[16,8]{0,1:T(8,128)}, u32[]{:S(2)}) copy-start(s32[16,8]{0,1:T(8,128)} %param.11) | copy-start | bytes 1540
  2.6 3.2 %collective-permute-start.100 = (bf16[128,1024]{1,0:T(8,128)(2,1)}, bf16[128,1024]{1,0:T(8,128)(2,1)S(1)}, u32[]{:S(2)}, u32[]{:S(2)}) collective-permute-start(bf16[128,1024]{1,0:T(8,128)(2,1)} %get-tuple-element.211), channel_id=1, source_target_pairs={{0,1},{1,0},{2,3},{3,2},{4,5},{5,4},{6,7},{7,6},{8,9},{9,8},{10,11... | collective-permute-start | bytes 786440 | tf_op jit(solution)/shard_map/ppermute | solution.py:230
  5.9 1.6 %collective-permute-start.29 = (bf16[128,1024]{1,0:T(8,128)(2,1)S(1)}, bf16[128,1024]{1,0:T(8,128)(2,1)S(1)}, u32[]{:S(2)}, u32[]{:S(2)}) collective-permute-start(bf16[128,1024]{1,0:T(8,128)(2,1)S(1)} %get-tuple-element.144), channel_id=1, source_target_pairs={{0,1},{1,0},{2,3},{3,2},{4,5},{5,4},{6,7},{7,6},{8,9},{9,8},{10,11... | collective-permute-start | bytes 786440 | tf_op jit(solution)/shard_map/cond/branch_1_fun/ppermute | solution.py:254
  6.0 5.8 %collective-permute-start.25 = (bf16[128,1024]{1,0:T(8,128)(2,1)S(1)}, bf16[128,1024]{1,0:T(8,128)(2,1)S(1)}, u32[]{:S(2)}, u32[]{:S(2)}) collective-permute-start(bf16[128,1024]{1,0:T(8,128)(2,1)S(1)} %broadcast_select_fusion.4), channel_id=1, source_target_pairs={{2,4},{3,5},{4,2},{5,3},{0,1},{1,0},{6,7},{7,6},{10,12},{11,13},{1... | collective-permute-start | bytes 786440 | tf_op jit(solution)/shard_map/cond/branch_1_fun/ppermute | solution.py:268
  6.5 5.3 %collective-permute-start.37 = (bf16[128,1024]{1,0:T(8,128)(2,1)S(1)}, bf16[128,1024]{1,0:T(8,128)(2,1)S(1)}, u32[]{:S(2)}, u32[]{:S(2)}) collective-permute-start(bf16[128,1024]{1,0:T(8,128)(2,1)S(1)} %get-tuple-element.150), channel_id=1, source_target_pairs={{0,1},{1,0},{2,3},{3,2},{4,5},{5,4},{6,7},{7,6},{8,9},{9,8},{10,11... | collective-permute-start | bytes 786440 | tf_op jit(solution)/shard_map/cond/branch_1_fun/ppermute | solution.py:254
  6.6 5.9 %collective-permute-start.42 = (bf16[128,1024]{1,0:T(8,128)(2,1)}, bf16[128,1024]{1,0:T(8,128)(2,1)S(1)}, u32[]{:S(2)}, u32[]{:S(2)}) collective-permute-start(bf16[128,1024]{1,0:T(8,128)(2,1)} %get-tuple-element.152), channel_id=1, source_target_pairs={{0,1},{1,0},{2,3},{3,2},{4,5},{5,4},{6,7},{7,6},{8,9},{9,8},{10,11... | collective-permute-start | bytes 786440 | tf_op jit(solution)/shard_map/cond/branch_1_fun/ppermute | solution.py:254
  7.5 12.5 %collective-permute-start.30 = (bf16[128,1024]{1,0:T(8,128)(2,1)S(1)}, bf16[128,1024]{1,0:T(8,128)(2,1)S(1)}, u32[]{:S(2)}, u32[]{:S(2)}) collective-permute-start(bf16[128,1024]{1,0:T(8,128)(2,1)S(1)} %broadcast_select_fusion.7), channel_id=1, source_target_pairs={{2,4},{3,5},{4,2},{5,3},{0,1},{1,0},{6,7},{7,6},{10,12},{11,13},{1... | collective-permute-start | bytes 786440 | tf_op jit(solution)/shard_map/cond/branch_1_fun/ppermute | solution.py:268
  7.7 12.3 %collective-permute-start.27 = (bf16[128,1024]{1,0:T(8,128)(2,1)S(1)}, bf16[128,1024]{1,0:T(8,128)(2,1)S(1)}, u32[]{:S(2)}, u32[]{:S(2)}) collective-permute-start(bf16[128,1024]{1,0:T(8,128)(2,1)S(1)} %broadcast_select_fusion.4), channel_id=1, source_target_pairs={{2,0},{3,1},{0,2},{1,3},{4,5},{5,4},{6,7},{7,6},{10,8},{11,9},{8,1... | collective-permute-start | bytes 786440 | tf_op jit(solution)/shard_map/cond/branch_1_fun/ppermute | solution.py:268
  11.8 12.1 %collective-permute-start.26 = (bf16[128,1024]{1,0:T(8,128)(2,1)S(1)}, bf16[128,1024]{1,0:T(8,128)(2,1)S(1)}, u32[]{:S(2)}, u32[]{:S(2)}) collective-permute-start(bf16[128,1024]{1,0:T(8,128)(2,1)S(1)} %collective-permute-done.25), channel_id=1, source_target_pairs={{4,6},{5,7},{6,4},{7,5},{0,1},{1,0},{2,3},{3,2},{12,14},{13,15},{1... | collective-permute-start | bytes 786440 | tf_op jit(solution)/shard_map/cond/branch_1_fun/ppermute | solution.py:268
  11.9 12.3 %collective-permute-start.38 = (bf16[128,1024]{1,0:T(8,128)(2,1)S(1)}, bf16[128,1024]{1,0:T(8,128)(2,1)S(1)}, u32[]{:S(2)}, u32[]{:S(2)}) collective-permute-start(bf16[128,1024]{1,0:T(8,128)(2,1)S(1)} %broadcast_select_fusion.6), channel_id=1, source_target_pairs={{2,4},{3,5},{4,2},{5,3},{0,1},{1,0},{6,7},{7,6},{10,12},{11,13},{1... | collective-permute-start | bytes 786440 | tf_op jit(solution)/shard_map/cond/branch_1_fun/ppermute | solution.py:268
  12.4 21.0 %copy-start.1 = (bf16[2048,1024]{1,0:T(8,128)(2,1)S(1)}, bf16[2048,1024]{1,0:T(8,128)(2,1)}, u32[]{:S(2)}) copy-start(bf16[2048,1024]{1,0:T(8,128)(2,1)} %get-tuple-element.138.green_ref) | copy-start | bytes 12582916 | tf_op jit(solution)/shard_map/cond
  12.5 13.0 %collective-permute-start.32 = (bf16[128,1024]{1,0:T(8,128)(2,1)S(1)}, bf16[128,1024]{1,0:T(8,128)(2,1)S(1)}, u32[]{:S(2)}, u32[]{:S(2)}) collective-permute-start(bf16[128,1024]{1,0:T(8,128)(2,1)S(1)} %broadcast_select_fusion.7), channel_id=1, source_target_pairs={{2,0},{3,1},{0,2},{1,3},{4,5},{5,4},{6,7},{7,6},{10,8},{11,9},{8,1... | collective-permute-start | bytes 786440 | tf_op jit(solution)/shard_map/cond/branch_1_fun/ppermute | solution.py:268
  19.9 5.5 %collective-permute-start.31 = (bf16[128,1024]{1,0:T(8,128)(2,1)S(1)}, bf16[128,1024]{1,0:T(8,128)(2,1)S(1)}, u32[]{:S(2)}, u32[]{:S(2)}) collective-permute-start(bf16[128,1024]{1,0:T(8,128)(2,1)S(1)} %collective-permute-done.30), channel_id=1, source_target_pairs={{4,6},{5,7},{6,4},{7,5},{0,1},{1,0},{2,3},{3,2},{12,14},{13,15},{1... | collective-permute-start | bytes 786440 | tf_op jit(solution)/shard_map/cond/branch_1_fun/ppermute | solution.py:268
  20.0 11.1 %collective-permute-start.40 = (bf16[128,1024]{1,0:T(8,128)(2,1)S(1)}, bf16[128,1024]{1,0:T(8,128)(2,1)S(1)}, u32[]{:S(2)}, u32[]{:S(2)}) collective-permute-start(bf16[128,1024]{1,0:T(8,128)(2,1)S(1)} %broadcast_select_fusion.6), channel_id=1, source_target_pairs={{2,0},{3,1},{0,2},{1,3},{4,5},{5,4},{6,7},{7,6},{10,8},{11,9},{8,1... | collective-permute-start | bytes 786440 | tf_op jit(solution)/shard_map/cond/branch_1_fun/ppermute | solution.py:268
  24.0 8.8 %collective-permute-start.43 = (bf16[128,1024]{1,0:T(8,128)(2,1)S(1)}, bf16[128,1024]{1,0:T(8,128)(2,1)S(1)}, u32[]{:S(2)}, u32[]{:S(2)}) collective-permute-start(bf16[128,1024]{1,0:T(8,128)(2,1)S(1)} %broadcast_select_fusion.5), channel_id=1, source_target_pairs={{2,4},{3,5},{4,2},{5,3},{0,1},{1,0},{6,7},{7,6},{10,12},{11,13},{1... | collective-permute-start | bytes 786440 | tf_op jit(solution)/shard_map/cond/branch_1_fun/ppermute | solution.py:268
  24.2 8.6 %collective-permute-start.39 = (bf16[128,1024]{1,0:T(8,128)(2,1)S(1)}, bf16[128,1024]{1,0:T(8,128)(2,1)S(1)}, u32[]{:S(2)}, u32[]{:S(2)}) collective-permute-start(bf16[128,1024]{1,0:T(8,128)(2,1)S(1)} %collective-permute-done.38), channel_id=1, source_target_pairs={{4,6},{5,7},{6,4},{7,5},{0,1},{1,0},{2,3},{3,2},{12,14},{13,15},{1... | collective-permute-start | bytes 786440 | tf_op jit(solution)/shard_map/cond/branch_1_fun/ppermute | solution.py:268
  25.5 8.0 %collective-permute-start.28 = (bf16[128,1024]{1,0:T(8,128)(2,1)S(1)}, bf16[128,1024]{1,0:T(8,128)(2,1)S(1)}, u32[]{:S(2)}, u32[]{:S(2)}) collective-permute-start(bf16[128,1024]{1,0:T(8,128)(2,1)S(1)} %select_select_fusion.5.refs_0_), channel_id=1, source_target_pairs={{0,1},{1,0},{2,3},{3,2},{4,5},{5,4},{6,7},{7,6},{8,9},{9,8},{10,11... | collective-permute-start | bytes 786440 | tf_op jit(solution)/shard_map/cond/branch_1_fun/ppermute | solution.py:275
  25.6 7.9 %collective-permute-start.33 = (bf16[128,1024]{1,0:T(8,128)(2,1)S(1)}, bf16[128,1024]{1,0:T(8,128)(2,1)S(1)}, u32[]{:S(2)}, u32[]{:S(2)}) collective-permute-start(bf16[128,1024]{1,0:T(8,128)(2,1)S(1)} %select_select_fusion.4.refs_2_), channel_id=1, source_target_pairs={{0,1},{1,0},{2,3},{3,2},{4,5},{5,4},{6,7},{7,6},{8,9},{9,8},{10,11... | collective-permute-start | bytes 786440 | tf_op jit(solution)/shard_map/cond/branch_1_fun/ppermute | solution.py:275
  31.1 8.2 %collective-permute-start.45 = (bf16[128,1024]{1,0:T(8,128)(2,1)S(1)}, bf16[128,1024]{1,0:T(8,128)(2,1)S(1)}, u32[]{:S(2)}, u32[]{:S(2)}) collective-permute-start(bf16[128,1024]{1,0:T(8,128)(2,1)S(1)} %broadcast_select_fusion.5), channel_id=1, source_target_pairs={{2,0},{3,1},{0,2},{1,3},{4,5},{5,4},{6,7},{7,6},{10,8},{11,9},{8,1... | collective-permute-start | bytes 786440 | tf_op jit(solution)/shard_map/cond/branch_1_fun/ppermute | solution.py:268
  32.8 6.5 %collective-permute-start.44 = (bf16[128,1024]{1,0:T(8,128)(2,1)S(1)}, bf16[128,1024]{1,0:T(8,128)(2,1)S(1)}, u32[]{:S(2)}, u32[]{:S(2)}) collective-permute-start(bf16[128,1024]{1,0:T(8,128)(2,1)S(1)} %collective-permute-done.43), channel_id=1, source_target_pairs={{4,6},{5,7},{6,4},{7,5},{0,1},{1,0},{2,3},{3,2},{12,14},{13,15},{1... | collective-permute-start | bytes 786440 | tf_op jit(solution)/shard_map/cond/branch_1_fun/ppermute | solution.py:268
  32.9 10.1 %collective-permute-start.41 = (bf16[128,1024]{1,0:T(8,128)(2,1)S(1)}, bf16[128,1024]{1,0:T(8,128)(2,1)S(1)}, u32[]{:S(2)}, u32[]{:S(2)}) collective-permute-start(bf16[128,1024]{1,0:T(8,128)(2,1)S(1)} %select_select_fusion.3.refs_0_), channel_id=1, source_target_pairs={{0,1},{1,0},{2,3},{3,2},{4,5},{5,4},{6,7},{7,6},{8,9},{9,8},{10,11... | collective-permute-start | bytes 786440 | tf_op jit(solution)/shard_map/cond/branch_1_fun/ppermute | solution.py:275
  39.4 3.6 %collective-permute-start.46 = (bf16[128,1024]{1,0:T(8,128)(2,1)S(1)}, bf16[128,1024]{1,0:T(8,128)(2,1)S(1)}, u32[]{:S(2)}, u32[]{:S(2)}) collective-permute-start(bf16[128,1024]{1,0:T(8,128)(2,1)S(1)} %select_add_fusion.1.refs_2_), channel_id=1, source_target_pairs={{0,1},{1,0},{2,3},{3,2},{4,5},{5,4},{6,7},{7,6},{8,9},{9,8},{10,11... | collective-permute-start | bytes 786440 | tf_op jit(solution)/shard_map/cond/branch_1_fun/ppermute | solution.py:275
  39.4 9.9 %collective-permute-start.34 = (bf16[256,256]{1,0:T(8,128)(2,1)S(1)}, bf16[256,256]{1,0:T(8,128)(2,1)S(1)}, u32[]{:S(2)}, u32[]{:S(2)}) collective-permute-start(bf16[256,256]{1,0:T(8,128)(2,1)S(1)} %get-tuple-element.146), channel_id=1, source_target_pairs={{0,8},{8,0},{16,24},{24,16},{1,9},{9,1},{17,25},{25,17},{2,10},{10... | collective-permute-start | bytes 393224 | tf_op jit(solution)/shard_map/cond/branch_1_fun/ppermute | solution.py:235
  41.0 8.8 %collective-permute-start.35 = (bf16[256,256]{1,0:T(8,128)(2,1)S(1)}, bf16[256,256]{1,0:T(8,128)(2,1)S(1)}, u32[]{:S(2)}, u32[]{:S(2)}) collective-permute-start(bf16[256,256]{1,0:T(8,128)(2,1)S(1)} %get-tuple-element.147), channel_id=1, source_target_pairs={{0,16},{8,24},{16,0},{24,8},{1,17},{9,25},{17,1},{25,9},{2,18},{10... | collective-permute-start | bytes 393224 | tf_op jit(solution)/shard_map/cond/branch_1_fun/ppermute | solution.py:235
  42.5 7.3 %collective-permute-start.36 = (bf16[256,256]{1,0:T(8,128)(2,1)S(1)}, bf16[256,256]{1,0:T(8,128)(2,1)S(1)}, u32[]{:S(2)}, u32[]{:S(2)}) collective-permute-start(bf16[256,256]{1,0:T(8,128)(2,1)S(1)} %get-tuple-element.148), channel_id=1, source_target_pairs={{0,24},{8,16},{16,8},{24,0},{1,25},{9,17},{17,9},{25,1},{2,26},{10... | collective-permute-start | bytes 393224 | tf_op jit(solution)/shard_map/cond/branch_1_fun/ppermute | solution.py:235
  46.2 5.5 %collective-permute-start.47 = (bf16[256,256]{1,0:T(8,128)(2,1)S(1)}, bf16[256,256]{1,0:T(8,128)(2,1)S(1)}, u32[]{:S(2)}, u32[]{:S(2)}) collective-permute-start(bf16[256,256]{1,0:T(8,128)(2,1)S(1)} %get-tuple-element.155), channel_id=1, source_target_pairs={{0,8},{8,0},{16,24},{24,16},{1,9},{9,1},{17,25},{25,17},{2,10},{10... | collective-permute-start | bytes 393224 | tf_op jit(solution)/shard_map/cond/branch_1_fun/ppermute | solution.py:235
  47.8 7.8 %collective-permute-start.48 = (bf16[256,256]{1,0:T(8,128)(2,1)S(1)}, bf16[256,256]{1,0:T(8,128)(2,1)S(1)}, u32[]{:S(2)}, u32[]{:S(2)}) collective-permute-start(bf16[256,256]{1,0:T(8,128)(2,1)S(1)} %get-tuple-element.156), channel_id=1, source_target_pairs={{0,16},{8,24},{16,0},{24,8},{1,17},{9,25},{17,1},{25,9},{2,18},{10... | collective-permute-start | bytes 393224 | tf_op jit(solution)/shard_map/cond/branch_1_fun/ppermute | solution.py:235
  49.3 6.3 %collective-permute-start.49 = (bf16[256,256]{1,0:T(8,128)(2,1)S(1)}, bf16[256,256]{1,0:T(8,128)(2,1)S(1)}, u32[]{:S(2)}, u32[]{:S(2)}) collective-permute-start(bf16[256,256]{1,0:T(8,128)(2,1)S(1)} %get-tuple-element.157), channel_id=1, source_target_pairs={{0,24},{8,16},{16,8},{24,0},{1,25},{9,17},{17,9},{25,1},{2,26},{10... | collective-permute-start | bytes 393224 | tf_op jit(solution)/shard_map/cond/branch_1_fun/ppermute | solution.py:235
  56.0 0.8 %copy-start.4 = (f32[256,512]{1,0:T(8,128)}, f32[256,512]{1,0:T(8,128)S(1)}, u32[]{:S(2)}) copy-start(f32[256,512]{1,0:T(8,128)S(1)} %get-tuple-element.360) | copy-start | bytes 1572868

commit v4 on v3

--- a/solution.py
+++ b/solution.py
@@ -9,8 +9,7 @@
 PANEL = 4
 CHUNKS = ((0,), (1,), (2,), (3,))
 BATCHES = ((0, 1), (2, 3))
-GATES = ((3, ((1, 0),)),)
-MERGE = False
+ALLPREP = False
 STEP = 4
 SWAPPED = True
 FULL = True
@@ -39,23 +38,32 @@
             ((fp_hbm, fp), (set_hbm, sets), (sw_hbm, sw), (scale_hbm, scale), (green_hbm.at[:, at], green))
         )
     ]
-    for copy in copies:
-        copy.start()
-    for copy in copies:
-        copy.wait()
-    core = lax.axis_index(lane) & 1
-    for side in (1, 0):
-        base = (core if side == 0 else 1 - core) * half_blocks
-        for i in range(half_blocks):
-            weight = scale[pl.ds(base + i, 1), :] * sw[sets[base + i]]
-            rows = pl.ds(pl.multiple_of((base + i) * width, width), width)
-            for n, cols in enumerate(chunks):
-                for m, col in enumerate(cols):
-                    block = green[rows, (col - low) * width : (col - low + 1) * width]
-                    value = (block.T.astype(jnp.float32) * weight).astype(jnp.bfloat16)
-                    keep = fp[first + col, base + i] != 0
-                    to = (slice(m * width, (m + 1) * width), slice(i * width, (i + 1) * width))
-                    outs[2 * n + side][to] = jnp.where(keep, value, jnp.zeros_like(value))
+    mine = lax.axis_index(lane) == panel[0] * PANEL // blocks
+
+    @pl.when(mine)
+    def _():
+        for copy in copies:
+            copy.start()
+        for copy in copies:
+            copy.wait()
+        core = lax.axis_index(lane) & 1
+        for side in (1, 0):
+            base = (core if side == 0 else 1 - core) * half_blocks
+            for i in range(half_blocks):
+                weight = scale[pl.ds(base + i, 1), :] * sw[sets[base + i]]
+                rows = pl.ds(pl.multiple_of((base + i) * width, width), width)
+                for n, cols in enumerate(chunks):
+                    for m, col in enumerate(cols):
+                        block = green[rows, (col - low) * width : (col - low + 1) * width]
+                        value = (block.T.astype(jnp.float32) * weight).astype(jnp.bfloat16)
+                        keep = fp[first + col, base + i] != 0
+                        to = (slice(m * width, (m + 1) * width), slice(i * width, (i + 1) * width))
+                        outs[2 * n + side][to] = jnp.where(keep, value, jnp.zeros_like(value))
+
+    @pl.when(jnp.logical_not(mine))
+    def _():
+        for out in outs:
+            out[...] = jnp.zeros_like(out)
 
 
 def prep(chunks, lane, panel_index, footprint, set_index, set_weight, scale, green):
@@ -81,28 +89,32 @@
     )(panel_index, footprint, set_index, set_weight, scale, green)
 
 
-def gram_body(shares, count, width, meta, fp_ref, green_ref, *refs):
-    pieces, outs, done_ref, total_ref, masked_ref = refs[:count], refs[count:-3], refs[-3], refs[-2], refs[-1]
-    done_ref[...] = jnp.zeros_like(done_ref)
+def gram_body(shares, count, width, fresh, meta, fp_ref, green_ref, *refs):
+    pieces, outs, total_ref = refs[:count], refs[count:-1], refs[-1]
     core, group = meta[0], meta[1]
     rows, cols = green_ref.shape
     half = rows // 2
-    step = masked_ref.shape[1]
+    step = STEP * width
+    masked_ref = green_ref
+    if fresh:
+        outs, done_ref, masked_ref = outs[:-2], outs[-2], outs[-1]
+        done_ref[...] = jnp.zeros_like(done_ref)
 
     @pl.loop(0, cols // step)
     def _(n):
-        for i in range(rows // width):
-            for j in range(step // width):
-                at = pl.ds(pl.multiple_of(n * step + j * width, width), width)
-                block = green_ref[i * width : (i + 1) * width, at]
-                block = jnp.where(fp_ref[n * (step // width) + j, i] != 0, block, jnp.zeros_like(block))
-                masked_ref[i * width : (i + 1) * width, j * width : (j + 1) * width] = block
+        here = pl.ds(pl.multiple_of(n * step, step), step)
+        if fresh:
+            for i in range(rows // width):
+                for j in range(step // width):
+                    at = (slice(i * width, (i + 1) * width), pl.ds(pl.multiple_of(n * step + j * width, width), width))
+                    block = green_ref[at]
+                    masked_ref[at] = jnp.where(fp_ref[n * (step // width) + j, i] != 0, block, jnp.zeros_like(block))
         total = 0.0
         for side in range(2):
             at = pl.ds(pl.multiple_of((core if side == 0 else 1 - core) * half, half), half)
             left = jnp.concatenate([p[...] for p in pieces[side::2]], 0)
-            total += jnp.dot(left, masked_ref[at, :], preferred_element_type=jnp.float32)
-        total_ref[:, pl.ds(pl.multiple_of(n * step, step), step)] = total
+            total += jnp.dot(left, masked_ref[at, here], preferred_element_type=jnp.float32)
+        total_ref[:, here] = total
 
     share = cols // shares
     for s in range(len(outs)):
@@ -112,26 +124,30 @@
             outs[s][...] = total_ref[...]
 
 
-def gram(shares, meta, footprint, green, pieces):
+def gram(shares, meta, footprint, green, pieces, fresh):
     rows, unknowns = green.shape
     width = rows // footprint.shape[1]
     share, wide = unknowns // shares, sum(p.shape[0] for p in pieces[::2])
     apart = share % width == 0
     shapes = [jax.ShapeDtypeStruct((wide, share), jnp.float32 if s == 0 else jnp.bfloat16) for s in range(shares)]
+    extra = [jax.ShapeDtypeStruct((8, rows // 2), jnp.bfloat16), jax.ShapeDtypeStruct(green.shape, green.dtype)]
+    all_shapes = (shapes if apart else [jax.ShapeDtypeStruct((wide, unknowns), jnp.float32)]) + (extra if fresh else [])
     out = pl.pallas_call(
-        functools.partial(gram_body, shares, len(pieces), width),
+        functools.partial(gram_body, shares, len(pieces), width, fresh),
         in_specs=[smem()] * 2 + [whole_vmem()] * (1 + len(pieces)),
-        out_specs=[whole_vmem()] * ((shares if apart else 1) + 1),
-        out_shape=(shapes if apart else [jax.ShapeDtypeStruct((wide, unknowns), jnp.float32)])
-        + [jax.ShapeDtypeStruct((8, rows // 2), jnp.bfloat16)],
-        scratch_shapes=[pltpu.VMEM((wide, unknowns), jnp.float32), pltpu.VMEM((rows, STEP * width), jnp.bfloat16)],
+        out_specs=[whole_vmem()] * len(all_shapes),
+        out_shape=all_shapes,
+        scratch_shapes=[pltpu.VMEM((wide, unknowns), jnp.float32)],
         compiler_params=pltpu.CompilerParams(vmem_limit_bytes=VMEM_LIMIT),
         name="partial_gram",
     )(meta, footprint, green, *pieces)
-    if apart:
-        return out
-    cut = [lax.dynamic_slice_in_dim(out[0], (meta[1] ^ s) * share, share, 1).astype(shapes[s].dtype) for s in range(shares)]
-    return [*cut, out[1]]
+    count = shares if apart else 1
+    parts, rest = out[:count], out[count:]
+    if not apart:
+        parts = [
+            lax.dynamic_slice_in_dim(out[0], (meta[1] ^ s) * share, share, 1).astype(shapes[s].dtype) for s in range(shares)
+        ]
+    return list(parts), rest
 
 
 def sum_body(shares, *refs):
@@ -226,9 +242,10 @@
     batches = BATCHES if len(chunks) == len(CHUNKS) else ((0,),)
     last = len(chunks) - 1
 
-    own, other = prep(chunks[:1], *small)
+    weighed = prep(chunks, *small) if ALLPREP else prep(chunks[:1], *small)
+    own, other = weighed[:2]
     start = jnp.where(row == owner, own, lax.ppermute(other, "row", swap))
-    rest = prep((sum(chunks[1:], ()),) if MERGE else chunks[1:], *small) if last else []
+    rest = weighed[2:] if ALLPREP else prep(chunks[1:], *small) if last else []
 
     def exchange(shares):
         return [shares[0]] + [
@@ -244,18 +261,12 @@
 
         def run(meta, met, green, start, *rest):
             sources = [start]
-            if rest and MERGE:
-                own, other = rest[0], lax.ppermute(rest[1], "row", swap)
-                for k in range(last):
-                    at = slice(k * width, (k + 1) * width)
-                    sources.append(jnp.where(row == owner, own[at], other[at]))
-            elif rest:
-                for k in range(last):
-                    sources.append(jnp.where(row == owner, rest[2 * k], lax.ppermute(rest[2 * k + 1], "row", swap)))
-            came, held, pieces, parts, signs = {}, list(sources), {}, [], {}
-            gates = {k: (lambda some=some: [signs[b][n] for b, n in some]) for k, some in GATES} if last else {}
+            for k in range(last):
+                sources.append(jnp.where(row == owner, rest[2 * k], lax.ppermute(rest[2 * k + 1], "row", swap)))
+            came, held, pieces, parts = {}, list(sources), {}, []
+            done, values = None, green
             for step in range(len(chunks) + deepest):
-                for n, (depth, edges) in enumerate(rounds):
+                for n, (depth, edges) in reversed(list(enumerate(rounds))):
                     k = step - depth
                     if not 0 <= k <= last:
                         continue
@@ -270,15 +281,16 @@
                         held[k] = jnp.where(chip == b, came[n, k], held[k])
                 k = step - deepest
                 if k >= 0:
-                    if k in gates:
-                        held[k] = after(held[k], *gates[k]())
+                    if k == last and done is not None:
+                        held[k] = after(held[k], done)
                     pieces[k] = (held[k], lax.ppermute(held[k], "row", swap))
                     for batch in batches:
                         if k == batch[-1]:
-                            shares = gram(groups, meta, met, green, [p for b in batch for p in pieces[b]])
-                            fresh = exchange(shares[:groups])
-                            parts += fresh
-                            signs[k] = (shares[groups], *(p[:1, :1] * jnp.bfloat16(0) for p in fresh[1:]))
+                            ready = [p for b in batch for p in pieces[b]]
+                            shares, extra = gram(groups, meta, met, values, ready, done is None)
+                            if extra:
+                                done, values = extra
+                            parts += exchange(shares)
             return total_of(groups, parts, PANEL * width)
 
         return run

time: 57 us -> 58.1 us (1.019)
  the two profiles are of different devices: /device:TPU:0 before, /device:TPU:8 now
where the time goes in v4:
time: 58.1 us; the launch traced here: 57.9 us
  waiting for transfers between devices  30.8 us (53%)
  starting transfers between devices  17.3 us (30%)
  Pallas kernels  7.29 us (13%)
  local copies, waits for them, and re-layouts  0.82 us (1%)
  between operations  0.76 us (1%)
    ppermute x12, waiting for transfers between devices, run(): lax.ppermute(sent, 'row', pairs(edges, rounds, depth == 0 and k == 0))  23 us
    ppermute x12, starting transfers between devices, run(): lax.ppermute(sent, 'row', pairs(edges, rounds, depth == 0 and k == 0))  9.37 us
    ppermute x6, starting transfers between devices, exchange(): lax.ppermute(shares[s], 'grp', [(g, g ^ s) for g in range(groups)])  7.11 us
    ppermute x6, waiting for transfers between devices, exchange(): lax.ppermute(shares[s], 'grp', [(g, g ^ s) for g in range(groups)])  6.32 us
    pallas_call x2, Pallas kernels, gram(): pl.pallas_call(functools.partial(gram_body, shares, len(pieces), width, f...  5.39 us
    pallas_call x2, Pallas kernels, prep(): pl.pallas_call(functools.partial(prep_body, chunks, lane, width), in_spec...  1.69 us
  transfers between devices with their start and end apart: 26, of which 10 were waited for; matrix products, arithmetic and copies ran while one was open for 1% of the time, Pallas kernels for 11%

profile of v4, /device:TPU:8, one launch (start us, length us, event | category | flops | bytes accessed | tf_op | source)
XLA Modules:
  0.0 57.9 jit_solution(16893488454440383133)
XLA Ops:
  0.7 0.8 %weigh_panel.2 = (bf16[128,1024]{1,0:T(8,128)(2,1)S(1)}, bf16[128,1024]{1,0:T(8,128)(2,1)}) custom-call(s32[1]{0:T(128)S(6)} %copy.15.panel, s32[8,16]{1,0:T(8,128)} %bitcast.5, s32[16]{0:T(128)} %set_hbm.3, f32[8]{0:T(128)} %sw_hbm.3, f32[16,128]{1,0:T(8,128)} %bitcast.11, bf16[2048,1024]{1,0:T(8,128)(2,1)} %green_hbm.3), custom_call_target="tpu_custom_call" | custom-call | tf_op jit(solution)/shard_map/weigh_panel/pallas_call | solution.py:74
  1.6 0.9 %weigh_panel.3 = (bf16[128,1024]{1,0:T(8,128)(2,1)S(1)}, bf16[128,1024]{1,0:T(8,128)(2,1)S(1)}, bf16[128,1024]{1,0:T(8,128)(2,1)S(1)}, bf16[128,1024]{1,0:T(8,12...) custom-call(s32[1]{0:T(128)S(6)} %copy.15.panel, s32[8,16]{1,0:T(8,128)S(1)} %bitcast.6, ...), custom_call_target="tpu_custom_call" | custom-call | tf_op jit(solution)/shard_map/weigh_panel/pallas_call | solution.py:74
  2.6 0.7 %collective-permute-done.100 = bf16[128,1024]{1,0:T(8,128)(2,1)S(1)} collective-permute-done((bf16[128,1024]{1,0:T(8,128)(2,1)}, bf16[128,1024]{1,0:T(8,128)(2,1)S(1)}, u32[]{:S(2)}, u32[]{:S(2)}) %collective-permute-start.100) | collective-permute-done | bytes 262176 | tf_op jit(solution)/shard_map/ppermute | solution.py:247
  3.3 53.8 %conditional.1 = (f32[256,512]{1,0:T(8,128)S(1)}) conditional(s32[]{:T(128)} %clamp.3, (s32[]{:T(128)}, s32[]{:T(128)}, s32[]{:T(128)}, s32[]{:T(128)}, bf16[128,1024]{1,0:T(8,128)(2,1)S(1)}, /*index=5*/bf16[128,1024]{1,0:T(8,128)(2,1)S(1)}, s32[2]{0:T(128)S(1)}, s32[8,16]{1,0:T(8,128)S(1)}, ...), branch_computations={%region_0.1_spmd, %region_1.2_spmd, %region_2.3_spmd, %region_3.4_... | conditional | flops 2228230 | bytes 48241744 | solution.py:298
  3.5 0.4 collective-permute-start
  4.1 0.8 %collective-permute-done.4 = bf16[128,1024]{1,0:T(8,128)(2,1)S(1)} collective-permute-done((bf16[128,1024]{1,0:T(8,128)(2,1)S(1)}, bf16[128,1024]{1,0:T(8,128)(2,1)S(1)}, u32[]{:S(2)}, u32[]{:S(2)}) %collective-permute-start.4) | collective-permute-done | bytes 262176 | tf_op jit(solution)/shard_map/cond/branch_0_fun/ppermute | solution.py:265
  4.9 0.7 %collective-permute-start.5 = (bf16[128,1024]{1,0:T(8,128)(2,1)S(1)}, bf16[128,1024]{1,0:T(8,128)(2,1)S(1)}, u32[]{:S(2)}, u32[]{:S(2)}) collective-permute-start(bf16[128,1024]{1,0:T(8,128)(2,1)S(1)} %broadcast_select_fusion.3), channel_id=1, source_target_pairs={{0,4},{1,5},{8,12},{9,13},{16,20},{17,21},{24,28},{25,29}} | collective-permute-start | bytes 786440 | tf_op jit(solution)/shard_map/cond/branch_0_fun/ppermute | solution.py:279
  6.2 0.7 %collective-permute-start.13 = (bf16[128,1024]{1,0:T(8,128)(2,1)S(1)}, bf16[128,1024]{1,0:T(8,128)(2,1)S(1)}, u32[]{:S(2)}, u32[]{:S(2)}) collective-permute-start(bf16[128,1024]{1,0:T(8,128)(2,1)S(1)} %broadcast_select_fusion.2), channel_id=1, source_target_pairs={{0,4},{1,5},{8,12},{9,13},{16,20},{17,21},{24,28},{25,29}} | collective-permute-start | bytes 786440 | tf_op jit(solution)/shard_map/cond/branch_0_fun/ppermute | solution.py:279
  6.9 1.3 %collective-permute-start.2 = (bf16[128,1024]{1,0:T(8,128)(2,1)S(1)}, bf16[128,1024]{1,0:T(8,128)(2,1)S(1)}, u32[]{:S(2)}, u32[]{:S(2)}) collective-permute-start(bf16[128,1024]{1,0:T(8,128)(2,1)S(1)} %collective-permute-done), channel_id=1, source_target_pairs={{4,2},{5,3},{12,10},{13,11},{20,18},{21,19},{28,26},{29,27}} | collective-permute-start | bytes 786440 | tf_op jit(solution)/shard_map/cond/branch_0_fun/ppermute | solution.py:279
  8.4 1.5 %collective-permute-start.7 = (bf16[128,1024]{1,0:T(8,128)(2,1)S(1)}, bf16[128,1024]{1,0:T(8,128)(2,1)S(1)}, u32[]{:S(2)}, u32[]{:S(2)}) collective-permute-start(bf16[128,1024]{1,0:T(8,128)(2,1)S(1)} %collective-permute-done.5), channel_id=1, source_target_pairs={{4,2},{5,3},{12,10},{13,11},{20,18},{21,19},{28,26},{29,27}} | collective-permute-start | bytes 786440 | tf_op jit(solution)/shard_map/cond/branch_0_fun/ppermute | solution.py:279
  10.0 0.7 %collective-permute-start.18 = (bf16[128,1024]{1,0:T(8,128)(2,1)S(1)}, bf16[128,1024]{1,0:T(8,128)(2,1)S(1)}, u32[]{:S(2)}, u32[]{:S(2)}) collective-permute-start(bf16[128,1024]{1,0:T(8,128)(2,1)S(1)} %broadcast_select_fusion.1), channel_id=1, source_target_pairs={{0,4},{1,5},{8,12},{9,13},{16,20},{17,21},{24,28},{25,29}} | collective-permute-start | bytes 786440 | tf_op jit(solution)/shard_map/cond/branch_0_fun/ppermute | solution.py:279
  10.7 0.4 collective-permute-start.14
  11.1 13.4 %collective-permute-done.2 = bf16[128,1024]{1,0:T(8,128)(2,1)S(1)} collective-permute-done((bf16[128,1024]{1,0:T(8,128)(2,1)S(1)}, bf16[128,1024]{1,0:T(8,128)(2,1)S(1)}, u32[]{:S(2)}, u32[]{:S(2)}) %collective-permute-start.2) | collective-permute-done | bytes 262176 | tf_op jit(solution)/shard_map/cond/branch_0_fun/ppermute | solution.py:279
  24.5 1.3 %collective-permute-start.15 = (bf16[128,1024]{1,0:T(8,128)(2,1)S(1)}, bf16[128,1024]{1,0:T(8,128)(2,1)S(1)}, u32[]{:S(2)}, u32[]{:S(2)}) collective-permute-start(bf16[128,1024]{1,0:T(8,128)(2,1)S(1)} %collective-permute-done.13), channel_id=1, source_target_pairs={{4,2},{5,3},{12,10},{13,11},{20,18},{21,19},{28,26},{29,27}} | collective-permute-start | bytes 786440 | tf_op jit(solution)/shard_map/cond/branch_0_fun/ppermute | solution.py:279
  26.0 4.2 %collective-permute-done.7 = bf16[128,1024]{1,0:T(8,128)(2,1)S(1)} collective-permute-done((bf16[128,1024]{1,0:T(8,128)(2,1)S(1)}, bf16[128,1024]{1,0:T(8,128)(2,1)S(1)}, u32[]{:S(2)}, u32[]{:S(2)}) %collective-permute-start.7) | collective-permute-done | bytes 262176 | tf_op jit(solution)/shard_map/cond/branch_0_fun/ppermute | solution.py:279
  30.3 0.5 collective-permute-start.19
  30.8 1.3 %collective-permute-start.20 = (bf16[128,1024]{1,0:T(8,128)(2,1)S(1)}, bf16[128,1024]{1,0:T(8,128)(2,1)S(1)}, u32[]{:S(2)}, u32[]{:S(2)}) collective-permute-start(bf16[128,1024]{1,0:T(8,128)(2,1)S(1)} %collective-permute-done.18), channel_id=1, source_target_pairs={{4,2},{5,3},{12,10},{13,11},{20,18},{21,19},{28,26},{29,27}} | collective-permute-start | bytes 786440 | tf_op jit(solution)/shard_map/cond/branch_0_fun/ppermute | solution.py:279
  32.1 2.4 %collective-permute-done.15 = bf16[128,1024]{1,0:T(8,128)(2,1)S(1)} collective-permute-done((bf16[128,1024]{1,0:T(8,128)(2,1)S(1)}, bf16[128,1024]{1,0:T(8,128)(2,1)S(1)}, u32[]{:S(2)}, u32[]{:S(2)}) %collective-permute-start.15) | collective-permute-done | bytes 262176 | tf_op jit(solution)/shard_map/cond/branch_0_fun/ppermute | solution.py:279
  34.7 3.3 %partial_gram.8 = (f32[256,256]{1,0:T(8,128)S(1)}, bf16[256,256]{1,0:T(8,128)(2,1)S(1)}, bf16[256,256]{1,0:T(8,128)(2,1)S(1)}, bf16[256,256]{1,0:T(8,128)(2,1)S(...) custom-call(s32[2]{0:T(128)S(1)} %get-tuple-element.112.meta, s32[8,16]{1,0:T(8,128)S(1)} %get-tuple-element.114.fp_ref, ...), custom_call_target="tpu_custom_call" | custom-call | tf_op jit(solution)/shard_map/cond/branch_0_fun/partial_gram/pallas_call | solution.py:135
  38.0 3.0 %collective-permute-done.20 = bf16[128,1024]{1,0:T(8,128)(2,1)S(1)} collective-permute-done((bf16[128,1024]{1,0:T(8,128)(2,1)S(1)}, bf16[128,1024]{1,0:T(8,128)(2,1)S(1)}, u32[]{:S(2)}, u32[]{:S(2)}) %collective-permute-start.20) | collective-permute-done | bytes 262176 | tf_op jit(solution)/shard_map/cond/branch_0_fun/ppermute | solution.py:279
  41.1 1.6 %collective-permute-start.9 = (bf16[256,256]{1,0:T(8,128)(2,1)S(1)}, bf16[256,256]{1,0:T(8,128)(2,1)S(1)}, u32[]{:S(2)}, u32[]{:S(2)}) collective-permute-start(bf16[256,256]{1,0:T(8,128)(2,1)S(1)} %get-tuple-element.124), channel_id=1, source_target_pairs={{0,8},{8,0},{16,24},{24,16},{1,9},{9,1},{17,25},{25,17},{2,10},{10... | collective-permute-start | bytes 393224 | tf_op jit(solution)/shard_map/cond/branch_0_fun/ppermute | solution.py:252
  42.7 1.5 %collective-permute-start.10 = (bf16[256,256]{1,0:T(8,128)(2,1)S(1)}, bf16[256,256]{1,0:T(8,128)(2,1)S(1)}, u32[]{:S(2)}, u32[]{:S(2)}) collective-permute-start(bf16[256,256]{1,0:T(8,128)(2,1)S(1)} %get-tuple-element.125), channel_id=1, source_target_pairs={{0,16},{8,24},{16,0},{24,8},{1,17},{9,25},{17,1},{25,9},{2,18},{10... | collective-permute-start | bytes 393224 | tf_op jit(solution)/shard_map/cond/branch_0_fun/ppermute | solution.py:252
  44.2 0.5 collective-permute-start.11
  44.7 2.1 %partial_gram.9 = (f32[256,256]{1,0:T(8,128)S(1)}, bf16[256,256]{1,0:T(8,128)(2,1)S(1)}, bf16[256,256]{1,0:T(8,128)(2,1)S(1)}, bf16[256,256]{1,0:T(8,128)(2,1)S(1)}) custom-call(s32[2]{0:T(128)S(1)} %get-tuple-element.112.meta, s32[8,16]{1,0:T(8,128)S(1)} %get-tuple-element.114.fp_ref, bf16[2048,1024]{1,0:T(8,128)(2,1)S(1)} %get-tuple-element.127.green_ref, ...), custom_call_target="tpu_custom_call" | custom-call | tf_op jit(solution)/shard_map/cond/branch_0_fun/partial_gram/pallas_call | solution.py:135
  46.8 1.6 %collective-permute-start.22 = (bf16[256,256]{1,0:T(8,128)(2,1)S(1)}, bf16[256,256]{1,0:T(8,128)(2,1)S(1)}, u32[]{:S(2)}, u32[]{:S(2)}) collective-permute-start(bf16[256,256]{1,0:T(8,128)(2,1)S(1)} %get-tuple-element.134), channel_id=1, source_target_pairs={{0,8},{8,0},{16,24},{24,16},{1,9},{9,1},{17,25},{25,17},{2,10},{10... | collective-permute-start | bytes 393224 | tf_op jit(solution)/shard_map/cond/branch_0_fun/ppermute | solution.py:252
  48.3 1.5 %collective-permute-start.23 = (bf16[256,256]{1,0:T(8,128)(2,1)S(1)}, bf16[256,256]{1,0:T(8,128)(2,1)S(1)}, u32[]{:S(2)}, u32[]{:S(2)}) collective-permute-start(bf16[256,256]{1,0:T(8,128)(2,1)S(1)} %get-tuple-element.135), channel_id=1, source_target_pairs={{0,16},{8,24},{16,0},{24,8},{1,17},{9,25},{17,1},{25,9},{2,18},{10... | collective-permute-start | bytes 393224 | tf_op jit(solution)/shard_map/cond/branch_0_fun/ppermute | solution.py:252
  49.9 0.5 collective-permute-start.24
  50.3 0.4 collective-permute-done.10.refs_2_
  50.7 0.8 %collective-permute-done.11.refs_3_ = bf16[256,256]{1,0:T(8,128)(2,1)S(1)} collective-permute-done((bf16[256,256]{1,0:T(8,128)(2,1)S(1)}, bf16[256,256]{1,0:T(8,128)(2,1)S(1)}, u32[]{:S(2)}, u32[]{:S(2)}) %collective-permute-start.11) | collective-permute-done | bytes 131104 | tf_op jit(solution)/shard_map/cond/branch_0_fun/ppermute | solution.py:252
  51.5 1.9 %collective-permute-done.22.refs_5_ = bf16[256,256]{1,0:T(8,128)(2,1)S(1)} collective-permute-done((bf16[256,256]{1,0:T(8,128)(2,1)S(1)}, bf16[256,256]{1,0:T(8,128)(2,1)S(1)}, u32[]{:S(2)}, u32[]{:S(2)}) %collective-permute-start.22) | collective-permute-done | bytes 131104 | tf_op jit(solution)/shard_map/cond/branch_0_fun/ppermute | solution.py:252
  53.4 3.3 %collective-permute-done.23.refs_6_ = bf16[256,256]{1,0:T(8,128)(2,1)S(1)} collective-permute-done((bf16[256,256]{1,0:T(8,128)(2,1)S(1)}, bf16[256,256]{1,0:T(8,128)(2,1)S(1)}, u32[]{:S(2)}, u32[]{:S(2)}) %collective-permute-start.23) | collective-permute-done | bytes 131104 | tf_op jit(solution)/shard_map/cond/branch_0_fun/ppermute | solution.py:252
  57.1 0.8 %copy-done.4 = f32[256,512]{1,0:T(8,128)} copy-done((f32[256,512]{1,0:T(8,128)}, f32[256,512]{1,0:T(8,128)S(1)}, u32[]{:S(2)}) %copy-start.4) | copy-done | bytes 524312
  (42 shorter events, 2.2 us)
Async XLA Ops:
  0.0 1.6 %copy-start.5 = (s32[16,8]{0,1:T(8,128)S(1)}, s32[16,8]{0,1:T(8,128)}, u32[]{:S(2)}) copy-start(s32[16,8]{0,1:T(8,128)} %param.11) | copy-start | bytes 1540
  1.5 1.8 %collective-permute-start.100 = (bf16[128,1024]{1,0:T(8,128)(2,1)}, bf16[128,1024]{1,0:T(8,128)(2,1)S(1)}, u32[]{:S(2)}, u32[]{:S(2)}) collective-permute-start(bf16[128,1024]{1,0:T(8,128)(2,1)} %get-tuple-element.215), channel_id=1, source_target_pairs={{0,1},{1,0},{2,3},{3,2},{4,5},{5,4},{6,7},{7,6},{8,9},{9,8},{10,11... | collective-permute-start | bytes 786440 | tf_op jit(solution)/shard_map/ppermute | solution.py:247
  3.3 1.5 %collective-permute-start.4 = (bf16[128,1024]{1,0:T(8,128)(2,1)S(1)}, bf16[128,1024]{1,0:T(8,128)(2,1)S(1)}, u32[]{:S(2)}, u32[]{:S(2)}) collective-permute-start(bf16[128,1024]{1,0:T(8,128)(2,1)S(1)} %get-tuple-element.122), channel_id=1, source_target_pairs={{0,1},{1,0},{2,3},{3,2},{4,5},{5,4},{6,7},{7,6},{8,9},{9,8},{10,11... | collective-permute-start | bytes 786440 | tf_op jit(solution)/shard_map/cond/branch_0_fun/ppermute | solution.py:265
  3.5 2.3 %collective-permute-start = (bf16[128,1024]{1,0:T(8,128)(2,1)S(1)}, bf16[128,1024]{1,0:T(8,128)(2,1)S(1)}, u32[]{:S(2)}, u32[]{:S(2)}) collective-permute-start(bf16[128,1024]{1,0:T(8,128)(2,1)S(1)} %broadcast_select_fusion), channel_id=1, source_target_pairs={{0,4},{1,5},{4,0},{5,1},{2,3},{3,2},{6,7},{7,6},{8,12},{9,13},{12,... | collective-permute-start | bytes 786440 | tf_op jit(solution)/shard_map/cond/branch_0_fun/ppermute | solution.py:279
  3.9 2.2 %collective-permute-start.12 = (bf16[128,1024]{1,0:T(8,128)(2,1)}, bf16[128,1024]{1,0:T(8,128)(2,1)S(1)}, u32[]{:S(2)}, u32[]{:S(2)}) collective-permute-start(bf16[128,1024]{1,0:T(8,128)(2,1)} %get-tuple-element.129), channel_id=1, source_target_pairs={{0,1},{1,0},{2,3},{3,2},{4,5},{5,4},{6,7},{7,6},{8,9},{9,8},{10,11... | collective-permute-start | bytes 786440 | tf_op jit(solution)/shard_map/cond/branch_0_fun/ppermute | solution.py:265
  4.9 3.3 %collective-permute-start.5 = (bf16[128,1024]{1,0:T(8,128)(2,1)S(1)}, bf16[128,1024]{1,0:T(8,128)(2,1)S(1)}, u32[]{:S(2)}, u32[]{:S(2)}) collective-permute-start(bf16[128,1024]{1,0:T(8,128)(2,1)S(1)} %broadcast_select_fusion.3), channel_id=1, source_target_pairs={{0,4},{1,5},{8,12},{9,13},{16,20},{17,21},{24,28},{25,29}} | collective-permute-start | bytes 786440 | tf_op jit(solution)/shard_map/cond/branch_0_fun/ppermute | solution.py:279
  5.6 2.8 %collective-permute-start.17 = (bf16[128,1024]{1,0:T(8,128)(2,1)S(1)}, bf16[128,1024]{1,0:T(8,128)(2,1)S(1)}, u32[]{:S(2)}, u32[]{:S(2)}) collective-permute-start(bf16[128,1024]{1,0:T(8,128)(2,1)S(1)} %get-tuple-element.131), channel_id=1, source_target_pairs={{0,1},{1,0},{2,3},{3,2},{4,5},{5,4},{6,7},{7,6},{8,9},{9,8},{10,11... | collective-permute-start | bytes 786440 | tf_op jit(solution)/shard_map/cond/branch_0_fun/ppermute | solution.py:265
  5.8 4.2 %collective-permute-start.1 = (bf16[128,1024]{1,0:T(8,128)(2,1)S(1)}, bf16[128,1024]{1,0:T(8,128)(2,1)S(1)}, u32[]{:S(2)}, u32[]{:S(2)}) collective-permute-start(bf16[128,1024]{1,0:T(8,128)(2,1)S(1)} %collective-permute-done), channel_id=1, source_target_pairs={{4,6},{5,7},{6,4},{7,5},{0,1},{1,0},{2,3},{3,2},{12,14},{13,15},{1... | collective-permute-start | bytes 786440 | tf_op jit(solution)/shard_map/cond/branch_0_fun/ppermute | solution.py:279
  6.2 4.5 %collective-permute-start.13 = (bf16[128,1024]{1,0:T(8,128)(2,1)S(1)}, bf16[128,1024]{1,0:T(8,128)(2,1)S(1)}, u32[]{:S(2)}, u32[]{:S(2)}) collective-permute-start(bf16[128,1024]{1,0:T(8,128)(2,1)S(1)} %broadcast_select_fusion.2), channel_id=1, source_target_pairs={{0,4},{1,5},{8,12},{9,13},{16,20},{17,21},{24,28},{25,29}} | collective-permute-start | bytes 786440 | tf_op jit(solution)/shard_map/cond/branch_0_fun/ppermute | solution.py:279
  6.9 17.7 %collective-permute-start.2 = (bf16[128,1024]{1,0:T(8,128)(2,1)S(1)}, bf16[128,1024]{1,0:T(8,128)(2,1)S(1)}, u32[]{:S(2)}, u32[]{:S(2)}) collective-permute-start(bf16[128,1024]{1,0:T(8,128)(2,1)S(1)} %collective-permute-done), channel_id=1, source_target_pairs={{4,2},{5,3},{12,10},{13,11},{20,18},{21,19},{28,26},{29,27}} | collective-permute-start | bytes 786440 | tf_op jit(solution)/shard_map/cond/branch_0_fun/ppermute | solution.py:279
  8.2 26.5 %copy-start = (bf16[2048,1024]{1,0:T(8,128)(2,1)S(1)}, bf16[2048,1024]{1,0:T(8,128)(2,1)}, u32[]{:S(2)}) copy-start(bf16[2048,1024]{1,0:T(8,128)(2,1)} %get-tuple-element.116.green_ref) | copy-start | bytes 12582916 | tf_op jit(solution)/shard_map/cond
  8.2 17.7 %collective-permute-start.6 = (bf16[128,1024]{1,0:T(8,128)(2,1)S(1)}, bf16[128,1024]{1,0:T(8,128)(2,1)S(1)}, u32[]{:S(2)}, u32[]{:S(2)}) collective-permute-start(bf16[128,1024]{1,0:T(8,128)(2,1)S(1)} %collective-permute-done.5), channel_id=1, source_target_pairs={{4,6},{5,7},{6,4},{7,5},{0,1},{1,0},{2,3},{3,2},{12,14},{13,15},{1... | collective-permute-start | bytes 786440 | tf_op jit(solution)/shard_map/cond/branch_0_fun/ppermute | solution.py:279
  8.4 21.7 %collective-permute-start.7 = (bf16[128,1024]{1,0:T(8,128)(2,1)S(1)}, bf16[128,1024]{1,0:T(8,128)(2,1)S(1)}, u32[]{:S(2)}, u32[]{:S(2)}) collective-permute-start(bf16[128,1024]{1,0:T(8,128)(2,1)S(1)} %collective-permute-done.5), channel_id=1, source_target_pairs={{4,2},{5,3},{12,10},{13,11},{20,18},{21,19},{28,26},{29,27}} | collective-permute-start | bytes 786440 | tf_op jit(solution)/shard_map/cond/branch_0_fun/ppermute | solution.py:279
  10.0 20.3 %collective-permute-start.18 = (bf16[128,1024]{1,0:T(8,128)(2,1)S(1)}, bf16[128,1024]{1,0:T(8,128)(2,1)S(1)}, u32[]{:S(2)}, u32[]{:S(2)}) collective-permute-start(bf16[128,1024]{1,0:T(8,128)(2,1)S(1)} %broadcast_select_fusion.1), channel_id=1, source_target_pairs={{0,4},{1,5},{8,12},{9,13},{16,20},{17,21},{24,28},{25,29}} | collective-permute-start | bytes 786440 | tf_op jit(solution)/shard_map/cond/branch_0_fun/ppermute | solution.py:279
  10.7 20.1 %collective-permute-start.14 = (bf16[128,1024]{1,0:T(8,128)(2,1)S(1)}, bf16[128,1024]{1,0:T(8,128)(2,1)S(1)}, u32[]{:S(2)}, u32[]{:S(2)}) collective-permute-start(bf16[128,1024]{1,0:T(8,128)(2,1)S(1)} %collective-permute-done.13), channel_id=1, source_target_pairs={{4,6},{5,7},{6,4},{7,5},{0,1},{1,0},{2,3},{3,2},{12,14},{13,15},{1... | collective-permute-start | bytes 786440 | tf_op jit(solution)/shard_map/cond/branch_0_fun/ppermute | solution.py:279
  24.5 10.0 %collective-permute-start.15 = (bf16[128,1024]{1,0:T(8,128)(2,1)S(1)}, bf16[128,1024]{1,0:T(8,128)(2,1)S(1)}, u32[]{:S(2)}, u32[]{:S(2)}) collective-permute-start(bf16[128,1024]{1,0:T(8,128)(2,1)S(1)} %collective-permute-done.13), channel_id=1, source_target_pairs={{4,2},{5,3},{12,10},{13,11},{20,18},{21,19},{28,26},{29,27}} | collective-permute-start | bytes 786440 | tf_op jit(solution)/shard_map/cond/branch_0_fun/ppermute | solution.py:279
  25.9 8.8 %collective-permute-start.3 = (bf16[128,1024]{1,0:T(8,128)(2,1)S(1)}, bf16[128,1024]{1,0:T(8,128)(2,1)S(1)}, u32[]{:S(2)}, u32[]{:S(2)}) collective-permute-start(bf16[128,1024]{1,0:T(8,128)(2,1)S(1)} %select_select_fusion.2.refs_0_), channel_id=1, source_target_pairs={{0,1},{1,0},{2,3},{3,2},{4,5},{5,4},{6,7},{7,6},{8,9},{9,8},{10,11... | collective-permute-start | bytes 786440 | tf_op jit(solution)/shard_map/cond/branch_0_fun/ppermute | solution.py:286
  30.2 4.4 %collective-permute-start.8 = (bf16[128,1024]{1,0:T(8,128)(2,1)S(1)}, bf16[128,1024]{1,0:T(8,128)(2,1)S(1)}, u32[]{:S(2)}, u32[]{:S(2)}) collective-permute-start(bf16[128,1024]{1,0:T(8,128)(2,1)S(1)} %select_select_fusion.1.refs_2_), channel_id=1, source_target_pairs={{0,1},{1,0},{2,3},{3,2},{4,5},{5,4},{6,7},{7,6},{8,9},{9,8},{10,11... | collective-permute-start | bytes 786440 | tf_op jit(solution)/shard_map/cond/branch_0_fun/ppermute | solution.py:286
  30.3 7.7 %collective-permute-start.19 = (bf16[128,1024]{1,0:T(8,128)(2,1)S(1)}, bf16[128,1024]{1,0:T(8,128)(2,1)S(1)}, u32[]{:S(2)}, u32[]{:S(2)}) collective-permute-start(bf16[128,1024]{1,0:T(8,128)(2,1)S(1)} %collective-permute-done.18), channel_id=1, source_target_pairs={{4,6},{5,7},{6,4},{7,5},{0,1},{1,0},{2,3},{3,2},{12,14},{13,15},{1... | collective-permute-start | bytes 786440 | tf_op jit(solution)/shard_map/cond/branch_0_fun/ppermute | solution.py:279
  30.8 10.2 %collective-permute-start.20 = (bf16[128,1024]{1,0:T(8,128)(2,1)S(1)}, bf16[128,1024]{1,0:T(8,128)(2,1)S(1)}, u32[]{:S(2)}, u32[]{:S(2)}) collective-permute-start(bf16[128,1024]{1,0:T(8,128)(2,1)S(1)} %collective-permute-done.18), channel_id=1, source_target_pairs={{4,2},{5,3},{12,10},{13,11},{20,18},{21,19},{28,26},{29,27}} | collective-permute-start | bytes 786440 | tf_op jit(solution)/shard_map/cond/branch_0_fun/ppermute | solution.py:279
  34.6 10.1 %collective-permute-start.16 = (bf16[128,1024]{1,0:T(8,128)(2,1)S(1)}, bf16[128,1024]{1,0:T(8,128)(2,1)S(1)}, u32[]{:S(2)}, u32[]{:S(2)}) collective-permute-start(bf16[128,1024]{1,0:T(8,128)(2,1)S(1)} %select_select_fusion.refs_0_), channel_id=1, source_target_pairs={{0,1},{1,0},{2,3},{3,2},{4,5},{5,4},{6,7},{7,6},{8,9},{9,8},{10,11... | collective-permute-start | bytes 786440 | tf_op jit(solution)/shard_map/cond/branch_0_fun/ppermute | solution.py:286
  41.0 3.6 %collective-permute-start.21 = (bf16[128,1024]{1,0:T(8,128)(2,1)S(1)}, bf16[128,1024]{1,0:T(8,128)(2,1)S(1)}, u32[]{:S(2)}, u32[]{:S(2)}) collective-permute-start(bf16[128,1024]{1,0:T(8,128)(2,1)S(1)} %select_add_fusion.refs_2_), channel_id=1, source_target_pairs={{0,1},{1,0},{2,3},{3,2},{4,5},{5,4},{6,7},{7,6},{8,9},{9,8},{10,11... | collective-permute-start | bytes 786440 | tf_op jit(solution)/shard_map/cond/branch_0_fun/ppermute | solution.py:286
  41.1 8.8 %collective-permute-start.9 = (bf16[256,256]{1,0:T(8,128)(2,1)S(1)}, bf16[256,256]{1,0:T(8,128)(2,1)S(1)}, u32[]{:S(2)}, u32[]{:S(2)}) collective-permute-start(bf16[256,256]{1,0:T(8,128)(2,1)S(1)} %get-tuple-element.124), channel_id=1, source_target_pairs={{0,8},{8,0},{16,24},{24,16},{1,9},{9,1},{17,25},{25,17},{2,10},{10... | collective-permute-start | bytes 393224 | tf_op jit(solution)/shard_map/cond/branch_0_fun/ppermute | solution.py:252
  42.7 8.1 %collective-permute-start.10 = (bf16[256,256]{1,0:T(8,128)(2,1)S(1)}, bf16[256,256]{1,0:T(8,128)(2,1)S(1)}, u32[]{:S(2)}, u32[]{:S(2)}) collective-permute-start(bf16[256,256]{1,0:T(8,128)(2,1)S(1)} %get-tuple-element.125), channel_id=1, source_target_pairs={{0,16},{8,24},{16,0},{24,8},{1,17},{9,25},{17,1},{25,9},{2,18},{10... | collective-permute-start | bytes 393224 | tf_op jit(solution)/shard_map/cond/branch_0_fun/ppermute | solution.py:252
  44.2 7.3 %collective-permute-start.11 = (bf16[256,256]{1,0:T(8,128)(2,1)S(1)}, bf16[256,256]{1,0:T(8,128)(2,1)S(1)}, u32[]{:S(2)}, u32[]{:S(2)}) collective-permute-start(bf16[256,256]{1,0:T(8,128)(2,1)S(1)} %get-tuple-element.126), channel_id=1, source_target_pairs={{0,24},{8,16},{16,8},{24,0},{1,25},{9,17},{17,9},{25,1},{2,26},{10... | collective-permute-start | bytes 393224 | tf_op jit(solution)/shard_map/cond/branch_0_fun/ppermute | solution.py:252
  46.8 6.6 %collective-permute-start.22 = (bf16[256,256]{1,0:T(8,128)(2,1)S(1)}, bf16[256,256]{1,0:T(8,128)(2,1)S(1)}, u32[]{:S(2)}, u32[]{:S(2)}) collective-permute-start(bf16[256,256]{1,0:T(8,128)(2,1)S(1)} %get-tuple-element.134), channel_id=1, source_target_pairs={{0,8},{8,0},{16,24},{24,16},{1,9},{9,1},{17,25},{25,17},{2,10},{10... | collective-permute-start | bytes 393224 | tf_op jit(solution)/shard_map/cond/branch_0_fun/ppermute | solution.py:252
  48.3 8.3 %collective-permute-start.23 = (bf16[256,256]{1,0:T(8,128)(2,1)S(1)}, bf16[256,256]{1,0:T(8,128)(2,1)S(1)}, u32[]{:S(2)}, u32[]{:S(2)}) collective-permute-start(bf16[256,256]{1,0:T(8,128)(2,1)S(1)} %get-tuple-element.135), channel_id=1, source_target_pairs={{0,16},{8,24},{16,0},{24,8},{1,17},{9,25},{17,1},{25,9},{2,18},{10... | collective-permute-start | bytes 393224 | tf_op jit(solution)/shard_map/cond/branch_0_fun/ppermute | solution.py:252
  49.9 6.8 %collective-permute-start.24 = (bf16[256,256]{1,0:T(8,128)(2,1)S(1)}, bf16[256,256]{1,0:T(8,128)(2,1)S(1)}, u32[]{:S(2)}, u32[]{:S(2)}) collective-permute-start(bf16[256,256]{1,0:T(8,128)(2,1)S(1)} %get-tuple-element.136), channel_id=1, source_target_pairs={{0,24},{8,16},{16,8},{24,0},{1,25},{9,17},{17,9},{25,1},{2,26},{10... | collective-permute-start | bytes 393224 | tf_op jit(solution)/shard_map/cond/branch_0_fun/ppermute | solution.py:252
  57.1 0.8 %copy-start.4 = (f32[256,512]{1,0:T(8,128)}, f32[256,512]{1,0:T(8,128)S(1)}, u32[]{:S(2)}) copy-start(f32[256,512]{1,0:T(8,128)S(1)} %get-tuple-element.364) | copy-start | bytes 1572868

commit v5 on v4

--- a/solution.py
+++ b/solution.py
@@ -66,7 +66,7 @@
             out[...] = jnp.zeros_like(out)
 
 
-def prep(chunks, lane, panel_index, footprint, set_index, set_weight, scale, green):
+def prep(limit, chunks, lane, panel_index, footprint, set_index, set_weight, scale, green):
     rows = green.shape[0]
     width = rows // footprint.shape[1]
     count = sum(len(cols) for cols in chunks)
@@ -84,7 +84,7 @@
             pltpu.VMEM((rows, count * width), jnp.bfloat16),
             pltpu.SemaphoreType.DMA((5,)),
         ],
-        compiler_params=pltpu.CompilerParams(vmem_limit_bytes=PREP_LIMIT),
+        compiler_params=pltpu.CompilerParams(vmem_limit_bytes=limit),
         name="weigh_panel",
     )(panel_index, footprint, set_index, set_weight, scale, green)
 
@@ -242,10 +242,10 @@
     batches = BATCHES if len(chunks) == len(CHUNKS) else ((0,),)
     last = len(chunks) - 1
 
-    weighed = prep(chunks, *small) if ALLPREP else prep(chunks[:1], *small)
+    weighed = prep(PREP_LIMIT, chunks[:2], *small)
     own, other = weighed[:2]
     start = jnp.where(row == owner, own, lax.ppermute(other, "row", swap))
-    rest = weighed[2:] if ALLPREP else prep(chunks[1:], *small) if last else []
+    rest = weighed[2:]
 
     def exchange(shares):
         return [shares[0]] + [
@@ -259,8 +259,10 @@
         deepest = rounds[-1][0]
         parent = {b: n for n, (_, edges) in enumerate(rounds) for _, b in edges}
 
-        def run(meta, met, green, start, *rest):
+        def run(meta, panel_index, met, set_index, set_weight, scale, green, start, *rest):
             sources = [start]
+            if last:
+                rest = [*rest, *prep(VMEM_LIMIT, chunks[2:], "row", panel_index, met, set_index, set_weight, scale, green)]
             for k in range(last):
                 sources.append(jnp.where(row == owner, rest[2 * k], lax.ppermute(rest[2 * k + 1], "row", swap)))
             came, held, pieces, parts = {}, list(sources), {}, []
@@ -276,7 +278,7 @@
                         sent = came[parent[edges[0][0]], k]
                         for a, _ in edges[1:]:
                             sent = jnp.where(chip == a, came[parent[a], k], sent)
-                    came[n, k] = lax.ppermute(sent, "row", pairs(edges, rounds, depth == 0 and k == 0))
+                    came[n, k] = lax.ppermute(sent, "row", pairs(edges, rounds, (depth == 0 and k == 0) or (depth > 0 and k == last > 0)))
                     for _, b in edges:
                         held[k] = jnp.where(chip == b, came[n, k], held[k])
                 k = step - deepest
@@ -295,7 +297,7 @@
 
         return run
 
-    return lax.switch(owner >> 1, [from_chip(source) for source in range(chips)], meta, met, green, start, *rest)
+    return lax.switch(owner >> 1, [from_chip(source) for source in range(chips)], meta, *small[1:], start, *rest)
 
 
 def solution(mesh):

time: 58.1 us -> 56 us (0.964)
  the two profiles are of different devices: /device:TPU:8 before, /device:TPU:0 now
where the time goes in v5:
time: 56 us; the launch traced here: 55.4 us
  starting transfers between devices  29.6 us (53%)
  waiting for transfers between devices  16.2 us (29%)
  Pallas kernels  7.2 us (13%)
  local copies, waits for them, and re-layouts  0.83 us (1%)
  between operations  0.74 us (1%)
    ppermute x12, starting transfers between devices, run(): lax.ppermute(sent, 'row', pairs(edges, rounds, depth == 0 and k == 0 or (...  19.8 us
    ppermute x12, waiting for transfers between devices, run(): lax.ppermute(sent, 'row', pairs(edges, rounds, depth == 0 and k == 0 or (...  8.53 us
    ppermute x6, starting transfers between devices, exchange(): lax.ppermute(shares[s], 'grp', [(g, g ^ s) for g in range(groups)])  7.11 us
    ppermute x6, waiting for transfers between devices, exchange(): lax.ppermute(shares[s], 'grp', [(g, g ^ s) for g in range(groups)])  6.32 us
    pallas_call x2, Pallas kernels, gram(): pl.pallas_call(functools.partial(gram_body, shares, len(pieces), width, f...  5.39 us
    pallas_call x2, Pallas kernels, prep(): pl.pallas_call(functools.partial(prep_body, chunks, lane, width), in_spec...  1.6 us
    ppermute x1, waiting for transfers between devices, on_device(): start = jnp.where(row == owner, own, lax.ppermute(other, 'row', swap))  1.3 us
    ppermute x4, starting transfers between devices, run(): pieces[k] = (held[k], lax.ppermute(held[k], 'row', swap))  1.21 us
  transfers between devices with their start and end apart: 26, of which 9 were waited for; matrix products, arithmetic and copies ran while one was open for 1% of the time, Pallas kernels for 11%

profile of v5, /device:TPU:0, one launch (start us, length us, event | category | flops | bytes accessed | tf_op | source)
XLA Modules:
  0.0 55.4 jit_solution(8482033020065027327)
XLA Ops:
  0.7 0.8 %weigh_panel.9 = (bf16[128,1024]{1,0:T(8,128)(2,1)S(1)}, bf16[128,1024]{1,0:T(8,128)(2,1)}, bf16[128,1024]{1,0:T(8,128)(2,1)S(1)}, bf16[128,1024]{1,0:T(8,128)(2,1)S(1)}) custom-call(s32[1]{0:T(128)S(6)} %copy.15.panel, s32[8,16]{1,0:T(8,128)} %bitcast.5, s32[16]{0:T(128)} %set_hbm.1, f32[8]{0:T(128)} %sw_hbm.1, f32[16,128]{1,0:T(8,128)} %bitcast.10, ...), custom_call_target="tpu_custom_call" | custom-call | tf_op jit(solution)/shard_map/weigh_panel/pallas_call | solution.py:74
  1.6 0.5 collective-permute-start.100
  2.1 1.3 %collective-permute-done.100 = bf16[128,1024]{1,0:T(8,128)(2,1)S(1)} collective-permute-done((bf16[128,1024]{1,0:T(8,128)(2,1)}, bf16[128,1024]{1,0:T(8,128)(2,1)S(1)}, u32[]{:S(2)}, u32[]{:S(2)}) %collective-permute-start.100) | collective-permute-done | bytes 262176 | tf_op jit(solution)/shard_map/ppermute | solution.py:247
  3.5 51.1 %conditional.1 = (f32[256,512]{1,0:T(8,128)S(1)}) conditional(s32[]{:T(128)} %clamp.3, (s32[]{:T(128)}, s32[]{:T(128)}, s32[]{:T(128)}, s32[]{:T(128)}, bf16[128,1024]{1,0:T(8,128)(2,1)S(1)}, /*index=5*/bf16[128,1024]{1,0:T(8,128)(2,1)S(1)}, s32[2]{0:T(128)S(1)}, s32[8,16]{1,0:T(8,128)S(1)}, ...), branch_computations={%region_0.1_spmd, %region_1.2_spmd, %region_2.3_spmd, %region_3.4_... | conditional | flops 2228230 | bytes 48241744 | solution.py:300
  3.5 0.4 collective-permute-start.29
  4.2 0.8 %weigh_panel.6 = (bf16[128,1024]{1,0:T(8,128)(2,1)S(1)}, bf16[128,1024]{1,0:T(8,128)(2,1)S(1)}, bf16[128,1024]{1,0:T(8,128)(2,1)S(1)}, bf16[128,1024]{1,0:T(8,128)(2,1)S(1)}) custom-call(s32[1]{0:T(128)} %get-tuple-element.155.panel, s32[8,16]{1,0:T(8,128)S(1)} %get-tuple-element.142.fp_ref.fp_hbm, s32[16]{0:T(128)S(1)} %get-tuple-element.156.set_hbm, ...), custom_call_target="tpu_custom_call" | custom-call | tf_op jit(solution)/shard_map/cond/branch_1_fun/weigh_panel/pallas_call | solution.py:74
  4.9 0.4 collective-permute-start.37
  5.6 0.4 collective-permute-start.30
  6.0 5.8 %collective-permute-start.27 = (bf16[128,1024]{1,0:T(8,128)(2,1)S(1)}, bf16[128,1024]{1,0:T(8,128)(2,1)S(1)}, u32[]{:S(2)}, u32[]{:S(2)}) collective-permute-start(bf16[128,1024]{1,0:T(8,128)(2,1)S(1)} %broadcast_select_fusion.4), channel_id=1, source_target_pairs={{2,0},{3,1},{0,2},{1,3},{4,5},{5,4},{6,7},{7,6},{10,8},{11,9},{8,1... | collective-permute-start | bytes 786440 | tf_op jit(solution)/shard_map/cond/branch_1_fun/ppermute | solution.py:281
  11.8 0.6 %collective-permute-start.38 = (bf16[128,1024]{1,0:T(8,128)(2,1)S(1)}, bf16[128,1024]{1,0:T(8,128)(2,1)S(1)}, u32[]{:S(2)}, u32[]{:S(2)}) collective-permute-start(bf16[128,1024]{1,0:T(8,128)(2,1)S(1)} %broadcast_select_fusion.6), channel_id=1, source_target_pairs={{2,4},{3,5},{4,2},{5,3},{0,1},{1,0},{6,7},{7,6},{10,12},{11,13},{1... | collective-permute-start | bytes 786440 | tf_op jit(solution)/shard_map/cond/branch_1_fun/ppermute | solution.py:281
  12.4 5.2 %collective-permute-start.32 = (bf16[128,1024]{1,0:T(8,128)(2,1)S(1)}, bf16[128,1024]{1,0:T(8,128)(2,1)S(1)}, u32[]{:S(2)}, u32[]{:S(2)}) collective-permute-start(bf16[128,1024]{1,0:T(8,128)(2,1)S(1)} %broadcast_select_fusion.7), channel_id=1, source_target_pairs={{2,0},{3,1},{0,2},{1,3},{4,5},{5,4},{6,7},{7,6},{10,8},{11,9},{8,1... | collective-permute-start | bytes 786440 | tf_op jit(solution)/shard_map/cond/branch_1_fun/ppermute | solution.py:281
  18.1 5.1 %collective-permute-start.40 = (bf16[128,1024]{1,0:T(8,128)(2,1)S(1)}, bf16[128,1024]{1,0:T(8,128)(2,1)S(1)}, u32[]{:S(2)}, u32[]{:S(2)}) collective-permute-start(bf16[128,1024]{1,0:T(8,128)(2,1)S(1)} %broadcast_select_fusion.6), channel_id=1, source_target_pairs={{2,0},{3,1},{0,2},{1,3},{4,5},{5,4},{6,7},{7,6},{10,8},{11,9},{8,1... | collective-permute-start | bytes 786440 | tf_op jit(solution)/shard_map/cond/branch_1_fun/ppermute | solution.py:281
  23.4 0.3 collective-permute-start.39
  23.7 0.9 %collective-permute-done.32 = bf16[128,1024]{1,0:T(8,128)(2,1)S(1)} collective-permute-done((bf16[128,1024]{1,0:T(8,128)(2,1)S(1)}, bf16[128,1024]{1,0:T(8,128)(2,1)S(1)}, u32[]{:S(2)}, u32[]{:S(2)}) %collective-permute-start.32) | collective-permute-done | bytes 262176 | tf_op jit(solution)/shard_map/cond/branch_1_fun/ppermute | solution.py:281
  24.7 0.6 %collective-permute-start.33 = (bf16[128,1024]{1,0:T(8,128)(2,1)S(1)}, bf16[128,1024]{1,0:T(8,128)(2,1)S(1)}, u32[]{:S(2)}, u32[]{:S(2)}) collective-permute-start(bf16[128,1024]{1,0:T(8,128)(2,1)S(1)} %select_select_fusion.4.refs_2_), channel_id=1, source_target_pairs={{0,1},{1,0},{2,3},{3,2},{4,5},{5,4},{6,7},{7,6},{8,9},{9,8},{10,11... | collective-permute-start | bytes 786440 | tf_op jit(solution)/shard_map/cond/branch_1_fun/ppermute | solution.py:288
  25.3 4.9 %collective-permute-done.40 = bf16[128,1024]{1,0:T(8,128)(2,1)S(1)} collective-permute-done((bf16[128,1024]{1,0:T(8,128)(2,1)S(1)}, bf16[128,1024]{1,0:T(8,128)(2,1)S(1)}, u32[]{:S(2)}, u32[]{:S(2)}) %collective-permute-start.40) | collective-permute-done | bytes 262176 | tf_op jit(solution)/shard_map/cond/branch_1_fun/ppermute | solution.py:281
  30.2 1.7 %collective-permute-start.45 = (bf16[128,1024]{1,0:T(8,128)(2,1)S(1)}, bf16[128,1024]{1,0:T(8,128)(2,1)S(1)}, u32[]{:S(2)}, u32[]{:S(2)}) collective-permute-start(bf16[128,1024]{1,0:T(8,128)(2,1)S(1)} %broadcast_select_fusion.5), channel_id=1, source_target_pairs={{2,0},{3,1},{0,2},{1,3},{4,5},{5,4},{6,7},{7,6},{10,8},{11,9},{8,1... | collective-permute-start | bytes 786440 | tf_op jit(solution)/shard_map/cond/branch_1_fun/ppermute | solution.py:281
  32.1 0.6 %collective-permute-start.41 = (bf16[128,1024]{1,0:T(8,128)(2,1)S(1)}, bf16[128,1024]{1,0:T(8,128)(2,1)S(1)}, u32[]{:S(2)}, u32[]{:S(2)}) collective-permute-start(bf16[128,1024]{1,0:T(8,128)(2,1)S(1)} %select_select_fusion.3.refs_0_), channel_id=1, source_target_pairs={{0,1},{1,0},{2,3},{3,2},{4,5},{5,4},{6,7},{7,6},{8,9},{9,8},{10,11... | collective-permute-start | bytes 786440 | tf_op jit(solution)/shard_map/cond/branch_1_fun/ppermute | solution.py:288
  32.6 3.3 %partial_gram.10 = (f32[256,256]{1,0:T(8,128)S(1)}, bf16[256,256]{1,0:T(8,128)(2,1)S(1)}, bf16[256,256]{1,0:T(8,128)(2,1)S(1)}, bf16[256,256]{1,0:T(8,128)(2,1)S...) custom-call(s32[2]{0:T(128)S(1)} %get-tuple-element.141.meta, ...), custom_call_target="tpu_custom_call" | custom-call | tf_op jit(solution)/shard_map/cond/branch_1_fun/partial_gram/pallas_call | solution.py:135
  36.0 2.5 %collective-permute-done.45 = bf16[128,1024]{1,0:T(8,128)(2,1)S(1)} collective-permute-done((bf16[128,1024]{1,0:T(8,128)(2,1)S(1)}, bf16[128,1024]{1,0:T(8,128)(2,1)S(1)}, u32[]{:S(2)}, u32[]{:S(2)}) %collective-permute-start.45) | collective-permute-done | bytes 262176 | tf_op jit(solution)/shard_map/cond/branch_1_fun/ppermute | solution.py:281
  38.6 1.6 %collective-permute-start.34 = (bf16[256,256]{1,0:T(8,128)(2,1)S(1)}, bf16[256,256]{1,0:T(8,128)(2,1)S(1)}, u32[]{:S(2)}, u32[]{:S(2)}) collective-permute-start(bf16[256,256]{1,0:T(8,128)(2,1)S(1)} %get-tuple-element.151), channel_id=1, source_target_pairs={{0,8},{8,0},{16,24},{24,16},{1,9},{9,1},{17,25},{25,17},{2,10},{10... | collective-permute-start | bytes 393224 | tf_op jit(solution)/shard_map/cond/branch_1_fun/ppermute | solution.py:252
  40.2 1.5 %collective-permute-start.35 = (bf16[256,256]{1,0:T(8,128)(2,1)S(1)}, bf16[256,256]{1,0:T(8,128)(2,1)S(1)}, u32[]{:S(2)}, u32[]{:S(2)}) collective-permute-start(bf16[256,256]{1,0:T(8,128)(2,1)S(1)} %get-tuple-element.152), channel_id=1, source_target_pairs={{0,16},{8,24},{16,0},{24,8},{1,17},{9,25},{17,1},{25,9},{2,18},{10... | collective-permute-start | bytes 393224 | tf_op jit(solution)/shard_map/cond/branch_1_fun/ppermute | solution.py:252
  41.7 0.5 collective-permute-start.36
  42.2 2.1 %partial_gram.11 = (f32[256,256]{1,0:T(8,128)S(1)}, bf16[256,256]{1,0:T(8,128)(2,1)S(1)}, bf16[256,256]{1,0:T(8,128)(2,1)S(1)}, bf16[256,256]{1,0:T(8,128)(2,1)S(1)}) custom-call(s32[2]{0:T(128)S(1)} %get-tuple-element.141.meta, s32[8,16]{1,0:T(8,128)S(1)} %get-tuple-element.142.fp_ref.fp_hbm, bf16[2048,1024]{1,0:T(8,128)(2,1)S(1)} %get-tuple-element.154.green_ref, ...), custom_call_target="tpu_custom_call" | custom-call | tf_op jit(solution)/shard_map/cond/branch_1_fun/partial_gram/pallas_call | solution.py:135
  44.3 1.6 %collective-permute-start.47 = (bf16[256,256]{1,0:T(8,128)(2,1)S(1)}, bf16[256,256]{1,0:T(8,128)(2,1)S(1)}, u32[]{:S(2)}, u32[]{:S(2)}) collective-permute-start(bf16[256,256]{1,0:T(8,128)(2,1)S(1)} %get-tuple-element.165), channel_id=1, source_target_pairs={{0,8},{8,0},{16,24},{24,16},{1,9},{9,1},{17,25},{25,17},{2,10},{10... | collective-permute-start | bytes 393224 | tf_op jit(solution)/shard_map/cond/branch_1_fun/ppermute | solution.py:252
  45.8 1.5 %collective-permute-start.48 = (bf16[256,256]{1,0:T(8,128)(2,1)S(1)}, bf16[256,256]{1,0:T(8,128)(2,1)S(1)}, u32[]{:S(2)}, u32[]{:S(2)}) collective-permute-start(bf16[256,256]{1,0:T(8,128)(2,1)S(1)} %get-tuple-element.166), channel_id=1, source_target_pairs={{0,16},{8,24},{16,0},{24,8},{1,17},{9,25},{17,1},{25,9},{2,18},{10... | collective-permute-start | bytes 393224 | tf_op jit(solution)/shard_map/cond/branch_1_fun/ppermute | solution.py:252
  47.4 0.5 collective-permute-start.49
  47.8 0.4 collective-permute-done.35.refs_2_
  48.2 0.8 %collective-permute-done.36.refs_3_ = bf16[256,256]{1,0:T(8,128)(2,1)S(1)} collective-permute-done((bf16[256,256]{1,0:T(8,128)(2,1)S(1)}, bf16[256,256]{1,0:T(8,128)(2,1)S(1)}, u32[]{:S(2)}, u32[]{:S(2)}) %collective-permute-start.36) | collective-permute-done | bytes 131104 | tf_op jit(solution)/shard_map/cond/branch_1_fun/ppermute | solution.py:252
  49.0 1.9 %collective-permute-done.47.refs_5_ = bf16[256,256]{1,0:T(8,128)(2,1)S(1)} collective-permute-done((bf16[256,256]{1,0:T(8,128)(2,1)S(1)}, bf16[256,256]{1,0:T(8,128)(2,1)S(1)}, u32[]{:S(2)}, u32[]{:S(2)}) %collective-permute-start.47) | collective-permute-done | bytes 131104 | tf_op jit(solution)/shard_map/cond/branch_1_fun/ppermute | solution.py:252
  50.9 3.3 %collective-permute-done.48.refs_6_ = bf16[256,256]{1,0:T(8,128)(2,1)S(1)} collective-permute-done((bf16[256,256]{1,0:T(8,128)(2,1)S(1)}, bf16[256,256]{1,0:T(8,128)(2,1)S(1)}, u32[]{:S(2)}, u32[]{:S(2)}) %collective-permute-start.48) | collective-permute-done | bytes 131104 | tf_op jit(solution)/shard_map/cond/branch_1_fun/ppermute | solution.py:252
  54.6 0.8 %copy-done.5 = f32[256,512]{1,0:T(8,128)} copy-done((f32[256,512]{1,0:T(8,128)}, f32[256,512]{1,0:T(8,128)S(1)}, u32[]{:S(2)}) %copy-start.5) | copy-done | bytes 524312
  (48 shorter events, 1.8 us)
Async XLA Ops:
  0.0 3.4 %copy-start.4 = (s32[16,8]{0,1:T(8,128)S(1)}, s32[16,8]{0,1:T(8,128)}, u32[]{:S(2)}) copy-start(s32[16,8]{0,1:T(8,128)} %param.11) | copy-start | bytes 1540
  0.0 3.4 %copy-start.7 = (s32[16]{0:T(128)S(1)}, s32[16]{0:T(128)}, u32[]{:S(2)}) copy-start(s32[16]{0:T(128)} %set_hbm.1) | copy-start | bytes 196
  0.0 3.4 %copy-start.8 = (f32[8]{0:T(128)S(1)}, f32[8]{0:T(128)}, u32[]{:S(2)}) copy-start(f32[8]{0:T(128)} %sw_hbm.1) | copy-start | bytes 100
  0.0 3.4 %copy-start.6 = (f32[2048]{0:T(1024)S(1)}, f32[2048]{0:T(1024)}, u32[]{:S(2)}) copy-start(f32[2048]{0:T(1024)} %param.14) | copy-start | bytes 24580
  1.6 1.9 %collective-permute-start.100 = (bf16[128,1024]{1,0:T(8,128)(2,1)}, bf16[128,1024]{1,0:T(8,128)(2,1)S(1)}, u32[]{:S(2)}, u32[]{:S(2)}) collective-permute-start(bf16[128,1024]{1,0:T(8,128)(2,1)} %get-tuple-element.227), channel_id=1, source_target_pairs={{0,1},{1,0},{2,3},{3,2},{4,5},{5,4},{6,7},{7,6},{8,9},{9,8},{10,11... | collective-permute-start | bytes 786440 | tf_op jit(solution)/shard_map/ppermute | solution.py:247
  3.5 2.0 %collective-permute-start.29 = (bf16[128,1024]{1,0:T(8,128)(2,1)S(1)}, bf16[128,1024]{1,0:T(8,128)(2,1)S(1)}, u32[]{:S(2)}, u32[]{:S(2)}) collective-permute-start(bf16[128,1024]{1,0:T(8,128)(2,1)S(1)} %get-tuple-element.149), channel_id=1, source_target_pairs={{0,1},{1,0},{2,3},{3,2},{4,5},{5,4},{6,7},{7,6},{8,9},{9,8},{10,11... | collective-permute-start | bytes 786440 | tf_op jit(solution)/shard_map/cond/branch_1_fun/ppermute | solution.py:267
  4.0 7.8 %collective-permute-start.25 = (bf16[128,1024]{1,0:T(8,128)(2,1)S(1)}, bf16[128,1024]{1,0:T(8,128)(2,1)S(1)}, u32[]{:S(2)}, u32[]{:S(2)}) collective-permute-start(bf16[128,1024]{1,0:T(8,128)(2,1)S(1)} %broadcast_select_fusion.4), channel_id=1, source_target_pairs={{2,4},{3,5},{4,2},{5,3},{0,1},{1,0},{6,7},{7,6},{10,12},{11,13},{1... | collective-permute-start | bytes 786440 | tf_op jit(solution)/shard_map/cond/branch_1_fun/ppermute | solution.py:281
  4.9 6.9 %collective-permute-start.37 = (bf16[128,1024]{1,0:T(8,128)(2,1)S(1)}, bf16[128,1024]{1,0:T(8,128)(2,1)S(1)}, u32[]{:S(2)}, u32[]{:S(2)}) collective-permute-start(bf16[128,1024]{1,0:T(8,128)(2,1)S(1)} %get-tuple-element.160), channel_id=1, source_target_pairs={{0,1},{1,0},{2,3},{3,2},{4,5},{5,4},{6,7},{7,6},{8,9},{9,8},{10,11... | collective-permute-start | bytes 786440 | tf_op jit(solution)/shard_map/cond/branch_1_fun/ppermute | solution.py:267
  5.4 7.0 %collective-permute-start.42 = (bf16[128,1024]{1,0:T(8,128)(2,1)S(1)}, bf16[128,1024]{1,0:T(8,128)(2,1)S(1)}, u32[]{:S(2)}, u32[]{:S(2)}) collective-permute-start(bf16[128,1024]{1,0:T(8,128)(2,1)S(1)} %get-tuple-element.162), channel_id=1, source_target_pairs={{0,1},{1,0},{2,3},{3,2},{4,5},{5,4},{6,7},{7,6},{8,9},{9,8},{10,11... | collective-permute-start | bytes 786440 | tf_op jit(solution)/shard_map/cond/branch_1_fun/ppermute | solution.py:267
  5.6 12.1 %collective-permute-start.30 = (bf16[128,1024]{1,0:T(8,128)(2,1)S(1)}, bf16[128,1024]{1,0:T(8,128)(2,1)S(1)}, u32[]{:S(2)}, u32[]{:S(2)}) collective-permute-start(bf16[128,1024]{1,0:T(8,128)(2,1)S(1)} %broadcast_select_fusion.7), channel_id=1, source_target_pairs={{2,4},{3,5},{4,2},{5,3},{0,1},{1,0},{6,7},{7,6},{10,12},{11,13},{1... | collective-permute-start | bytes 786440 | tf_op jit(solution)/shard_map/cond/branch_1_fun/ppermute | solution.py:281
  6.0 12.0 %collective-permute-start.27 = (bf16[128,1024]{1,0:T(8,128)(2,1)S(1)}, bf16[128,1024]{1,0:T(8,128)(2,1)S(1)}, u32[]{:S(2)}, u32[]{:S(2)}) collective-permute-start(bf16[128,1024]{1,0:T(8,128)(2,1)S(1)} %broadcast_select_fusion.4), channel_id=1, source_target_pairs={{2,0},{3,1},{0,2},{1,3},{4,5},{5,4},{6,7},{7,6},{10,8},{11,9},{8,1... | collective-permute-start | bytes 786440 | tf_op jit(solution)/shard_map/cond/branch_1_fun/ppermute | solution.py:281
  11.8 11.4 %collective-permute-start.26 = (bf16[128,1024]{1,0:T(8,128)(2,1)S(1)}, bf16[128,1024]{1,0:T(8,128)(2,1)S(1)}, u32[]{:S(2)}, u32[]{:S(2)}) collective-permute-start(bf16[128,1024]{1,0:T(8,128)(2,1)S(1)} %collective-permute-done.25), channel_id=1, source_target_pairs={{4,6},{5,7},{6,4},{7,5},{0,1},{1,0},{2,3},{3,2},{12,14},{13,15},{1... | collective-permute-start | bytes 786440 | tf_op jit(solution)/shard_map/cond/branch_1_fun/ppermute | solution.py:281
  11.8 11.5 %collective-permute-start.38 = (bf16[128,1024]{1,0:T(8,128)(2,1)S(1)}, bf16[128,1024]{1,0:T(8,128)(2,1)S(1)}, u32[]{:S(2)}, u32[]{:S(2)}) collective-permute-start(bf16[128,1024]{1,0:T(8,128)(2,1)S(1)} %broadcast_select_fusion.6), channel_id=1, source_target_pairs={{2,4},{3,5},{4,2},{5,3},{0,1},{1,0},{6,7},{7,6},{10,12},{11,13},{1... | collective-permute-start | bytes 786440 | tf_op jit(solution)/shard_map/cond/branch_1_fun/ppermute | solution.py:281
  12.4 20.2 %copy-start.1 = (bf16[2048,1024]{1,0:T(8,128)(2,1)S(1)}, bf16[2048,1024]{1,0:T(8,128)(2,1)}, u32[]{:S(2)}) copy-start(bf16[2048,1024]{1,0:T(8,128)(2,1)} %get-tuple-element.143.green_ref.green_hbm) | copy-start | bytes 12582916 | tf_op jit(solution)/shard_map/cond
  12.4 12.2 %collective-permute-start.32 = (bf16[128,1024]{1,0:T(8,128)(2,1)S(1)}, bf16[128,1024]{1,0:T(8,128)(2,1)S(1)}, u32[]{:S(2)}, u32[]{:S(2)}) collective-permute-start(bf16[128,1024]{1,0:T(8,128)(2,1)S(1)} %broadcast_select_fusion.7), channel_id=1, source_target_pairs={{2,0},{3,1},{0,2},{1,3},{4,5},{5,4},{6,7},{7,6},{10,8},{11,9},{8,1... | collective-permute-start | bytes 786440 | tf_op jit(solution)/shard_map/cond/branch_1_fun/ppermute | solution.py:281
  17.6 7.0 %collective-permute-start.31 = (bf16[128,1024]{1,0:T(8,128)(2,1)S(1)}, bf16[128,1024]{1,0:T(8,128)(2,1)S(1)}, u32[]{:S(2)}, u32[]{:S(2)}) collective-permute-start(bf16[128,1024]{1,0:T(8,128)(2,1)S(1)} %collective-permute-done.30), channel_id=1, source_target_pairs={{4,6},{5,7},{6,4},{7,5},{0,1},{1,0},{2,3},{3,2},{12,14},{13,15},{1... | collective-permute-start | bytes 786440 | tf_op jit(solution)/shard_map/cond/branch_1_fun/ppermute | solution.py:281
  18.1 12.2 %collective-permute-start.40 = (bf16[128,1024]{1,0:T(8,128)(2,1)S(1)}, bf16[128,1024]{1,0:T(8,128)(2,1)S(1)}, u32[]{:S(2)}, u32[]{:S(2)}) collective-permute-start(bf16[128,1024]{1,0:T(8,128)(2,1)S(1)} %broadcast_select_fusion.6), channel_id=1, source_target_pairs={{2,0},{3,1},{0,2},{1,3},{4,5},{5,4},{6,7},{7,6},{10,8},{11,9},{8,1... | collective-permute-start | bytes 786440 | tf_op jit(solution)/shard_map/cond/branch_1_fun/ppermute | solution.py:281
  23.2 8.8 %collective-permute-start.43 = (bf16[128,1024]{1,0:T(8,128)(2,1)S(1)}, bf16[128,1024]{1,0:T(8,128)(2,1)S(1)}, u32[]{:S(2)}, u32[]{:S(2)}) collective-permute-start(bf16[128,1024]{1,0:T(8,128)(2,1)S(1)} %broadcast_select_fusion.5), channel_id=1, source_target_pairs={{2,4},{3,5},{4,2},{5,3},{0,1},{1,0},{6,7},{7,6},{10,12},{11,13},{1... | collective-permute-start | bytes 786440 | tf_op jit(solution)/shard_map/cond/branch_1_fun/ppermute | solution.py:281
  23.4 8.6 %collective-permute-start.39 = (bf16[128,1024]{1,0:T(8,128)(2,1)S(1)}, bf16[128,1024]{1,0:T(8,128)(2,1)S(1)}, u32[]{:S(2)}, u32[]{:S(2)}) collective-permute-start(bf16[128,1024]{1,0:T(8,128)(2,1)S(1)} %collective-permute-done.38), channel_id=1, source_target_pairs={{4,6},{5,7},{6,4},{7,5},{0,1},{1,0},{2,3},{3,2},{12,14},{13,15},{1... | collective-permute-start | bytes 786440 | tf_op jit(solution)/shard_map/cond/branch_1_fun/ppermute | solution.py:281
  24.7 8.0 %collective-permute-start.28 = (bf16[128,1024]{1,0:T(8,128)(2,1)S(1)}, bf16[128,1024]{1,0:T(8,128)(2,1)S(1)}, u32[]{:S(2)}, u32[]{:S(2)}) collective-permute-start(bf16[128,1024]{1,0:T(8,128)(2,1)S(1)} %select_select_fusion.5.refs_0_), channel_id=1, source_target_pairs={{0,1},{1,0},{2,3},{3,2},{4,5},{5,4},{6,7},{7,6},{8,9},{9,8},{10,11... | collective-permute-start | bytes 786440 | tf_op jit(solution)/shard_map/cond/branch_1_fun/ppermute | solution.py:288
  24.7 7.9 %collective-permute-start.33 = (bf16[128,1024]{1,0:T(8,128)(2,1)S(1)}, bf16[128,1024]{1,0:T(8,128)(2,1)S(1)}, u32[]{:S(2)}, u32[]{:S(2)}) collective-permute-start(bf16[128,1024]{1,0:T(8,128)(2,1)S(1)} %select_select_fusion.4.refs_2_), channel_id=1, source_target_pairs={{0,1},{1,0},{2,3},{3,2},{4,5},{5,4},{6,7},{7,6},{8,9},{9,8},{10,11... | collective-permute-start | bytes 786440 | tf_op jit(solution)/shard_map/cond/branch_1_fun/ppermute | solution.py:288
  30.2 8.2 %collective-permute-start.45 = (bf16[128,1024]{1,0:T(8,128)(2,1)S(1)}, bf16[128,1024]{1,0:T(8,128)(2,1)S(1)}, u32[]{:S(2)}, u32[]{:S(2)}) collective-permute-start(bf16[128,1024]{1,0:T(8,128)(2,1)S(1)} %broadcast_select_fusion.5), channel_id=1, source_target_pairs={{2,0},{3,1},{0,2},{1,3},{4,5},{5,4},{6,7},{7,6},{10,8},{11,9},{8,1... | collective-permute-start | bytes 786440 | tf_op jit(solution)/shard_map/cond/branch_1_fun/ppermute | solution.py:281
  32.0 6.5 %collective-permute-start.44 = (bf16[128,1024]{1,0:T(8,128)(2,1)S(1)}, bf16[128,1024]{1,0:T(8,128)(2,1)S(1)}, u32[]{:S(2)}, u32[]{:S(2)}) collective-permute-start(bf16[128,1024]{1,0:T(8,128)(2,1)S(1)} %collective-permute-done.43), channel_id=1, source_target_pairs={{4,6},{5,7},{6,4},{7,5},{0,1},{1,0},{2,3},{3,2},{12,14},{13,15},{1... | collective-permute-start | bytes 786440 | tf_op jit(solution)/shard_map/cond/branch_1_fun/ppermute | solution.py:281
  32.1 10.1 %collective-permute-start.41 = (bf16[128,1024]{1,0:T(8,128)(2,1)S(1)}, bf16[128,1024]{1,0:T(8,128)(2,1)S(1)}, u32[]{:S(2)}, u32[]{:S(2)}) collective-permute-start(bf16[128,1024]{1,0:T(8,128)(2,1)S(1)} %select_select_fusion.3.refs_0_), channel_id=1, source_target_pairs={{0,1},{1,0},{2,3},{3,2},{4,5},{5,4},{6,7},{7,6},{8,9},{9,8},{10,11... | collective-permute-start | bytes 786440 | tf_op jit(solution)/shard_map/cond/branch_1_fun/ppermute | solution.py:288
  38.5 3.6 %collective-permute-start.46 = (bf16[128,1024]{1,0:T(8,128)(2,1)S(1)}, bf16[128,1024]{1,0:T(8,128)(2,1)S(1)}, u32[]{:S(2)}, u32[]{:S(2)}) collective-permute-start(bf16[128,1024]{1,0:T(8,128)(2,1)S(1)} %select_add_fusion.1.refs_2_), channel_id=1, source_target_pairs={{0,1},{1,0},{2,3},{3,2},{4,5},{5,4},{6,7},{7,6},{8,9},{9,8},{10,11... | collective-permute-start | bytes 786440 | tf_op jit(solution)/shard_map/cond/branch_1_fun/ppermute | solution.py:288
  38.6 8.8 %collective-permute-start.34 = (bf16[256,256]{1,0:T(8,128)(2,1)S(1)}, bf16[256,256]{1,0:T(8,128)(2,1)S(1)}, u32[]{:S(2)}, u32[]{:S(2)}) collective-permute-start(bf16[256,256]{1,0:T(8,128)(2,1)S(1)} %get-tuple-element.151), channel_id=1, source_target_pairs={{0,8},{8,0},{16,24},{24,16},{1,9},{9,1},{17,25},{25,17},{2,10},{10... | collective-permute-start | bytes 393224 | tf_op jit(solution)/shard_map/cond/branch_1_fun/ppermute | solution.py:252
  40.2 8.1 %collective-permute-start.35 = (bf16[256,256]{1,0:T(8,128)(2,1)S(1)}, bf16[256,256]{1,0:T(8,128)(2,1)S(1)}, u32[]{:S(2)}, u32[]{:S(2)}) collective-permute-start(bf16[256,256]{1,0:T(8,128)(2,1)S(1)} %get-tuple-element.152), channel_id=1, source_target_pairs={{0,16},{8,24},{16,0},{24,8},{1,17},{9,25},{17,1},{25,9},{2,18},{10... | collective-permute-start | bytes 393224 | tf_op jit(solution)/shard_map/cond/branch_1_fun/ppermute | solution.py:252
  41.7 7.3 %collective-permute-start.36 = (bf16[256,256]{1,0:T(8,128)(2,1)S(1)}, bf16[256,256]{1,0:T(8,128)(2,1)S(1)}, u32[]{:S(2)}, u32[]{:S(2)}) collective-permute-start(bf16[256,256]{1,0:T(8,128)(2,1)S(1)} %get-tuple-element.153), channel_id=1, source_target_pairs={{0,24},{8,16},{16,8},{24,0},{1,25},{9,17},{17,9},{25,1},{2,26},{10... | collective-permute-start | bytes 393224 | tf_op jit(solution)/shard_map/cond/branch_1_fun/ppermute | solution.py:252
  44.3 6.6 %collective-permute-start.47 = (bf16[256,256]{1,0:T(8,128)(2,1)S(1)}, bf16[256,256]{1,0:T(8,128)(2,1)S(1)}, u32[]{:S(2)}, u32[]{:S(2)}) collective-permute-start(bf16[256,256]{1,0:T(8,128)(2,1)S(1)} %get-tuple-element.165), channel_id=1, source_target_pairs={{0,8},{8,0},{16,24},{24,16},{1,9},{9,1},{17,25},{25,17},{2,10},{10... | collective-permute-start | bytes 393224 | tf_op jit(solution)/shard_map/cond/branch_1_fun/ppermute | solution.py:252
  45.8 8.3 %collective-permute-start.48 = (bf16[256,256]{1,0:T(8,128)(2,1)S(1)}, bf16[256,256]{1,0:T(8,128)(2,1)S(1)}, u32[]{:S(2)}, u32[]{:S(2)}) collective-permute-start(bf16[256,256]{1,0:T(8,128)(2,1)S(1)} %get-tuple-element.166), channel_id=1, source_target_pairs={{0,16},{8,24},{16,0},{24,8},{1,17},{9,25},{17,1},{25,9},{2,18},{10... | collective-permute-start | bytes 393224 | tf_op jit(solution)/shard_map/cond/branch_1_fun/ppermute | solution.py:252
  47.4 6.8 %collective-permute-start.49 = (bf16[256,256]{1,0:T(8,128)(2,1)S(1)}, bf16[256,256]{1,0:T(8,128)(2,1)S(1)}, u32[]{:S(2)}, u32[]{:S(2)}) collective-permute-start(bf16[256,256]{1,0:T(8,128)(2,1)S(1)} %get-tuple-element.167), channel_id=1, source_target_pairs={{0,24},{8,16},{16,8},{24,0},{1,25},{9,17},{17,9},{25,1},{2,26},{10... | collective-permute-start | bytes 393224 | tf_op jit(solution)/shard_map/cond/branch_1_fun/ppermute | solution.py:252
  54.6 0.8 %copy-start.5 = (f32[256,512]{1,0:T(8,128)}, f32[256,512]{1,0:T(8,128)S(1)}, u32[]{:S(2)}) copy-start(f32[256,512]{1,0:T(8,128)S(1)} %get-tuple-element.380) | copy-start | bytes 1572868
